TPU v7x, 512 devices: a whole 4x8x8 slice. The times are simulated.
512 devices in a mesh: dp: 8 (over x, z_lo), dap: 64 (over y, z_hi, core).
Axes of the slice: x: 4, y: 8, z: 8 (z_hi: 4, z_lo: 2; z = z_hi * 2 + z_lo), core: 2. Of those that a mesh axis runs over, the one named last changes fastest.
Arguments:
- alignment_activations: bfloat16 [8, 512, 128, 256], P('dp', None, 'dap'), may hold values from -6 to 6
- upstream_adjoint: bfloat16 [8, 512, 128, 256], P('dp', 'dap'), may hold values from -6 to 6
- homolog_presence_flags: int32 [8, 512], P('dp'), may hold values from 0 to 1, as said below
- amino_presence_flags: int32 [8, 128], P('dp', 'dap'), may hold values from 0 to 1, as said below
- asking_projection_matrix: bfloat16 [256, 256], replicated, may hold values from -0.375 to 0.375
- lookup_projection_matrix: bfloat16 [256, 256], replicated, may hold values from -0.375 to 0.375
- content_projection_matrix: bfloat16 [256, 256], replicated, may hold values from -0.375 to 0.375
- sigmoid_projection_matrix: bfloat16 [256, 256], replicated, may hold values from -0.375 to 0.375
- sigmoid_offset_array: float32 [256], replicated, may hold values from -4 to 4
- emission_projection_matrix: bfloat16 [256, 256], replicated, may hold values from -0.375 to 0.375
- standardizer_multiplier: float32 [256], replicated, may hold values from 0.1 to 1.9
- standardizer_offset: float32 [256], replicated, may hold values from -3 to 3
Outputs:
- alignment_adjoint: bfloat16 [8, 512, 128, 256], P('dp', 'dap')
- grad_wquery: float32 [256, 256], replicated
- grad_wkey: float32 [256, 256], replicated
- grad_wvalue: float32 [256, 256], replicated
- grad_wgate: float32 [256, 256], replicated
- grad_wout: float32 [256, 256], replicated
- grad_vectors: float32 [4, 256], replicated
Inputs may be any that keep to these rules, and one draw needn't show every extreme that they name: `homolog_presence_flags`: in each complex the real sequences form a prefix of 256 or more sequences. `amino_presence_flags`: in each complex the real residues form a prefix of 64 or more residues.
All inputs are finite; a program needn't handle non-finite values.
Results may differ from a plain program's by a relative error of at most 0.02.
Values may be sent and summed in bfloat16 or wider, within the bound.
No kernel may reach another device: no remote copies, remote signals or barrier semaphores. Data moves between devices by JAX's collectives and lax.ppermute only.
A program may use at most 64 MiB of HBM per device.

v0:
```python
import jax
import jax.numpy as jnp
from jax import lax
from jax.sharding import PartitionSpec as P

HEADS = 8


EPS = 1e-05
MASKED = 1000000000.0


def product(form, left, right):
    return jnp.einsum(form, left, right, preferred_element_type=jnp.float32)


def against(left, weight):
    return lax.dot_general(
        left, weight, (((1,), (1,)), ((), ())), preferred_element_type=jnp.float32
    )


def outer(left, right):
    return lax.dot_general(
        left, right, (((0,), (0,)), ((), ())), preferred_element_type=jnp.float32
    )


def standardize_lines(alignment_swapped):
    content_lines = alignment_swapped.astype(jnp.float32)
    centred = content_lines - jnp.mean(content_lines, -1, keepdims=True)
    reciprocal_spread = lax.rsqrt(jnp.mean(centred * centred, -1, keepdims=True) + EPS)
    return (centred * reciprocal_spread, reciprocal_spread)


def split_heads(array, stack_members, homolog_lines, head_dim):
    return jnp.transpose(
        array.reshape(stack_members, homolog_lines, HEADS, head_dim), (0, 2, 1, 3)
    ).reshape(stack_members * HEADS, homolog_lines, head_dim)


def join_heads(array, stack_members, homolog_lines, head_dim):
    return jnp.transpose(
        array.reshape(stack_members, HEADS, homolog_lines, head_dim), (0, 2, 1, 3)
    ).reshape(stack_members * homolog_lines, HEADS * head_dim)


def attention_back(query, key_rows, value, gate, d_gated, key_bias, scale):
    scores = product("sd,td->st", query, key_rows) + key_bias[None, :]
    raised = jnp.exp(scores)
    probs = raised / jnp.sum(raised, -1, keepdims=True)
    probs_b = probs.astype(jnp.bfloat16)
    attended = product("st,td->sd", probs_b, value)
    gated = (gate * attended).astype(jnp.bfloat16)
    d_attended = (d_gated * gate).astype(jnp.bfloat16)
    d_logit = (d_gated * attended * gate * (1.0 - gate)).astype(jnp.bfloat16)
    delta = jnp.sum(d_attended.astype(jnp.float32) * attended, -1)
    d_probs = product("sd,td->st", d_attended, value)
    d_scores = (probs * (d_probs - delta[:, None])).astype(jnp.bfloat16)
    d_query = (product("st,td->sd", d_scores, key_rows) * scale).astype(jnp.bfloat16)
    d_key = product("st,sd->td", d_scores, query).astype(jnp.bfloat16)
    d_value = product("st,sd->td", probs_b, d_attended).astype(jnp.bfloat16)
    return (gated, d_logit, d_query, d_key, d_value)


def front_portion(
    alignment_swapped,
    upstream_adjoint_swapped,
    homolog_present,
    amino_present,
    asking_projection_matrix,
    lookup_projection_matrix,
    content_projection_matrix,
    sigmoid_projection_matrix,
    sigmoid_offset_array,
    emission_projection_matrix,
    standardizer_multiplier,
    standardizer_offset,
):
    stack_members, homolog_lines, feature_depth = alignment_swapped.shape
    head_dim = feature_depth // HEADS
    scale = head_dim ** (-0.5)
    standardized_estimate, reciprocal_spread = standardize_lines(alignment_swapped)
    flat = (
        (standardized_estimate * standardizer_multiplier + standardizer_offset)
        .astype(jnp.bfloat16)
        .reshape(stack_members * homolog_lines, feature_depth)
    )
    query = (
        jnp.dot(flat, asking_projection_matrix, preferred_element_type=jnp.float32) * scale
    ).astype(jnp.bfloat16)
    key_rows = jnp.dot(flat, lookup_projection_matrix, preferred_element_type=jnp.float32).astype(
        jnp.bfloat16
    )
    value = jnp.dot(flat, content_projection_matrix, preferred_element_type=jnp.float32).astype(
        jnp.bfloat16
    )
    gate = jax.nn.sigmoid(
        jnp.dot(flat, sigmoid_projection_matrix, preferred_element_type=jnp.float32)
        + sigmoid_offset_array
    )
    d_update = upstream_adjoint_swapped * amino_present.astype(jnp.bfloat16)[:, None, None]
    d_flat = d_update.reshape(stack_members * homolog_lines, feature_depth)
    d_gated = against(d_flat, emission_projection_matrix)
    key_bias = (homolog_present.astype(jnp.float32) - 1.0) * MASKED
    items = tuple(
        (
            split_heads(a, stack_members, homolog_lines, head_dim)
            for a in (query, key_rows, value, gate, d_gated)
        )
    )
    results = lax.map(lambda item: attention_back(*item, key_bias, scale), items)
    gated, d_logit, d_query, d_key, d_value = (
        join_heads(a, stack_members, homolog_lines, head_dim) for a in results
    )
    opening_portion = jnp.concatenate(
        [
            outer(gated, d_flat),
            outer(flat, d_logit),
            jnp.sum(d_logit.astype(jnp.float32), 0)[None],
            jnp.sum(d_flat.astype(jnp.float32), 0)[None],
        ],
        0,
    )
    running_tally = (
        flat,
        standardized_estimate,
        reciprocal_spread,
        d_logit,
        d_query,
        d_key,
        d_value,
    )
    return (running_tally, opening_portion)


def back_part(
    running_tally,
    asking_projection_matrix,
    lookup_projection_matrix,
    content_projection_matrix,
    sigmoid_projection_matrix,
    standardizer_multiplier,
):
    flat, standardized_estimate, reciprocal_spread, d_logit, d_query, d_key, d_value = running_tally
    d_normed = (
        against(d_query, asking_projection_matrix)
        + against(d_key, lookup_projection_matrix)
        + against(d_value, content_projection_matrix)
        + against(d_logit, sigmoid_projection_matrix)
    )
    d_normed = d_normed.reshape(standardized_estimate.shape)
    gain_grad = jnp.sum(d_normed * standardized_estimate, (0, 1))
    bias_grad = jnp.sum(d_normed, (0, 1))
    d_hat = d_normed * standardizer_multiplier
    d_branch = reciprocal_spread * (
        d_hat
        - jnp.mean(d_hat, -1, keepdims=True)
        - standardized_estimate * jnp.mean(d_hat * standardized_estimate, -1, keepdims=True)
    )
    second = jnp.concatenate(
        [
            outer(flat, d_query),
            outer(flat, d_key),
            outer(flat, d_value),
            gain_grad[None],
            bias_grad[None],
        ],
        0,
    )
    return (d_branch, second)


def shards(
    alignment_activations,
    upstream_adjoint,
    homolog_presence_flags,
    amino_presence_flags,
    asking_projection_matrix,
    lookup_projection_matrix,
    content_projection_matrix,
    sigmoid_projection_matrix,
    sigmoid_offset_array,
    emission_projection_matrix,
    standardizer_multiplier,
    standardizer_offset,
):
    local_cot = lax.all_to_all(upstream_adjoint, "dap", split_axis=2, concat_axis=1, tiled=True)
    alignment_swapped = jnp.transpose(alignment_activations[0], (1, 0, 2))
    upstream_adjoint_swapped = jnp.transpose(local_cot[0], (1, 0, 2))
    running_tally, opening_portion = front_portion(
        alignment_swapped,
        upstream_adjoint_swapped,
        homolog_presence_flags[0],
        amino_presence_flags[0],
        asking_projection_matrix,
        lookup_projection_matrix,
        content_projection_matrix,
        sigmoid_projection_matrix,
        sigmoid_offset_array,
        emission_projection_matrix,
        standardizer_multiplier,
        standardizer_offset,
    )
    d_branch, second = back_part(
        running_tally,
        asking_projection_matrix,
        lookup_projection_matrix,
        content_projection_matrix,
        sigmoid_projection_matrix,
        standardizer_multiplier,
    )
    returned_answer = (upstream_adjoint_swapped.astype(jnp.float32) + d_branch).astype(jnp.bfloat16)
    returned_answer = jnp.transpose(returned_answer, (1, 0, 2))[None]
    alignment_adjoint = lax.all_to_all(
        returned_answer, "dap", split_axis=1, concat_axis=2, tiled=True
    )
    opening_portion, second = lax.psum((opening_portion, second), ("dp", "dap"))
    feature_depth = alignment_activations.shape[3]
    scale_factor = (
        lax.axis_size("dp")
        * alignment_activations.shape[1]
        * amino_presence_flags.shape[1]
        * lax.axis_size("dap")
    ) ** (-0.5)
    opening_portion = opening_portion * scale_factor
    second = second * scale_factor
    arrays_collected = jnp.stack(
        [
            opening_portion[2 * feature_depth],
            opening_portion[2 * feature_depth + 1],
            second[3 * feature_depth],
            second[3 * feature_depth + 1],
        ],
        0,
    )
    return (
        alignment_adjoint,
        second[:feature_depth],
        second[feature_depth : 2 * feature_depth],
        second[2 * feature_depth : 3 * feature_depth],
        opening_portion[feature_depth : 2 * feature_depth],
        opening_portion[:feature_depth],
        arrays_collected,
    )


def solution(mesh):
    in_specs = (
        P("dp", None, "dap", None),
        P("dp", "dap", None, None),
        P("dp", None),
        P("dp", "dap"),
        P(),
        P(),
        P(),
        P(),
        P(),
        P(),
        P(),
        P(),
    )
    out_specs = (P("dp", "dap", None, None), P(), P(), P(), P(), P(), P())
    return jax.shard_map(shards, mesh=mesh, in_specs=in_specs, out_specs=out_specs, check_vma=False)
```

profile of v0, /device:TPU:1, one launch (start us, length us, event | category | flops | bytes accessed | tf_op | source)
XLA Modules:
  0.0 517.3 jit_solution(3457835866331970476)
XLA Ops:
  7.2 2.2 copy.63
  9.4 17.8 %all-to-all-start = ((bf16[1,8,128,256]{3,1,0,2:T(8,128)(2,1)}), bf16[1,8,128,256]{3,1,0,2:T(8,128)(2,1)}, u32[]{:S(2)}, u32[]{:S(2)}) async-start(bf16[1,8,128,256]{3,1,0,2:T(8,128)(2,1)} %copy.63), calls=%async_computation | async-start | bytes 1048576 | tf_op jit(solution)/shard_map/all_to_all | solution.py:188
  34.1 2.7 copy.86
  38.0 2.1 copy.70
  40.0 2.3 reshape.138
  42.3 3.4 copy.87
  46.7 2.1 copy.72
  48.8 2.2 reshape.140
  51.0 3.4 copy.88
  55.6 2.0 convert_reduce_fusion
  59.8 141.2 %while.18 = (s32[]{:T(128)}, bf16[16,512,32]{1,2,0:T(8,128)(2,1)}, bf16[16,512,32]{1,2,0:T(8,128)(2,1)}, bf16[16,512,32]{1,2,0:T(8,128)(2,1)}, bf16[16,512,32]{1...) while((s32[]{:T(128)}, bf16[16,512,32]{1,2,0:T(8,128)(2,1)}, ...), condition=%wide.region_5.6_spmd, body=%wide.region_2.5_spmd.sunk | while | flops 103054336 | bytes 7849601 | solution.py:112
  61.2 1.8 fusion.135
  70.0 1.8 fusion.135
  78.8 1.8 fusion.135
  87.6 1.8 fusion.135
  96.5 1.8 fusion.135
  105.3 1.8 fusion.135
  114.1 1.8 fusion.135
  122.9 1.8 fusion.135
  131.7 1.8 fusion.135
  140.6 1.8 fusion.135
  149.4 1.8 fusion.135
  158.2 1.8 fusion.135
  167.0 1.8 fusion.135
  175.9 1.8 fusion.135
  184.7 1.8 fusion.135
  193.5 1.8 fusion.135
  202.6 1.9 convert_reduce_fusion.1
  217.5 4.4 concatenate.6
  222.0 1.9 fusion.62
  225.3 12.7 %all-to-all-start.1 = ((bf16[1,512,2,256]{3,2,0,1:T(2,128)(2,1)}), bf16[1,512,2,256]{3,2,0,1:T(2,128)(2,1)S(1)}, u32[]{:S(2)}, u32[]{:S(2)}) async-start(bf16[1,512,2,256]{3,2,0,1:T(2,128)(2,1)} %copy.81), calls=%async_computation.1 | async-start | bytes 1048576 | tf_op jit(solution)/shard_map/all_to_all | solution.py:215
  238.0 267.2 %all-reduce.3.cloned.1.call-done = (f32[770,256]{1,0:T(8,128)}, f32[514,256]{1,0:T(8,128)}) async-done(((f32[770,256]{1,0:T(8,128)}, f32[514,256]{1,0:T(8,128)}), (f32[770,256]{1,0:T(8,128)}, f32[514,256]{1,0:T(8,128)})) %all-reduce.3.cloned.1.call-update) | async-done | bytes 1314832 | tf_op jit(solution)/shard_map/psum | solution.py:218
  (218 shorter events, 145.4 us)
Async XLA Ops:
  7.2 21.1 %copy-start = (bf16[256,256]{1,0:T(8,128)(2,1)S(1)}, bf16[256,256]{1,0:T(8,128)(2,1)}, u32[]{:S(2)}) copy-start(bf16[256,256]{1,0:T(8,128)(2,1)} %param.21) | copy-start | bytes 393220
  7.2 20.1 %copy-start.1 = (bf16[1,512,2,256]{3,2,1,0:T(2,128)(2,1)S(1)}, bf16[1,512,2,256]{3,2,1,0:T(2,128)(2,1)}, u32[]{:S(2)}) copy-start(bf16[1,512,2,256]{3,2,1,0:T(2,128)(2,1)} %param.14) | copy-start | bytes 1572868
  7.2 20.7 %copy-start.15 = (f32[256]{0:T(256)S(1)}, f32[256]{0:T(256)}, u32[]{:S(2)}) copy-start(f32[256]{0:T(256)} %param.24) | copy-start | bytes 3076
  7.2 20.7 %copy-start.20 = (f32[256]{0:T(256)S(1)}, f32[256]{0:T(256)}, u32[]{:S(2)}) copy-start(f32[256]{0:T(256)} %param.25) | copy-start | bytes 3076
  7.2 21.1 %copy-start.21 = (f32[256]{0:T(256)S(1)}, f32[256]{0:T(256)}, u32[]{:S(2)}) copy-start(f32[256]{0:T(256)} %param.22) | copy-start | bytes 3076
  9.4 46.2 %all-to-all-start = ((bf16[1,8,128,256]{3,1,0,2:T(8,128)(2,1)}), bf16[1,8,128,256]{3,1,0,2:T(8,128)(2,1)}, u32[]{:S(2)}, u32[]{:S(2)}) async-start(bf16[1,8,128,256]{3,1,0,2:T(8,128)(2,1)} %copy.63), calls=%async_computation | async-start | bytes 1048576 | tf_op jit(solution)/shard_map/all_to_all | solution.py:188
  27.2 477.9 %all-reduce.3.cloned.1.call-start = ((), (), s32[]{:S(2)}) async-start(), calls=%async_computation.2 | async-start | bytes 2654208 | tf_op jit(solution)/shard_map/psum | solution.py:218
  28.3 0.9 copy-start.9
  31.6 1.2 copy-start.4
  32.9 3.9 copy-start.10
  40.0 5.6 %copy-start.12 = (bf16[256,256]{1,0:T(8,128)(2,1)S(1)}, bf16[256,256]{1,0:T(8,128)(2,1)}, u32[]{:S(2)}) copy-start(bf16[256,256]{1,0:T(8,128)(2,1)} %param.20) | copy-start | bytes 393220
  48.8 5.6 %copy-start.22 = (s32[1,2]{1,0:T(1,128)S(1)}, s32[1,2]{1,0:T(1,128)}, u32[]{:S(2)}) copy-start(s32[1,2]{1,0:T(1,128)} %param.17) | copy-start | bytes 28
  51.0 7.4 %copy-start.14 = (bf16[256,256]{1,0:T(8,128)(2,1)S(1)}, bf16[256,256]{1,0:T(8,128)(2,1)}, u32[]{:S(2)}) copy-start(bf16[256,256]{1,0:T(8,128)(2,1)} %param.23) | copy-start | bytes 393220
  57.6 0.8 copy-start.2
  206.5 1.5 copy-start.7
  209.2 2.8 copy-start.11
  210.9 1.4 copy-start.8
  212.4 1.7 copy-start.13
  214.1 1.4 copy-start.16
  214.4 1.9 copy-start.3
  215.4 1.3 copy-start.5
  215.4 1.3 copy-start.18
  215.4 1.3 copy-start.19
  215.4 2.1 copy-start.6
  216.7 5.4 %copy-start.17 = (f32[256]{0:T(256)S(1)}, f32[256]{0:T(256)}, u32[]{:S(2)}) copy-start(f32[256]{0:T(256)} %param.24) | copy-start | bytes 3076
  225.3 283.9 %all-to-all-start.1 = ((bf16[1,512,2,256]{3,2,0,1:T(2,128)(2,1)}), bf16[1,512,2,256]{3,2,0,1:T(2,128)(2,1)S(1)}, u32[]{:S(2)}, u32[]{:S(2)}) async-start(bf16[1,512,2,256]{3,2,0,1:T(2,128)(2,1)} %copy.81), calls=%async_computation.1 | async-start | bytes 1048576 | tf_op jit(solution)/shard_map/all_to_all | solution.py:215
Sparse Core Ops, SparseCore 0:
  222.1 282.9 all-reduce.2
where the time goes:
time: 520 us; the launch traced here: 517 us
  waiting for transfers between devices  267 us (51%)
  matrix products  135 us (26%)
  local copies, waits for them, and re-layouts  40.4 us (8%)
  starting transfers between devices  30.6 us (6%)
  other arithmetic  29.1 us (6%)
  between operations  14.5 us (3%)
    psum x1, waiting for transfers between devices, shards(): opening_portion, second = lax.psum((opening_portion, second), ('dp', 'dap'))  267 us
    dot_general x96, matrix products, product(): return jnp.einsum(form, left, right, preferred_element_type=jnp.float32)  124 us
    all_to_all x1, starting transfers between devices, shards(): lax.all_to_all(upstream_adjoint, 'dap', split_axis=2, concat_axis=1, tile...  17.8 us
    reduce_sum x16, other arithmetic, attention_back(): delta = jnp.sum(d_attended.astype(jnp.float32) * attended, -1)  14.5 us
    all_to_all x1, starting transfers between devices, shards(): lax.all_to_all(returned_answer, 'dap', split_axis=1, concat_axis=2, tiled...  12.7 us
  transfers between devices with their start and end apart: 3, of which 1 were waited for; matrix products, arithmetic and copies ran while one was open for 7% of the time, Pallas kernels for 0%

commit v1 on v0

v1 whole, which is shorter than its diff:
```python
import functools

import jax
import jax.numpy as jnp
from jax import lax
from jax.experimental import pallas as pl
from jax.experimental.pallas import tpu as pltpu
from jax.sharding import PartitionSpec as P

HEADS = 8
HEAD_DIM = 32
LANES = 128
PIECE = 48
EPS = 1e-05
MASKED = 1000000000.0
F32, BF16 = jnp.float32, jnp.bfloat16


def mm(left, right):
    return lax.dot_general(left, right, (((1,), (0,)), ((), ())), preferred_element_type=F32)


def against(left, weight):
    return lax.dot_general(left, weight, (((1,), (1,)), ((), ())), preferred_element_type=F32)


def row_sum(a):
    return jnp.sum(a, 0, keepdims=True)


def block_kernel(
    x_ref,
    up_ref,
    hom_ref,
    amino_ref,
    core_ref,
    wq_ref,
    wk_ref,
    wv_ref,
    wg_ref,
    bg_ref,
    wo_ref,
    gain_ref,
    off_ref,
    out_ref,
    keep_ref,
    send_ref,
    q_s,
    k_s,
    v_s,
    do_s,
    qt_s,
    dot_s,
    att_s,
    dq_s,
    dkt_s,
    dvt_s,
    gate_s,
    dg_s,
    out_s,
    grad_s,
    vec_s,
):
    members, lines, depth = x_ref.shape
    scale = HEAD_DIM**-0.5
    bias = (hom_ref[...].astype(F32) - 1.0) * MASKED
    lane_head = lax.broadcasted_iota(jnp.int32, (1, depth), 1) // HEAD_DIM
    vec_s[...] = jnp.zeros_like(vec_s)
    for r in range(members):
        x = x_ref[r].astype(F32)
        centred = x - jnp.mean(x, -1, keepdims=True)
        inv = lax.rsqrt(jnp.mean(centred * centred, -1, keepdims=True) + EPS)
        xhat = centred * inv
        normed = (xhat * gain_ref[...] + off_ref[...]).astype(BF16)
        query = (mm(normed, wq_ref[...]) * scale).astype(BF16)
        q_s[...] = query
        k_s[...] = mm(normed, wk_ref[...]).astype(BF16)
        v_s[...] = mm(normed, wv_ref[...]).astype(BF16)
        gate_s[...] = jax.nn.sigmoid(mm(normed, wg_ref[...]) + bg_ref[...])
        amino = amino_ref[0, r].astype(F32)
        up = up_ref[...].astype(F32)[:, 8 * r : 8 * r + 8, :].reshape(lines, depth)
        d_update = (up * amino).astype(BF16)
        dg_s[...] = against(d_update, wo_ref[...])
        d_att = (dg_s[...] * gate_s[...]).astype(BF16)
        do_s[...] = d_att
        qt_s[...] = query.T
        dot_s[...] = d_att.T
        att_s[...] = jnp.zeros_like(att_s)
        dq_s[...] = jnp.zeros_like(dq_s)

        def head(h, carry):
            own = (lane_head == h).astype(F32).astype(BF16)
            keys, values = k_s[...], v_s[...]
            q_h = q_s[...] * own
            do_h = do_s[...] * own
            rows = pl.ds(pl.multiple_of(h * HEAD_DIM, HEAD_DIM), HEAD_DIM)
            raised = jnp.exp(against(q_h, keys) + bias)
            probs = raised * (1.0 / jnp.sum(raised, -1, keepdims=True))
            probs_b = probs.astype(BF16)
            att = mm(probs_b, values * own)
            att_s[...] += att
            delta = jnp.sum(do_h.astype(F32) * att, -1, keepdims=True)
            d_scores = (probs * (against(do_h, values) - delta)).astype(BF16)
            dq_s[...] += mm(d_scores, keys * own)
            dkt_s[rows, :] = mm(qt_s[rows, :], d_scores).astype(BF16)
            dvt_s[rows, :] = mm(dot_s[rows, :], probs_b).astype(BF16)
            return carry

        lax.fori_loop(0, HEADS, head, 0, unroll=2)

        att, gate, d_gated = att_s[...], gate_s[...], dg_s[...]
        gated = (gate * att).astype(BF16)
        d_logit = (d_gated * att * gate * (1.0 - gate)).astype(BF16)
        dq = (dq_s[...] * scale).astype(BF16)
        dk = dkt_s[...].T
        dv = dvt_s[...].T
        d_normed = (
            against(dq, wq_ref[...])
            + against(dk, wk_ref[...])
            + against(dv, wv_ref[...])
            + against(d_logit, wg_ref[...])
        )
        d_hat = d_normed * gain_ref[...]
        d_branch = inv * (
            d_hat
            - jnp.mean(d_hat, -1, keepdims=True)
            - xhat * jnp.mean(d_hat * xhat, -1, keepdims=True)
        )
        out_s[:, 8 * r : 8 * r + 8, :] = (up + d_branch).reshape(lines // 8, 8, depth)
        normed_t = normed.T
        mats = (
            mm(normed_t, dq),
            mm(normed_t, dk),
            mm(normed_t, dv),
            mm(normed_t, d_logit),
            mm(gated.T, d_update),
        )
        vecs = (
            row_sum(d_logit.astype(F32)),
            row_sum(d_update.astype(F32)),
            row_sum(d_normed * xhat),
            row_sum(d_normed),
        )
        for i, g in enumerate(mats):
            grad_s[i] = g if r == 0 else grad_s[i] + g
        for i, g in enumerate(vecs):
            vec_s[i : i + 1, :] += g
    out_ref[...] = out_s[...].astype(BF16)
    low = core_ref[0] == 0
    pieces = []
    for half in range(2):
        lanes = slice(half * LANES, (half + 1) * LANES)
        parts = [grad_s[i][:, lanes].reshape(depth // 8, 8, LANES) for i in range(5)]
        parts.append(jnp.broadcast_to(vec_s[:, lanes][None], (depth // 8, 8, LANES)))
        pieces.append(jnp.concatenate(parts, 1))
    keep_ref[...] = jnp.where(low, pieces[0], pieces[1]).astype(BF16)
    send_ref[...] = jnp.where(low, pieces[1], pieces[0]).astype(BF16)


def block(x, up, hom, amino, core, wq, wk, wv, wg, bg, wo, gain, off):
    members, lines, depth = x.shape
    vm = pl.BlockSpec(memory_space=pltpu.VMEM)
    sm = pl.BlockSpec(memory_space=pltpu.SMEM)
    piece = jax.ShapeDtypeStruct((depth // 8, PIECE, LANES), BF16)
    tall, wide = (lines, depth), (depth, lines)
    pairs = members * HEADS
    return pl.pallas_call(
        block_kernel,
        out_shape=(jax.ShapeDtypeStruct(up.shape, BF16), piece, piece),
        in_specs=[vm, vm, vm, sm, sm] + [vm] * 8,
        out_specs=(vm, vm, vm),
        scratch_shapes=[pltpu.VMEM(tall, BF16)] * 4
        + [pltpu.VMEM(wide, BF16)] * 2
        + [pltpu.VMEM(tall, F32)] * 2
        + [pltpu.VMEM(wide, BF16)] * 2
        + [pltpu.VMEM(tall, F32)] * 2
        + [
            pltpu.VMEM(up.shape, F32),
            pltpu.VMEM((5, depth, depth), F32),
            pltpu.VMEM((8, depth), F32),
        ],
        compiler_params=pltpu.CompilerParams(vmem_limit_bytes=48 << 20),
        cost_estimate=pl.CostEstimate(
            flops=pairs * 12 * lines * lines * HEAD_DIM,
            bytes_accessed=4 << 20,
            transcendentals=pairs * lines * lines,
        ),
        name="attention_block",
    )(x, up, hom, amino, core, wq, wk, wv, wg, bg, wo, gain, off)


def unpack_kernel(factor, core_ref, own_ref, other_ref, *out_refs):
    low = core_ref[0] == 0
    for half in range(2):
        lanes = slice(half * LANES, (half + 1) * LANES)
        first = low if half == 0 else jnp.logical_not(low)
        own = own_ref[...].astype(F32)
        other = other_ref[...].astype(F32)
        g = jnp.where(first, own, other) * factor
        depth = out_refs[0].shape[0]
        for i in range(5):
            out_refs[i][:, lanes] = g[:, 8 * i : 8 * i + 8, :].reshape(depth, LANES)
        out_refs[5][:, lanes] = g[0, 40:44, :]


def unpack(core, own, other, depth, factor):
    vm = pl.BlockSpec(memory_space=pltpu.VMEM)
    sm = pl.BlockSpec(memory_space=pltpu.SMEM)
    return pl.pallas_call(
        functools.partial(unpack_kernel, factor),
        out_shape=(jax.ShapeDtypeStruct((depth, depth), F32),) * 5
        + (jax.ShapeDtypeStruct((4, depth), F32),),
        in_specs=[sm, vm, vm],
        out_specs=(vm,) * 6,
        compiler_params=pltpu.CompilerParams(vmem_limit_bytes=32 << 20),
        name="unpack",
    )(core, own, other)


def exchange(a, axis, groups=None):
    return lax.all_to_all(
        a, axis, split_axis=0, concat_axis=0, tiled=True, axis_index_groups=groups
    )


def merge_kernel(parts_ref, out_ref):
    total = jnp.sum(parts_ref[...].astype(F32), 0, keepdims=True)
    out_ref[...] = jnp.broadcast_to(total, out_ref.shape).astype(BF16)


def merge(parts, copies):
    vm = pl.BlockSpec(memory_space=pltpu.VMEM)
    return pl.pallas_call(
        merge_kernel,
        out_shape=jax.ShapeDtypeStruct((copies,) + parts.shape[1:], BF16),
        in_specs=[vm],
        out_specs=vm,
        compiler_params=pltpu.CompilerParams(vmem_limit_bytes=16 << 20),
        name="merge",
    )(parts)


def shards(x, up, hom, amino, wq, wk, wv, wg, bg, wo, gain, off):
    _, near, residues, depth = up.shape
    n_dp, n_dap = lax.axis_size("dp"), lax.axis_size("dap")
    lines, members = x.shape[1], x.shape[2]
    chips = n_dap // 2
    partner = [(i, i ^ 1) for i in range(n_dap)]
    same_core = [[2 * i + c for i in range(chips)] for c in range(2)]
    core = (lax.axis_index("dap") % 2).astype(jnp.int32).reshape(1)

    rows = jnp.transpose(up[0].reshape(near, n_dap, members, depth), (1, 2, 0, 3))
    local_up = exchange(rows.reshape(n_dap, members * near, depth), "dap")
    swapped = jnp.transpose(x[0], (1, 0, 2))
    out, keep, send = block(
        swapped, local_up, hom, amino, core, wq, wk, wv, wg, bg[None], wo, gain[None], off[None]
    )

    got = lax.ppermute(send, "dap", partner)
    half = (keep.astype(F32) + got.astype(F32)).astype(BF16)
    parts = exchange(half, "dap", same_core)
    parts = exchange(merge(parts, n_dp), "dp")
    pieces = merge(parts, chips)
    own = exchange(pieces, "dap", same_core)
    other = lax.ppermute(own, "dap", partner)
    factor = float((n_dp * lines * residues) ** (-0.5))
    grads = unpack(core, own, other, depth, factor)

    back = exchange(out, "dap").reshape(n_dap, members, near, depth)
    adjoint = jnp.transpose(back, (2, 0, 1, 3)).reshape(1, near, residues, depth)
    return (adjoint,) + tuple(grads)


def solution(mesh):
    in_specs = (
        P("dp", None, "dap", None),
        P("dp", "dap", None, None),
        P("dp", None),
        P("dp", "dap"),
    ) + (P(),) * 8
    out_specs = (P("dp", "dap", None, None),) + (P(),) * 6
    return jax.shard_map(shards, mesh=mesh, in_specs=in_specs, out_specs=out_specs, check_vma=False)
```

time: 520 us -> 147 us (0.28)
  waiting for transfers between devices: 267 us -> 38.3 us
  matrix products: 135 us -> 0 us
  blocking collectives: 0 us -> 48.7 us
  local copies, waits for them, and re-layouts: 40.4 us -> 3.77 us
  other arithmetic: 29.1 us -> 0.11 us
  Pallas kernels: 0 us -> 22.4 us
  between operations: 14.5 us -> 0.82 us
    psum x1 -> x0, waiting for transfers between devices: 267 us -> none  [shards(): opening_portion, second = lax.psum((opening_portion, second), ('dp', 'dap'))]
    dot_general x110 -> x0, matrix products: 135 us -> none  [the longest x96 124 us: product(): return jnp.einsum(form, left, right, preferred_element_type=jnp.float32)]
    all_to_all x0 -> x3, blocking collectives: none -> 48.7 us  [exchange(): lax.all_to_all(a, axis, split_axis=0, concat_axis=0, tiled=True, axis_ind...]
    all_to_all x2, waiting for transfers between devices: 0.01 us -> 36.6 us  [exchange(): lax.all_to_all(a, axis, split_axis=0, concat_axis=0, tiled=True, axis_ind...]
    pallas_call x0 -> x4, Pallas kernels: none -> 22.4 us  [the longest x1 21.2 us: block(): pl.pallas_call(block_kernel, out_shape=(jax.ShapeDtypeStruct(up.shape, BF...]
    reshape x12 -> x1, local copies, waits for them, and re-layouts: 21.9 us -> 0.89 us  [shards(): jnp.transpose(back, (2, 0, 1, 3)).reshape(1, near, residues, depth)]
    reduce_sum x21 -> x0, other arithmetic: 19.9 us -> none  [the longest x16 14.5 us: attention_back(): delta = jnp.sum(d_attended.astype(jnp.float32) * attended, -1)]
  transfers between devices with their start and end apart: 3 -> 4, of which waited for: 1 -> 3; matrix products, arithmetic and copies ran while one was open for 7% -> 1% of each run, Pallas kernels for 0% -> 0%
where the time goes in v1:
time: 147 us; the launch traced here: 146 us
  blocking collectives  48.7 us (33%)
  waiting for transfers between devices  38.3 us (26%)
  starting transfers between devices  32 us (22%)
  Pallas kernels  22.4 us (15%)
  local copies, waits for them, and re-layouts  3.77 us (3%)
    all_to_all x3, blocking collectives, exchange(): lax.all_to_all(a, axis, split_axis=0, concat_axis=0, tiled=True, axis_ind...  48.7 us
    all_to_all x2, waiting for transfers between devices, exchange(): lax.all_to_all(a, axis, split_axis=0, concat_axis=0, tiled=True, axis_ind...  36.6 us
    all_to_all x2, starting transfers between devices, exchange(): lax.all_to_all(a, axis, split_axis=0, concat_axis=0, tiled=True, axis_ind...  27.7 us
    pallas_call x1, Pallas kernels, block(): pl.pallas_call(block_kernel, out_shape=(jax.ShapeDtypeStruct(up.shape, BF...  21.2 us
  transfers between devices with their start and end apart: 4, of which 3 were waited for; matrix products, arithmetic and copies ran while one was open for 1% of the time, Pallas kernels for 0%

profile of v1, /device:TPU:1, one launch (start us, length us, event | category | flops | bytes accessed | tf_op | source)
XLA Modules:
  0.0 146.1 jit_solution(18375169523291398948)
XLA Ops:
  0.6 2.1 %copy.22 = bf16[1,8,128,256]{3,1,2,0:T(8,128)(2,1)} copy(bf16[1,8,128,256]{3,2,1,0:T(8,128)(2,1)} %param.13) | data formatting | bytes 1048576 | tf_op jit(solution)/shard_map/reshape;squeeze | solution.py:252
  2.8 17.8 %all-to-all-start = ((bf16[64,16,256]{2,1,0:T(8,128)(2,1)}), bf16[64,16,256]{2,1,0:T(8,128)(2,1)S(1)}, u32[]{:S(2)}, u32[]{:S(2)}) async-start(bf16[64,16,256]{2,1,0:T(8,128)(2,1)} %bitcast.4), calls=%async_computation | async-start | bytes 1048576 | tf_op jit(solution)/shard_map/all_to_all | solution.py:221
  20.5 0.0 copy-start
  20.6 0.0 copy-start.1
  20.6 0.0 copy-start.2
  20.6 0.0 copy-start.3
  20.6 0.0 copy-start.4
  20.6 0.0 copy-start.7
  20.6 0.0 copy-start.8
  20.6 0.1 copy.25
  20.7 19.4 %all-to-all-done.up_ref = bf16[64,16,256]{2,1,0:T(8,128)(2,1)S(1)} async-done(((bf16[64,16,256]{2,1,0:T(8,128)(2,1)}), bf16[64,16,256]{2,1,0:T(8,128)(2,1)S(1)}, u32[]{:S(2)}, u32[]{:S(2)}) %all-to-all-start) | async-done | bytes 524320 | tf_op jit(solution)/shard_map/all_to_all | solution.py:221
  40.1 0.0 copy-done.1
  40.1 0.0 copy-done.2
  40.1 0.0 copy-done.3
  40.2 0.0 copy-done.4
  40.2 0.0 copy-done.7
  40.2 0.6 copy-done.5
  40.8 0.0 copy-done.6
  40.8 21.2 %attention_block.1 = (bf16[64,16,256]{2,1,0:T(8,128)(2,1)}, bf16[32,48,128]{2,1,0:T(8,128)(2,1)S(1)}, bf16[32,48,128]{2,1,0:T(8,128)(2,1)S(1)}) custom-call(bf16[2,512,256]{2,1,0:T(8,128)(2,1)S(1)} %bitcast.19, bf16[64,16,256]{2,1,0:T(8,128)(2,1)S(1)} %all-to-all-done.up_ref, s32[1,512]{1,0:T(1,128)S(1)} %copy-done.5, s32[1,2]{1,0:T(1,128)S(1)} %copy-done.9, ...), custom_call_target="tpu_custom_call" | custom-call | flops 1610612736 | bytes 4194304 | tf_op jit(solution)/shard_map/attention_block/pallas_call | solution.py:167
  62.0 1.9 %collective-permute-start = (bf16[32,48,128]{2,1,0:T(8,128)(2,1)S(1)}, bf16[32,48,128]{2,1,0:T(8,128)(2,1)S(1)}, u32[]{:S(2)}, u32[]{:S(2)}) collective-permute-start(bf16[32,48,128]{2,1,0:T(8,128)(2,1)S(1)} %get-tuple-element.18), channel_id=1, source_target_pairs={{0,1},{1,0},{2,3},{3,2},{4,5},{5,4},{6,7},{7,6},{8,9},{9,8},{10,11... | collective-permute-start | bytes 1179656 | tf_op jit(solution)/shard_map/ppermute | solution.py:259
  64.0 1.7 %collective-permute-done = bf16[32,48,128]{2,1,0:T(8,128)(2,1)S(1)} collective-permute-done((bf16[32,48,128]{2,1,0:T(8,128)(2,1)S(1)}, bf16[32,48,128]{2,1,0:T(8,128)(2,1)S(1)}, u32[]{:S(2)}, u32[]{:S(2)}) %collective-permute-start) | collective-permute-done | bytes 393248 | tf_op jit(solution)/shard_map/ppermute | solution.py:259
  65.6 0.1 add_convert_fusion
  65.8 19.7 %all_to_all.25.parts_ref = bf16[32,48,128]{2,1,0:T(8,128)(2,1)S(1)} all-to-all(bf16[32,48,128]{2,1,0:T(8,128)(2,1)S(1)} %add_convert_fusion), channel_id=1, replica_groups={{0,2,4,6,8,10,12,14,16,18,20,22,24,26,28,30,32,34,36,38,40,42,44,46,48,..., dimensions={0} | all-to-all | bytes 786432 | tf_op jit(solution)/shard_map/all_to_all | solution.py:221
  85.4 0.1 merge.2
  85.5 10.1 %all_to_all.26.parts_ref = bf16[8,48,128]{2,1,0:T(8,128)(2,1)S(1)} all-to-all(bf16[8,48,128]{2,1,0:T(8,128)(2,1)S(1)} %merge.2), channel_id=1, replica_groups=mesh['dp'=8,'dap'=64] {'dp'}, dimensions={0} | all-to-all | bytes 196608 | tf_op jit(solution)/shard_map/all_to_all | solution.py:221
  95.6 18.9 %all_to_all.27.own_ref = bf16[32,48,128]{2,1,0:T(8,128)(2,1)S(1)} all-to-all(bf16[32,48,128]{2,1,0:T(8,128)(2,1)S(1)} %merge.3), channel_id=1, replica_groups={{0,2,4,6,8,10,12,14,16,18,20,22,24,26,28,30,32,34,36,38,40,42,44,46,48,..., dimensions={0} | all-to-all | bytes 786432 | tf_op jit(solution)/shard_map/all_to_all | solution.py:221
  114.6 10.0 %all-to-all-start.1 = ((bf16[64,16,256]{2,1,0:T(8,128)(2,1)}), bf16[64,16,256]{2,1,0:T(8,128)(2,1)S(1)}, u32[]{:S(2)}, u32[]{:S(2)}) async-start(bf16[64,16,256]{2,1,0:T(8,128)(2,1)} %get-tuple-element.16), calls=%async_computation.1 | async-start | bytes 1048576 | tf_op jit(solution)/shard_map/all_to_all | solution.py:221
  124.6 2.4 %collective-permute-start.1 = (bf16[32,48,128]{2,1,0:T(8,128)(2,1)S(1)}, bf16[32,48,128]{2,1,0:T(8,128)(2,1)S(1)}, u32[]{:S(2)}, u32[]{:S(2)}) collective-permute-start(bf16[32,48,128]{2,1,0:T(8,128)(2,1)S(1)} %all_to_all.27.own_ref), channel_id=1, source_target_pairs={{0,1},{1,0},{2,3},{3,2},{4,5},{5,4},{6,7},{7,6},{8,9},{9,8},{10,11... | collective-permute-start | bytes 1179656 | tf_op jit(solution)/shard_map/ppermute | solution.py:265
  126.9 17.2 %all-to-all-done.1 = bf16[64,16,256]{2,1,0:T(8,128)(2,1)S(1)} async-done(((bf16[64,16,256]{2,1,0:T(8,128)(2,1)}), bf16[64,16,256]{2,1,0:T(8,128)(2,1)S(1)}, u32[]{:S(2)}, u32[]{:S(2)}) %all-to-all-start.1) | async-done | bytes 524320 | tf_op jit(solution)/shard_map/all_to_all | solution.py:221
  144.1 0.9 copy.23
  145.0 0.0 collective-permute-done.1.other_ref
  145.0 1.1 unpack.1
  (9 shorter events, 0.1 us)
Async XLA Ops:
  2.8 17.8 %copy-start.10 = (bf16[1,512,2,256]{3,2,1,0:T(2,128)(2,1)S(1)}, bf16[1,512,2,256]{3,2,1,0:T(2,128)(2,1)}, u32[]{:S(2)}) copy-start(bf16[1,512,2,256]{3,2,1,0:T(2,128)(2,1)} %param.12) | copy-start | bytes 1572868
  2.8 37.4 %all-to-all-start = ((bf16[64,16,256]{2,1,0:T(8,128)(2,1)}), bf16[64,16,256]{2,1,0:T(8,128)(2,1)S(1)}, u32[]{:S(2)}, u32[]{:S(2)}) async-start(bf16[64,16,256]{2,1,0:T(8,128)(2,1)} %bitcast.4), calls=%async_computation | async-start | bytes 1048576 | tf_op jit(solution)/shard_map/all_to_all | solution.py:221
  20.5 19.6 %copy-start = (bf16[256,256]{1,0:T(8,128)(2,1)S(1)}, bf16[256,256]{1,0:T(8,128)(2,1)}, u32[]{:S(2)}) copy-start(bf16[256,256]{1,0:T(8,128)(2,1)} %wq_ref.1) | copy-start | bytes 393220
  20.6 19.6 %copy-start.1 = (bf16[256,256]{1,0:T(8,128)(2,1)S(1)}, bf16[256,256]{1,0:T(8,128)(2,1)}, u32[]{:S(2)}) copy-start(bf16[256,256]{1,0:T(8,128)(2,1)} %wk_ref.1) | copy-start | bytes 393220
  20.6 19.6 %copy-start.2 = (bf16[256,256]{1,0:T(8,128)(2,1)S(1)}, bf16[256,256]{1,0:T(8,128)(2,1)}, u32[]{:S(2)}) copy-start(bf16[256,256]{1,0:T(8,128)(2,1)} %wv_ref.1) | copy-start | bytes 393220
  20.6 19.6 %copy-start.3 = (bf16[256,256]{1,0:T(8,128)(2,1)S(1)}, bf16[256,256]{1,0:T(8,128)(2,1)}, u32[]{:S(2)}) copy-start(bf16[256,256]{1,0:T(8,128)(2,1)} %wg_ref.1) | copy-start | bytes 393220
  20.6 19.6 %copy-start.4 = (bf16[256,256]{1,0:T(8,128)(2,1)S(1)}, bf16[256,256]{1,0:T(8,128)(2,1)}, u32[]{:S(2)}) copy-start(bf16[256,256]{1,0:T(8,128)(2,1)} %wo_ref.1) | copy-start | bytes 393220
  20.6 19.6 %copy-start.7 = (f32[256]{0:T(256)S(1)}, f32[256]{0:T(256)}, u32[]{:S(2)}) copy-start(f32[256]{0:T(256)} %param.22) | copy-start | bytes 3076
  20.6 19.6 %copy-start.8 = (f32[256]{0:T(256)S(1)}, f32[256]{0:T(256)}, u32[]{:S(2)}) copy-start(f32[256]{0:T(256)} %param.23) | copy-start | bytes 3076
  40.1 0.7 copy-start.5
  40.1 0.7 copy-start.6
  40.1 0.7 copy-start.9
  62.0 3.6 %collective-permute-start = (bf16[32,48,128]{2,1,0:T(8,128)(2,1)S(1)}, bf16[32,48,128]{2,1,0:T(8,128)(2,1)S(1)}, u32[]{:S(2)}, u32[]{:S(2)}) collective-permute-start(bf16[32,48,128]{2,1,0:T(8,128)(2,1)S(1)} %get-tuple-element.18), channel_id=1, source_target_pairs={{0,1},{1,0},{2,3},{3,2},{4,5},{5,4},{6,7},{7,6},{8,9},{9,8},{10,11... | collective-permute-start | bytes 1179656 | tf_op jit(solution)/shard_map/ppermute | solution.py:259
  114.6 29.6 %all-to-all-start.1 = ((bf16[64,16,256]{2,1,0:T(8,128)(2,1)}), bf16[64,16,256]{2,1,0:T(8,128)(2,1)S(1)}, u32[]{:S(2)}, u32[]{:S(2)}) async-start(bf16[64,16,256]{2,1,0:T(8,128)(2,1)} %get-tuple-element.16), calls=%async_computation.1 | async-start | bytes 1048576 | tf_op jit(solution)/shard_map/all_to_all | solution.py:221
  124.6 20.5 %collective-permute-start.1 = (bf16[32,48,128]{2,1,0:T(8,128)(2,1)S(1)}, bf16[32,48,128]{2,1,0:T(8,128)(2,1)S(1)}, u32[]{:S(2)}, u32[]{:S(2)}) collective-permute-start(bf16[32,48,128]{2,1,0:T(8,128)(2,1)S(1)} %all_to_all.27.own_ref), channel_id=1, source_target_pairs={{0,1},{1,0},{2,3},{3,2},{4,5},{5,4},{6,7},{7,6},{8,9},{9,8},{10,11... | collective-permute-start | bytes 1179656 | tf_op jit(solution)/shard_map/ppermute | solution.py:265

commit v2 on v1

v2 whole, which is shorter than its diff:
```python
import functools

import jax
import jax.numpy as jnp
from jax import lax
from jax.experimental import pallas as pl
from jax.experimental.pallas import tpu as pltpu
from jax.sharding import PartitionSpec as P

HEADS = 8
HEAD_DIM = 32
LANES = 128
PIECE = 48
MSA = 32
EPS = 1e-05
MASKED = 1000000000.0
F32, BF16 = jnp.float32, jnp.bfloat16


def mm(left, right):
    return lax.dot_general(left, right, (((1,), (0,)), ((), ())), preferred_element_type=F32)


def against(left, weight):
    return lax.dot_general(left, weight, (((1,), (1,)), ((), ())), preferred_element_type=F32)


def row_sum(a):
    return jnp.sum(a, 0, keepdims=True)


def front_kernel(
    x_ref,
    hom_ref,
    wq_ref,
    wk_ref,
    wv_ref,
    wg_ref,
    bg_ref,
    gain_ref,
    off_ref,
    xhat_ref,
    inv_ref,
    nt_ref,
    k_ref,
    v_ref,
    qt_ref,
    gate_ref,
    att_ref,
    probs_ref,
    q_s,
):
    members, lines, depth = x_ref.shape
    bias = (hom_ref[...].astype(F32) - 1.0) * MASKED
    lane_head = lax.broadcasted_iota(jnp.int32, (1, depth), 1) // HEAD_DIM
    for r in range(members):
        x = x_ref[r].astype(F32)
        centred = x - jnp.mean(x, -1, keepdims=True)
        inv = lax.rsqrt(jnp.mean(centred * centred, -1, keepdims=True) + EPS)
        xhat = centred * inv
        xhat_ref[r] = xhat
        inv_ref[r] = jnp.broadcast_to(inv, (lines, LANES))
        normed = (xhat * gain_ref[...] + off_ref[...]).astype(BF16)
        nt_ref[r] = normed.T
        query = (mm(normed, wq_ref[...]) * HEAD_DIM**-0.5).astype(BF16)
        q_s[...] = query
        qt_ref[r] = query.T
        k_ref[r] = mm(normed, wk_ref[...]).astype(BF16)
        v_ref[r] = mm(normed, wv_ref[...]).astype(BF16)
        gate_ref[r] = jax.nn.sigmoid(mm(normed, wg_ref[...]) + bg_ref[...])
        att_ref[r] = jnp.zeros((lines, depth), F32)

        def head(h, carry):
            own = (lane_head == h).astype(F32).astype(BF16)
            raised = jnp.exp(against(q_s[...] * own, k_ref[r]) + bias)
            probs = raised * (1.0 / jnp.sum(raised, -1, keepdims=True))
            probs_b = probs.astype(BF16)
            probs_ref[r, h] = probs_b
            att_ref[r] += mm(probs_b, v_ref[r] * own)
            return carry

        lax.fori_loop(0, HEADS, head, 0, unroll=2)


def back_kernel(
    up_ref,
    amino_ref,
    core_ref,
    xhat_ref,
    inv_ref,
    nt_ref,
    k_ref,
    v_ref,
    qt_ref,
    gate_ref,
    att_ref,
    probs_ref,
    wq_ref,
    wk_ref,
    wv_ref,
    wg_ref,
    wo_ref,
    gain_ref,
    keep_ref,
    send_ref,
    do_s,
    dot_s,
    prod_s,
    dg_s,
    dq_s,
    dkt_s,
    dvt_s,
    out_s,
    grad_s,
    vec_s,
):
    members, lines, depth = xhat_ref.shape
    lane_head = lax.broadcasted_iota(jnp.int32, (1, depth), 1) // HEAD_DIM
    vec_s[...] = jnp.zeros_like(vec_s)
    for r in range(members):
        amino = amino_ref[0, r].astype(F32)
        up = up_ref[...].astype(F32)[:, 8 * r : 8 * r + 8, :].reshape(lines, depth)
        d_update = (up * amino).astype(BF16)
        dg_s[...] = against(d_update, wo_ref[...])
        d_att = (dg_s[...] * gate_ref[r]).astype(BF16)
        do_s[...] = d_att
        dot_s[...] = d_att.T
        prod_s[...] = d_att.astype(F32) * att_ref[r]
        dq_s[...] = jnp.zeros_like(dq_s)

        def head(h, carry):
            mask = (lane_head == h).astype(F32)
            own = mask.astype(BF16)
            rows = pl.ds(pl.multiple_of(h * HEAD_DIM, HEAD_DIM), HEAD_DIM)
            probs_b = probs_ref[r, h]
            delta = jnp.sum(prod_s[...] * mask, -1, keepdims=True)
            d_probs = against(do_s[...] * own, v_ref[r])
            d_scores = (probs_b.astype(F32) * (d_probs - delta)).astype(BF16)
            dq_s[...] += mm(d_scores, k_ref[r] * own)
            dkt_s[rows, :] = mm(qt_ref[r, rows, :], d_scores).astype(BF16)
            dvt_s[rows, :] = mm(dot_s[rows, :], probs_b).astype(BF16)
            return carry

        lax.fori_loop(0, HEADS, head, 0, unroll=2)

        att, gate, d_gated, xhat = att_ref[r], gate_ref[r], dg_s[...], xhat_ref[r]
        gated = (gate * att).astype(BF16)
        d_logit = (d_gated * att * gate * (1.0 - gate)).astype(BF16)
        dq = (dq_s[...] * HEAD_DIM**-0.5).astype(BF16)
        dk = dkt_s[...].T
        dv = dvt_s[...].T
        d_normed = (
            against(dq, wq_ref[...])
            + against(dk, wk_ref[...])
            + against(dv, wv_ref[...])
            + against(d_logit, wg_ref[...])
        )
        d_hat = d_normed * gain_ref[...]
        d_branch = inv_ref[r][:, :1] * (
            d_hat
            - jnp.mean(d_hat, -1, keepdims=True)
            - xhat * jnp.mean(d_hat * xhat, -1, keepdims=True)
        )
        out_s[:, 8 * r : 8 * r + 8, :] = (up + d_branch).reshape(lines // 8, 8, depth)
        normed_t = nt_ref[r]
        mats = (
            mm(normed_t, dq),
            mm(normed_t, dk),
            mm(normed_t, dv),
            mm(normed_t, d_logit),
            mm(gated.T, d_update),
        )
        vecs = (
            row_sum(d_logit.astype(F32)),
            row_sum(d_update.astype(F32)),
            row_sum(d_normed * xhat),
            row_sum(d_normed),
        )
        for i, g in enumerate(mats):
            grad_s[i] = g if r == 0 else grad_s[i] + g
        for i, g in enumerate(vecs):
            vec_s[i : i + 1, :] += g
    low = core_ref[0] == 0
    chips = depth // 8
    pairs = out_s[...].reshape(chips, 2, 16, depth)
    for half in range(2):
        lanes = slice(half * LANES, (half + 1) * LANES)
        rows = slice(16 * half, 16 * half + 16)
        zero, one = pairs[:, 0, :, lanes], pairs[:, 1, :, lanes]
        keep_ref[:, rows, :] = jnp.where(low, zero, one).astype(BF16)
        send_ref[:, rows, :] = jnp.where(low, one, zero).astype(BF16)
    pieces = []
    for half in range(2):
        lanes = slice(half * LANES, (half + 1) * LANES)
        parts = [grad_s[i][:, lanes].reshape(chips, 8, LANES) for i in range(5)]
        parts.append(jnp.broadcast_to(vec_s[:, lanes][None], (chips, 8, LANES)))
        pieces.append(jnp.concatenate(parts, 1))
    keep_ref[:, MSA:, :] = jnp.where(low, pieces[0], pieces[1]).astype(BF16)
    send_ref[:, MSA:, :] = jnp.where(low, pieces[1], pieces[0]).astype(BF16)


def specs(n):
    return [pl.BlockSpec(memory_space=pltpu.VMEM)] * n


SMEM = pl.BlockSpec(memory_space=pltpu.SMEM)


def shape(dims, dtype):
    return jax.ShapeDtypeStruct(dims, dtype)


def front(x, hom, wq, wk, wv, wg, bg, gain, off):
    members, lines, depth = x.shape
    tall, wide = (members, lines, depth), (members, depth, lines)
    pairs = members * HEADS
    return pl.pallas_call(
        front_kernel,
        out_shape=(
            shape(tall, F32),
            shape((members, lines, LANES), F32),
            shape(wide, BF16),
            shape(tall, BF16),
            shape(tall, BF16),
            shape(wide, BF16),
            shape(tall, F32),
            shape(tall, F32),
            shape((members, HEADS, lines, lines), BF16),
        ),
        in_specs=specs(9),
        out_specs=specs(9),
        scratch_shapes=[pltpu.VMEM((lines, depth), BF16)],
        compiler_params=pltpu.CompilerParams(vmem_limit_bytes=28 << 20),
        cost_estimate=pl.CostEstimate(
            flops=pairs * 32 * lines * lines * HEAD_DIM,
            bytes_accessed=4 << 20,
            transcendentals=pairs * lines * lines,
        ),
        name="attention_front",
    )(x, hom, wq, wk, wv, wg, bg, gain, off)


def back(up, amino, core, saved, wq, wk, wv, wg, wo, gain):
    members, lines, depth = saved[0].shape
    tall, wide = (lines, depth), (depth, lines)
    pairs = members * HEADS
    parcel = shape((depth // 8, MSA + PIECE, LANES), BF16)
    return pl.pallas_call(
        back_kernel,
        out_shape=(parcel, parcel),
        in_specs=specs(1) + [SMEM, SMEM] + specs(15),
        out_specs=specs(2),
        scratch_shapes=[
            pltpu.VMEM(tall, BF16),
            pltpu.VMEM(wide, BF16),
            pltpu.VMEM(tall, F32),
            pltpu.VMEM(tall, F32),
            pltpu.VMEM(tall, F32),
            pltpu.VMEM(wide, BF16),
            pltpu.VMEM(wide, BF16),
            pltpu.VMEM(up.shape, F32),
            pltpu.VMEM((5, depth, depth), F32),
            pltpu.VMEM((8, depth), F32),
        ],
        compiler_params=pltpu.CompilerParams(vmem_limit_bytes=36 << 20),
        cost_estimate=pl.CostEstimate(
            flops=pairs * 64 * lines * lines * HEAD_DIM,
            bytes_accessed=4 << 20,
            transcendentals=0,
        ),
        name="attention_back",
    )(up, amino, core, *saved, wq, wk, wv, wg, wo, gain)


def combine_kernel(core_ref, keep_ref, got_ref, ride_ref):
    low = core_ref[0] == 0
    for half in range(2):
        rows = slice(16 * half, 16 * half + 16)
        keep, got = keep_ref[:, rows, :], got_ref[:, rows, :]
        at = 32 * half
        ride_ref[:, at : at + 16, :] = jnp.where(low, keep, got)
        ride_ref[:, at + 16 : at + 32, :] = jnp.where(low, got, keep)
    total = keep_ref[:, MSA:, :].astype(F32) + got_ref[:, MSA:, :].astype(F32)
    ride_ref[:, 2 * MSA :, :] = total.astype(BF16)


def combine(core, keep, got):
    return pl.pallas_call(
        combine_kernel,
        out_shape=shape((keep.shape[0], 2 * MSA + PIECE, LANES), BF16),
        in_specs=[SMEM] + specs(2),
        out_specs=specs(1)[0],
        compiler_params=pltpu.CompilerParams(vmem_limit_bytes=16 << 20),
        name="combine",
    )(core, keep, got)


def merge_kernel(parts_ref, out_ref):
    start = parts_ref.shape[1] - PIECE
    total = jnp.sum(parts_ref[:, start:, :].astype(F32), 0, keepdims=True)
    out_ref[...] = jnp.broadcast_to(total, out_ref.shape).astype(BF16)


def merge(parts, copies):
    return pl.pallas_call(
        merge_kernel,
        out_shape=shape((copies, PIECE, LANES), BF16),
        in_specs=specs(1),
        out_specs=specs(1)[0],
        compiler_params=pltpu.CompilerParams(vmem_limit_bytes=16 << 20),
        name="merge",
    )(parts)


def unpack_kernel(factor, core_ref, own_ref, other_ref, *out_refs):
    low = core_ref[0] == 0
    for half in range(2):
        lanes = slice(half * LANES, (half + 1) * LANES)
        first = low if half == 0 else jnp.logical_not(low)
        own = own_ref[...].astype(F32)
        other = other_ref[...].astype(F32)
        g = jnp.where(first, own, other) * factor
        depth = out_refs[0].shape[0]
        for i in range(5):
            out_refs[i][:, lanes] = g[:, 8 * i : 8 * i + 8, :].reshape(depth, LANES)
        out_refs[5][:, lanes] = g[0, 40:44, :]


def unpack(core, own, other, depth, factor):
    vm = pl.BlockSpec(memory_space=pltpu.VMEM)
    sm = pl.BlockSpec(memory_space=pltpu.SMEM)
    return pl.pallas_call(
        functools.partial(unpack_kernel, factor),
        out_shape=(jax.ShapeDtypeStruct((depth, depth), F32),) * 5
        + (jax.ShapeDtypeStruct((4, depth), F32),),
        in_specs=[sm, vm, vm],
        out_specs=(vm,) * 6,
        compiler_params=pltpu.CompilerParams(vmem_limit_bytes=32 << 20),
        name="unpack",
    )(core, own, other)


def exchange(a, axis, groups=None):
    return lax.all_to_all(
        a, axis, split_axis=0, concat_axis=0, tiled=True, axis_index_groups=groups
    )


def shards(x, up, hom, amino, wq, wk, wv, wg, bg, wo, gain, off):
    _, near, residues, depth = up.shape
    n_dp, n_dap = lax.axis_size("dp"), lax.axis_size("dap")
    lines, members = x.shape[1], x.shape[2]
    chips = n_dap // 2
    partner = [(i, i ^ 1) for i in range(n_dap)]
    same_core = [[2 * i + c for i in range(chips)] for c in range(2)]
    core = (lax.axis_index("dap") % 2).astype(jnp.int32).reshape(1)

    rows = jnp.transpose(up[0].reshape(near, n_dap, members, depth), (1, 2, 0, 3))
    local_up = exchange(rows.reshape(n_dap, members * near, depth), "dap")
    swapped = jnp.transpose(x[0], (1, 0, 2))
    gain, off, bg = gain[None], off[None], bg[None]
    saved = front(swapped, hom, wq, wk, wv, wg, bg, gain, off)
    keep, send = back(local_up, amino, core, saved, wq, wk, wv, wg, wo, gain)

    got = lax.ppermute(send, "dap", partner)
    parts = exchange(combine(core, keep, got), "dap", same_core)
    pieces = exchange(merge(parts, n_dp), "dp")
    own = exchange(merge(pieces, chips), "dap", same_core)
    other = lax.ppermute(own, "dap", partner)
    factor = float((n_dp * lines * residues) ** (-0.5))
    grads = unpack(core, own, other, depth, factor)

    msa = parts[:, : 2 * MSA].reshape(chips, depth // LANES, 2, members, near, LANES)
    adjoint = jnp.transpose(msa, (4, 0, 2, 3, 1, 5)).reshape(1, near, residues, depth)
    return (adjoint,) + tuple(grads)


def solution(mesh):
    in_specs = (
        P("dp", None, "dap", None),
        P("dp", "dap", None, None),
        P("dp", None),
        P("dp", "dap"),
    ) + (P(),) * 8
    out_specs = (P("dp", "dap", None, None),) + (P(),) * 6
    return jax.shard_map(shards, mesh=mesh, in_specs=in_specs, out_specs=out_specs, check_vma=False)
```

time: 147 us -> 150 us (1.020)
  waiting for transfers between devices: 38.3 us -> 1.71 us
  local copies, waits for them, and re-layouts: 3.77 us -> 29.8 us
  blocking collectives: 48.7 us -> 66.6 us
  starting transfers between devices: 32 us -> 26.7 us
    all_to_all x2 -> x1, waiting for transfers between devices: 36.6 us -> 0.01 us  [exchange(): lax.all_to_all(a, axis, split_axis=0, concat_axis=0, tiled=True, axis_ind...]
    unnamed x23 -> x59, local copies, waits for them, and re-layouts: 0.75 us -> 26.1 us
    all_to_all x3, blocking collectives: 48.7 us -> 66.6 us  [exchange(): lax.all_to_all(a, axis, split_axis=0, concat_axis=0, tiled=True, axis_ind...]
    all_to_all x2 -> x1, starting transfers between devices: 27.7 us -> 17.6 us  [exchange(): lax.all_to_all(a, axis, split_axis=0, concat_axis=0, tiled=True, axis_ind...]
    ppermute x1, starting transfers between devices: 2.36 us -> 6.73 us  [shards(): other = lax.ppermute(own, 'dap', partner)]
    pallas_call x3 -> x5, Pallas kernels: 21.3 us -> 22.7 us  [the longest x1 12.3 us: back(): pl.pallas_call(back_kernel, out_shape=(parcel, parcel), in_specs=specs(1)...]
  transfers between devices with their start and end apart: 4 -> 3, of which waited for: 3 -> 1; matrix products, arithmetic and copies ran while one was open for 1% -> 2% of each run, Pallas kernels for 0% -> 7%
where the time goes in v2:
time: 150 us; the launch traced here: 149 us
  blocking collectives  66.6 us (44%)
  local copies, waits for them, and re-layouts  29.8 us (20%)
  starting transfers between devices  26.7 us (18%)
  Pallas kernels  23.8 us (16%)
  waiting for transfers between devices  1.71 us (1%)
    all_to_all x3, blocking collectives, exchange(): lax.all_to_all(a, axis, split_axis=0, concat_axis=0, tiled=True, axis_ind...  66.6 us
    unnamed x59, local copies, waits for them, and re-layouts  26.1 us
    all_to_all x1, starting transfers between devices, exchange(): lax.all_to_all(a, axis, split_axis=0, concat_axis=0, tiled=True, axis_ind...  17.6 us
    pallas_call x1, Pallas kernels, back(): pl.pallas_call(back_kernel, out_shape=(parcel, parcel), in_specs=specs(1)...  12.3 us
    pallas_call x1, Pallas kernels, front(): pl.pallas_call(front_kernel, out_shape=(shape(tall, F32), shape((members,...  10.1 us
    ppermute x1, starting transfers between devices, shards(): other = lax.ppermute(own, 'dap', partner)  6.73 us
  transfers between devices with their start and end apart: 3, of which 1 were waited for; matrix products, arithmetic and copies ran while one was open for 2% of the time, Pallas kernels for 7%

profile of v2, /device:TPU:1, one launch (start us, length us, event | category | flops | bytes accessed | tf_op | source)
XLA Modules:
  0.0 149.5 jit_solution(11831667634798412073)
XLA Ops:
  0.6 2.1 %copy.22 = bf16[1,8,128,256]{3,1,2,0:T(8,128)(2,1)} copy(bf16[1,8,128,256]{3,2,1,0:T(8,128)(2,1)} %param.13) | data formatting | bytes 1048576 | tf_op jit(solution)/shard_map/reshape;squeeze | solution.py:358
  2.8 17.6 %all-to-all-start = ((bf16[64,16,256]{2,1,0:T(8,128)(2,1)}), bf16[64,16,256]{2,1,0:T(8,128)(2,1)S(1)}, u32[]{:S(2)}, u32[]{:S(2)}) async-start(bf16[64,16,256]{2,1,0:T(8,128)(2,1)} %bitcast.3), calls=%async_computation | async-start | bytes 1048576 | tf_op jit(solution)/shard_map/all_to_all | solution.py:344
  20.5 1.2 copy.24
  21.7 0.9 copy-done
  22.6 0.9 copy-done.2
  23.5 0.9 copy-done.4
  24.4 0.9 copy-done.6
  25.3 0.7 copy-done.9
  28.1 10.1 %attention_front.1 = (f32[2,512,256]{2,1,0:T(8,128)S(1)}, f32[2,512,128]{2,1,0:T(8,128)S(1)}, bf16[2,256,512]{2,1,0:T(8,128)(2,1)S(1)}, bf16[2,512,256]{2,1,0:T(...) custom-call(bf16[2,512,256]{2,1,0:T(8,128)(2,1)S(1)} %bitcast.17, ...), custom_call_target="tpu_custom_call" | custom-call | flops 4294967296 | bytes 4194304 | tf_op jit(solution)/shard_map/attention_front/pallas_call | solution.py:217
  38.2 3.3 %copy-done.15 = bf16[2,8,512,512]{3,2,1,0:T(8,128)(2,1)} copy-done((bf16[2,8,512,512]{3,2,1,0:T(8,128)(2,1)}, bf16[2,8,512,512]{3,2,1,0:T(8,128)(2,1)S(1)}, u32[]{:S(2)}) %copy-start.15) | copy-done | bytes 8388632
  41.4 1.0 copy-done.17
  42.5 1.0 copy-done.19
  43.5 0.8 copy-done.21
  44.3 0.8 copy-done.23
  45.1 0.8 copy-done.25
  45.8 0.8 copy-done.27
  46.7 3.4 %copy-done.16 = bf16[2,8,512,512]{3,2,1,0:T(8,128)(2,1)S(1)} copy-done((bf16[2,8,512,512]{3,2,1,0:T(8,128)(2,1)S(1)}, bf16[2,8,512,512]{3,2,1,0:T(8,128)(2,1)}, u32[]{:S(2)}) %copy-start.16) | copy-done | bytes 8388632
  50.1 1.2 copy-done.18
  51.3 1.2 copy-done.20
  52.6 1.0 copy-done.22
  53.6 1.0 copy-done.24
  54.6 1.0 copy-done.26
  55.7 1.0 copy-done.28
  56.7 12.3 %attention_back.1 = (bf16[32,80,128]{2,1,0:T(8,128)(2,1)S(1)}, bf16[32,80,128]{2,1,0:T(8,128)(2,1)S(1)}) custom-call(bf16[64,16,256]{2,1,0:T(8,128)(2,1)S(1)} %all-to-all-done.up_ref, s32[1,2]{1,0:T(1,128)S(1)} %copy-done.14, s32[1]{0:T(128)} %bitcast.core_ref, f32[2,512,256]{2,1,0:T(8,128)S(1)} %get-tuple-element.24.xhat_ref, ...), custom_call_target="tpu_custom_call" | custom-call | flops 8589934592 | bytes 4194304 | tf_op jit(solution)/shard_map/attention_back/pallas_call | solution.py:248
  69.0 2.4 %collective-permute-start = (bf16[32,80,128]{2,1,0:T(8,128)(2,1)S(1)}, bf16[32,80,128]{2,1,0:T(8,128)(2,1)S(1)}, u32[]{:S(2)}, u32[]{:S(2)}) collective-permute-start(bf16[32,80,128]{2,1,0:T(8,128)(2,1)S(1)} %get-tuple-element.34), channel_id=1, source_target_pairs={{0,1},{1,0},{2,3},{3,2},{4,5},{5,4},{6,7},{7,6},{8,9},{9,8},{10,11... | collective-permute-start | bytes 1966088 | tf_op jit(solution)/shard_map/ppermute | solution.py:365
  71.4 1.7 %collective-permute-done.got_ref = bf16[32,80,128]{2,1,0:T(8,128)(2,1)S(1)} collective-permute-done((bf16[32,80,128]{2,1,0:T(8,128)(2,1)S(1)}, bf16[32,80,128]{2,1,0:T(8,128)(2,1)S(1)}, u32[]{:S(2)}, u32[]{:S(2)}) %collective-permute-start) | collective-permute-done | bytes 655392 | tf_op jit(solution)/shard_map/ppermute | solution.py:365
  73.3 37.3 %all_to_all.20.parts_ref = bf16[32,112,128]{2,1,0:T(8,128)(2,1)S(1)} all-to-all(bf16[32,112,128]{2,1,0:T(8,128)(2,1)S(1)} %combine.1), channel_id=1, replica_groups={{0,2,4,6,8,10,12,14,16,18,20,22,24,26,28,30,32,34,36,38,40,42,44,46,48,..., dimensions={0} | all-to-all | bytes 1835008 | tf_op jit(solution)/shard_map/all_to_all | solution.py:344
  110.6 9.9 %all_to_all.21.parts_ref = bf16[8,48,128]{2,1,0:T(8,128)(2,1)S(1)} all-to-all(bf16[8,48,128]{2,1,0:T(8,128)(2,1)S(1)} %merge.2), channel_id=1, replica_groups=mesh['dp'=8,'dap'=64] {'dp'}, dimensions={0} | all-to-all | bytes 196608 | tf_op jit(solution)/shard_map/all_to_all | solution.py:344
  120.5 19.5 %all_to_all.22.own_ref = bf16[32,48,128]{2,1,0:T(8,128)(2,1)S(1)} all-to-all(bf16[32,48,128]{2,1,0:T(8,128)(2,1)S(1)} %merge.3), channel_id=1, replica_groups={{0,2,4,6,8,10,12,14,16,18,20,22,24,26,28,30,32,34,36,38,40,42,44,46,48,..., dimensions={0} | all-to-all | bytes 786432 | tf_op jit(solution)/shard_map/all_to_all | solution.py:344
  140.0 6.7 %collective-permute-start.1 = (bf16[32,48,128]{2,1,0:T(8,128)(2,1)S(1)}, bf16[32,48,128]{2,1,0:T(8,128)(2,1)S(1)}, u32[]{:S(2)}, u32[]{:S(2)}) collective-permute-start(bf16[32,48,128]{2,1,0:T(8,128)(2,1)S(1)} %all_to_all.22.own_ref), channel_id=1, source_target_pairs={{0,1},{1,0},{2,3},{3,2},{4,5},{5,4},{6,7},{7,6},{8,9},{9,8},{10,11... | collective-permute-start | bytes 1179656 | tf_op jit(solution)/shard_map/ppermute | solution.py:369
  147.3 1.1 reshape.29
  148.4 1.1 unpack.1
  (46 shorter events, 2.9 us)
Async XLA Ops:
  2.8 43.9 %all-to-all-start = ((bf16[64,16,256]{2,1,0:T(8,128)(2,1)}), bf16[64,16,256]{2,1,0:T(8,128)(2,1)S(1)}, u32[]{:S(2)}, u32[]{:S(2)}) async-start(bf16[64,16,256]{2,1,0:T(8,128)(2,1)} %bitcast.3), calls=%async_computation | async-start | bytes 1048576 | tf_op jit(solution)/shard_map/all_to_all | solution.py:344
  20.4 26.3 %copy-start.1 = (bf16[256,256]{1,0:T(8,128)(2,1)S(1)}, bf16[256,256]{1,0:T(8,128)(2,1)}, u32[]{:S(2)}) copy-start(bf16[256,256]{1,0:T(8,128)(2,1)} %wq_ref.3) | copy-start | bytes 393220
  20.4 26.3 %copy-start.3 = (bf16[256,256]{1,0:T(8,128)(2,1)S(1)}, bf16[256,256]{1,0:T(8,128)(2,1)}, u32[]{:S(2)}) copy-start(bf16[256,256]{1,0:T(8,128)(2,1)} %wk_ref.3) | copy-start | bytes 393220
  20.4 26.2 %copy-start.5 = (bf16[256,256]{1,0:T(8,128)(2,1)S(1)}, bf16[256,256]{1,0:T(8,128)(2,1)}, u32[]{:S(2)}) copy-start(bf16[256,256]{1,0:T(8,128)(2,1)} %wv_ref.3) | copy-start | bytes 393220
  20.4 26.2 %copy-start.7 = (bf16[256,256]{1,0:T(8,128)(2,1)S(1)}, bf16[256,256]{1,0:T(8,128)(2,1)}, u32[]{:S(2)}) copy-start(bf16[256,256]{1,0:T(8,128)(2,1)} %wg_ref.3) | copy-start | bytes 393220
  20.4 26.2 %copy-start.8 = (bf16[256,256]{1,0:T(8,128)(2,1)S(1)}, bf16[256,256]{1,0:T(8,128)(2,1)}, u32[]{:S(2)}) copy-start(bf16[256,256]{1,0:T(8,128)(2,1)} %wo_ref.1) | copy-start | bytes 393220
  20.5 26.2 %copy-start.13 = (f32[256]{0:T(256)S(1)}, f32[256]{0:T(256)}, u32[]{:S(2)}) copy-start(f32[256]{0:T(256)} %param.22) | copy-start | bytes 3076
  20.5 26.2 %copy-start.14 = (s32[1,2]{1,0:T(1,128)S(1)}, s32[1,2]{1,0:T(1,128)}, u32[]{:S(2)}) copy-start(s32[1,2]{1,0:T(1,128)} %amino_ref.1) | copy-start | bytes 28
  21.7 0.9 copy-start
  22.6 0.9 copy-start.2
  23.5 0.9 copy-start.4
  24.4 0.9 copy-start.6
  25.3 0.7 copy-start.9
  26.0 0.7 copy-start.10
  26.7 0.7 copy-start.11
  27.4 0.7 copy-start.12
  38.2 3.3 %copy-start.15 = (bf16[2,8,512,512]{3,2,1,0:T(8,128)(2,1)}, bf16[2,8,512,512]{3,2,1,0:T(8,128)(2,1)S(1)}, u32[]{:S(2)}) copy-start(bf16[2,8,512,512]{3,2,1,0:T(8,128)(2,1)S(1)} %get-tuple-element.32.probs_ref) | copy-start | bytes 25165828
  41.4 1.0 copy-start.17
  42.5 1.0 copy-start.19
  43.5 0.8 copy-start.21
  44.3 0.8 copy-start.23
  45.0 0.8 copy-start.25
  45.8 0.8 copy-start.27
  46.7 3.4 %copy-start.16 = (bf16[2,8,512,512]{3,2,1,0:T(8,128)(2,1)S(1)}, bf16[2,8,512,512]{3,2,1,0:T(8,128)(2,1)}, u32[]{:S(2)}) copy-start(bf16[2,8,512,512]{3,2,1,0:T(8,128)(2,1)} %copy-done.15) | copy-start | bytes 25165828
  50.1 1.2 copy-start.18
  51.3 1.2 copy-start.20
  52.5 1.0 copy-start.22
  53.6 1.0 copy-start.24
  54.6 1.0 copy-start.26
  55.7 1.0 copy-start.28
  69.0 4.1 %collective-permute-start = (bf16[32,80,128]{2,1,0:T(8,128)(2,1)S(1)}, bf16[32,80,128]{2,1,0:T(8,128)(2,1)S(1)}, u32[]{:S(2)}, u32[]{:S(2)}) collective-permute-start(bf16[32,80,128]{2,1,0:T(8,128)(2,1)S(1)} %get-tuple-element.34), channel_id=1, source_target_pairs={{0,1},{1,0},{2,3},{3,2},{4,5},{5,4},{6,7},{7,6},{8,9},{9,8},{10,11... | collective-permute-start | bytes 1966088 | tf_op jit(solution)/shard_map/ppermute | solution.py:365
  140.0 8.3 %collective-permute-start.1 = (bf16[32,48,128]{2,1,0:T(8,128)(2,1)S(1)}, bf16[32,48,128]{2,1,0:T(8,128)(2,1)S(1)}, u32[]{:S(2)}, u32[]{:S(2)}) collective-permute-start(bf16[32,48,128]{2,1,0:T(8,128)(2,1)S(1)} %all_to_all.22.own_ref), channel_id=1, source_target_pairs={{0,1},{1,0},{2,3},{3,2},{4,5},{5,4},{6,7},{7,6},{8,9},{9,8},{10,11... | collective-permute-start | bytes 1179656 | tf_op jit(solution)/shard_map/ppermute | solution.py:369

commit v3 on v2

v3 whole, which is shorter than its diff:
```python
import functools

import jax
import jax.numpy as jnp
from jax import lax
from jax.experimental import pallas as pl
from jax.experimental.pallas import tpu as pltpu
from jax.sharding import PartitionSpec as P

HEADS = 8
HEAD_DIM = 32
LANES = 128
PIECE = 48
MSA = 32
GROUP = 8
VMEM_BYTES = 60 << 20
EPS = 1e-05
MASKED = 1000000000.0
F32, BF16 = jnp.float32, jnp.bfloat16


def mm(left, right):
    return lax.dot_general(left, right, (((1,), (0,)), ((), ())), preferred_element_type=F32)


def against(left, weight):
    return lax.dot_general(left, weight, (((1,), (1,)), ((), ())), preferred_element_type=F32)


def row_sum(a):
    return jnp.sum(a, 0, keepdims=True)


def front_kernel(
    x_ref,
    hom_ref,
    wq_ref,
    wk_ref,
    wv_ref,
    wg_ref,
    bg_ref,
    gain_ref,
    off_ref,
    xhat_ref,
    inv_ref,
    nt_ref,
    k_ref,
    v_ref,
    qt_ref,
    gate_ref,
    att_ref,
    probs_ref,
    q_s,
):
    _, lines, depth = x_ref.shape
    group = probs_ref.shape[1]
    step = pl.program_id(1)
    bias = (hom_ref[...].astype(F32) - 1.0) * MASKED
    lane_head = lax.broadcasted_iota(jnp.int32, (1, depth), 1) // HEAD_DIM

    @pl.when(step == 0)
    def _():
        x = x_ref[0].astype(F32)
        centred = x - jnp.mean(x, -1, keepdims=True)
        inv = lax.rsqrt(jnp.mean(centred * centred, -1, keepdims=True) + EPS)
        xhat = centred * inv
        xhat_ref[0] = xhat
        inv_ref[0] = jnp.broadcast_to(inv, (lines, LANES))
        normed = (xhat * gain_ref[...] + off_ref[...]).astype(BF16)
        nt_ref[0] = normed.T
        query = (mm(normed, wq_ref[...]) * HEAD_DIM**-0.5).astype(BF16)
        q_s[...] = query
        qt_ref[0] = query.T
        k_ref[0] = mm(normed, wk_ref[...]).astype(BF16)
        v_ref[0] = mm(normed, wv_ref[...]).astype(BF16)
        gate_ref[0] = jax.nn.sigmoid(mm(normed, wg_ref[...]) + bg_ref[...])
        att_ref[0] = jnp.zeros((lines, depth), F32)

    for j in range(group):
        own = (lane_head == step * group + j).astype(F32).astype(BF16)
        raised = jnp.exp(against(q_s[...] * own, k_ref[0]) + bias)
        probs = raised * (1.0 / jnp.sum(raised, -1, keepdims=True))
        probs_b = probs.astype(BF16)
        probs_ref[0, j] = probs_b
        att_ref[0] += mm(probs_b, v_ref[0] * own)


def back_kernel(
    up_ref,
    amino_ref,
    core_ref,
    xhat_ref,
    inv_ref,
    nt_ref,
    k_ref,
    v_ref,
    qt_ref,
    gate_ref,
    att_ref,
    probs_ref,
    wq_ref,
    wk_ref,
    wv_ref,
    wg_ref,
    wo_ref,
    gain_ref,
    keep_ref,
    send_ref,
    up_s,
    do_s,
    dot_s,
    prod_s,
    dg_s,
    dq_s,
    dkt_s,
    dvt_s,
    out_s,
    grad_s,
    vec_s,
):
    members, lines, depth = up_s.shape
    group = probs_ref.shape[1]
    r, step = pl.program_id(0), pl.program_id(1)
    last = pl.num_programs(1) - 1
    lane_head = lax.broadcasted_iota(jnp.int32, (1, depth), 1) // HEAD_DIM

    def update():
        return (up_s[r] * amino_ref[0, r].astype(F32)).astype(BF16)

    @pl.when(jnp.logical_and(r == 0, step == 0))
    def _():
        up = up_ref[...].astype(F32)
        for i in range(members):
            up_s[i] = up[:, 8 * i : 8 * i + 8, :].reshape(lines, depth)
        grad_s[...] = jnp.zeros_like(grad_s)
        vec_s[...] = jnp.zeros_like(vec_s)

    @pl.when(step == 0)
    def _():
        dg_s[...] = against(update(), wo_ref[...])
        d_att = (dg_s[...] * gate_ref[0]).astype(BF16)
        do_s[...] = d_att
        dot_s[...] = d_att.T
        prod_s[...] = d_att.astype(F32) * att_ref[0]
        dq_s[...] = jnp.zeros_like(dq_s)

    for j in range(group):
        h = step * group + j
        mask = (lane_head == h).astype(F32)
        own = mask.astype(BF16)
        rows = pl.ds(pl.multiple_of(h * HEAD_DIM, HEAD_DIM), HEAD_DIM)
        probs_b = probs_ref[0, j]
        delta = jnp.sum(prod_s[...] * mask, -1, keepdims=True)
        d_probs = against(do_s[...] * own, v_ref[0])
        d_scores = (probs_b.astype(F32) * (d_probs - delta)).astype(BF16)
        dq_s[...] += mm(d_scores, k_ref[0] * own)
        dkt_s[rows, :] = mm(qt_ref[0, rows, :], d_scores).astype(BF16)
        dvt_s[rows, :] = mm(dot_s[rows, :], probs_b).astype(BF16)

    @pl.when(step == last)
    def _():
        att, gate, d_gated, xhat = att_ref[0], gate_ref[0], dg_s[...], xhat_ref[0]
        d_update = update()
        gated = (gate * att).astype(BF16)
        d_logit = (d_gated * att * gate * (1.0 - gate)).astype(BF16)
        dq = (dq_s[...] * HEAD_DIM**-0.5).astype(BF16)
        dk = dkt_s[...].T
        dv = dvt_s[...].T
        d_normed = (
            against(dq, wq_ref[...])
            + against(dk, wk_ref[...])
            + against(dv, wv_ref[...])
            + against(d_logit, wg_ref[...])
        )
        d_hat = d_normed * gain_ref[...]
        d_branch = inv_ref[0][:, :1] * (
            d_hat
            - jnp.mean(d_hat, -1, keepdims=True)
            - xhat * jnp.mean(d_hat * xhat, -1, keepdims=True)
        )
        out_s[r] = (up_s[r] + d_branch).reshape(lines // 8, 8, depth)
        normed_t = nt_ref[0]
        mats = (
            mm(normed_t, dq),
            mm(normed_t, dk),
            mm(normed_t, dv),
            mm(normed_t, d_logit),
            mm(gated.T, d_update),
        )
        vecs = (
            row_sum(d_logit.astype(F32)),
            row_sum(d_update.astype(F32)),
            row_sum(d_normed * xhat),
            row_sum(d_normed),
        )
        for i, g in enumerate(mats):
            grad_s[i] += g
        for i, g in enumerate(vecs):
            vec_s[i : i + 1, :] += g

    @pl.when(jnp.logical_and(r == members - 1, step == last))
    def _():
        low = core_ref[0] == 0
        chips = depth // 8
        pairs = jnp.concatenate([out_s[i] for i in range(members)], 1)
        pairs = pairs.reshape(chips, 2, 8 * members, depth)
        for half in range(2):
            lanes = slice(half * LANES, (half + 1) * LANES)
            rows = slice(16 * half, 16 * half + 16)
            zero, one = pairs[:, 0, :, lanes], pairs[:, 1, :, lanes]
            keep_ref[:, rows, :] = jnp.where(low, zero, one).astype(BF16)
            send_ref[:, rows, :] = jnp.where(low, one, zero).astype(BF16)
        pieces = []
        for half in range(2):
            lanes = slice(half * LANES, (half + 1) * LANES)
            parts = [grad_s[i][:, lanes].reshape(chips, 8, LANES) for i in range(5)]
            parts.append(jnp.broadcast_to(vec_s[:, lanes][None], (chips, 8, LANES)))
            pieces.append(jnp.concatenate(parts, 1))
        keep_ref[:, MSA:, :] = jnp.where(low, pieces[0], pieces[1]).astype(BF16)
        send_ref[:, MSA:, :] = jnp.where(low, pieces[1], pieces[0]).astype(BF16)


def specs(n):
    return [pl.BlockSpec(memory_space=pltpu.VMEM)] * n


SMEM = pl.BlockSpec(memory_space=pltpu.SMEM)


def shape(dims, dtype):
    return jax.ShapeDtypeStruct(dims, dtype)


def whole(a):
    return pl.BlockSpec(a.shape, lambda r, h: (0,) * len(a.shape))


def by_member(a):
    return pl.BlockSpec((1,) + a.shape[1:], lambda r, h: (r,) + (0,) * (len(a.shape) - 1))


def by_group(a):
    return pl.BlockSpec((1, GROUP) + a.shape[2:], lambda r, h: (r, h, 0, 0))


def front(x, hom, wq, wk, wv, wg, bg, gain, off):
    members, lines, depth = x.shape
    tall, wide = (members, lines, depth), (members, depth, lines)
    pairs = members * HEADS
    outs = (
        shape(tall, F32),
        shape((members, lines, LANES), F32),
        shape(wide, BF16),
        shape(tall, BF16),
        shape(tall, BF16),
        shape(wide, BF16),
        shape(tall, F32),
        shape(tall, F32),
        shape((members, HEADS, lines, lines), BF16),
    )
    return pl.pallas_call(
        front_kernel,
        grid=(members, HEADS // GROUP),
        out_shape=outs,
        in_specs=[by_member(x)] + [whole(a) for a in (hom, wq, wk, wv, wg, bg, gain, off)],
        out_specs=[by_member(a) for a in outs[:-1]] + [by_group(outs[-1])],
        scratch_shapes=[pltpu.VMEM((lines, depth), BF16)],
        compiler_params=pltpu.CompilerParams(vmem_limit_bytes=VMEM_BYTES),
        cost_estimate=pl.CostEstimate(
            flops=pairs * 32 * lines * lines * HEAD_DIM,
            bytes_accessed=14 << 20,
            transcendentals=pairs * lines * lines,
        ),
        name="attention_front",
    )(x, hom, wq, wk, wv, wg, bg, gain, off)


def back(up, amino, core, saved, wq, wk, wv, wg, wo, gain):
    members, lines, depth = saved[0].shape
    tall, wide = (lines, depth), (depth, lines)
    pairs = members * HEADS
    parcel = shape((depth // 8, MSA + PIECE, LANES), BF16)
    return pl.pallas_call(
        back_kernel,
        grid=(members, HEADS // GROUP),
        out_shape=(parcel, parcel),
        in_specs=[whole(up), SMEM, SMEM]
        + [by_member(a) for a in saved[:-1]]
        + [by_group(saved[-1])]
        + [whole(a) for a in (wq, wk, wv, wg, wo, gain)],
        out_specs=[whole(parcel), whole(parcel)],
        scratch_shapes=[
            pltpu.VMEM((members,) + tall, F32),
            pltpu.VMEM(tall, BF16),
            pltpu.VMEM(wide, BF16),
            pltpu.VMEM(tall, F32),
            pltpu.VMEM(tall, F32),
            pltpu.VMEM(tall, F32),
            pltpu.VMEM(wide, BF16),
            pltpu.VMEM(wide, BF16),
            pltpu.VMEM((members, lines // 8, 8, depth), F32),
            pltpu.VMEM((5, depth, depth), F32),
            pltpu.VMEM((8, depth), F32),
        ],
        compiler_params=pltpu.CompilerParams(vmem_limit_bytes=VMEM_BYTES),
        cost_estimate=pl.CostEstimate(
            flops=pairs * 64 * lines * lines * HEAD_DIM,
            bytes_accessed=14 << 20,
            transcendentals=0,
        ),
        name="attention_back",
    )(up, amino, core, *saved, wq, wk, wv, wg, wo, gain)


def combine_kernel(core_ref, keep_ref, got_ref, out_ref):
    total = keep_ref[:, MSA:, :].astype(F32) + got_ref[:, MSA:, :].astype(F32)
    out_ref[...] = total.astype(BF16)


def combine(core, keep, got):
    return pl.pallas_call(
        combine_kernel,
        out_shape=shape((keep.shape[0], PIECE, LANES), BF16),
        in_specs=[SMEM] + specs(2),
        out_specs=specs(1)[0],
        compiler_params=pltpu.CompilerParams(vmem_limit_bytes=16 << 20),
        name="combine",
    )(core, keep, got)


def pack_kernel(core_ref, keep_ref, got_ref, after_ref, out_ref):
    low = core_ref[0] == 0
    for half in range(2):
        rows = slice(16 * half, 16 * half + 16)
        keep, got = keep_ref[:, rows, :], got_ref[:, rows, :]
        at = 32 * half
        out_ref[:, at : at + 16, :] = jnp.where(low, keep, got)
        out_ref[:, at + 16 : at + 32, :] = jnp.where(low, got, keep)


def pack(core, keep, got, after):
    return pl.pallas_call(
        pack_kernel,
        out_shape=shape((keep.shape[0], 2 * MSA, LANES), BF16),
        in_specs=[SMEM] + specs(2) + [pl.BlockSpec(memory_space=pl.ANY)],
        out_specs=specs(1)[0],
        compiler_params=pltpu.CompilerParams(vmem_limit_bytes=16 << 20),
        name="pack",
    )(core, keep, got, after)


def merge_kernel(parts_ref, out_ref):
    out_ref[...] = jnp.sum(parts_ref[...].astype(F32), 0).astype(BF16)


def merge(parts):
    return pl.pallas_call(
        merge_kernel,
        out_shape=shape((PIECE, LANES), BF16),
        in_specs=specs(1),
        out_specs=specs(1)[0],
        compiler_params=pltpu.CompilerParams(vmem_limit_bytes=16 << 20),
        name="merge",
    )(parts)


def spread_kernel(piece_ref, got_ref, after_ref, out_ref):
    total = piece_ref[...].astype(F32) + got_ref[...].astype(F32)
    out_ref[...] = jnp.broadcast_to(total[None], out_ref.shape).astype(BF16)


def spread(piece, got, after, copies):
    return pl.pallas_call(
        spread_kernel,
        out_shape=shape((copies, PIECE, LANES), BF16),
        in_specs=specs(2) + [pl.BlockSpec(memory_space=pl.ANY)],
        out_specs=specs(1)[0],
        compiler_params=pltpu.CompilerParams(vmem_limit_bytes=16 << 20),
        name="spread",
    )(piece, got, after)


def unpack_kernel(factor, core_ref, own_ref, other_ref, *out_refs):
    low = core_ref[0] == 0
    for half in range(2):
        lanes = slice(half * LANES, (half + 1) * LANES)
        first = low if half == 0 else jnp.logical_not(low)
        own = own_ref[...].astype(F32)
        other = other_ref[...].astype(F32)
        g = jnp.where(first, own, other) * factor
        depth = out_refs[0].shape[0]
        for i in range(5):
            out_refs[i][:, lanes] = g[:, 8 * i : 8 * i + 8, :].reshape(depth, LANES)
        out_refs[5][:, lanes] = g[0, 40:44, :]


def unpack(core, own, other, depth, factor):
    vm = pl.BlockSpec(memory_space=pltpu.VMEM)
    sm = pl.BlockSpec(memory_space=pltpu.SMEM)
    return pl.pallas_call(
        functools.partial(unpack_kernel, factor),
        out_shape=(jax.ShapeDtypeStruct((depth, depth), F32),) * 5
        + (jax.ShapeDtypeStruct((4, depth), F32),),
        in_specs=[sm, vm, vm],
        out_specs=(vm,) * 6,
        compiler_params=pltpu.CompilerParams(vmem_limit_bytes=32 << 20),
        name="unpack",
    )(core, own, other)


def exchange(a, axis, groups=None):
    return lax.all_to_all(
        a, axis, split_axis=0, concat_axis=0, tiled=True, axis_index_groups=groups
    )


def shards(x, up, hom, amino, wq, wk, wv, wg, bg, wo, gain, off):
    _, near, residues, depth = up.shape
    n_dp, n_dap = lax.axis_size("dp"), lax.axis_size("dap")
    lines, members = x.shape[1], x.shape[2]
    chips = n_dap // 2
    partner = [(i, i ^ 1) for i in range(n_dap)]
    same_core = [[2 * i + c for i in range(chips)] for c in range(2)]
    core = (lax.axis_index("dap") % 2).astype(jnp.int32).reshape(1)

    rows = jnp.transpose(up[0].reshape(near, n_dap, members, depth), (1, 2, 0, 3))
    local_up = exchange(rows.reshape(n_dap, members * near, depth), "dap")
    swapped = jnp.transpose(x[0], (1, 0, 2))
    gain, off, bg = gain[None], off[None], bg[None]
    saved = front(swapped, hom, wq, wk, wv, wg, bg, gain, off)
    keep, send = back(local_up, amino, core, saved, wq, wk, wv, wg, wo, gain)

    got = lax.ppermute(send, "dap", partner)
    parts = exchange(combine(core, keep, got), "dap", same_core)
    msa = exchange(pack(core, keep, got, parts), "dap", same_core)
    piece = merge(parts)
    near_z = [(i, i ^ 1) for i in range(n_dp)]
    near_x = [(i, i ^ 2) for i in range(n_dp)]
    mirror_x = [(i, n_dp - 2 - (i & ~1) + (i & 1)) for i in range(n_dp)]
    for pairs in (near_z, near_x):
        other = lax.ppermute(piece, "dp", pairs)
        piece = (piece.astype(F32) + other.astype(F32)).astype(BF16)
    pieces = spread(piece, lax.ppermute(piece, "dp", mirror_x), msa, chips)
    own = exchange(pieces, "dap", same_core)
    other = lax.ppermute(own, "dap", partner)
    factor = float((n_dp * lines * residues) ** (-0.5))
    grads = unpack(core, own, other, depth, factor)

    msa = msa.reshape(chips, depth // LANES, 2, members, near, LANES)
    adjoint = jnp.transpose(msa, (4, 0, 2, 3, 1, 5)).reshape(1, near, residues, depth)
    return (adjoint,) + tuple(grads)


def solution(mesh):
    in_specs = (
        P("dp", None, "dap", None),
        P("dp", "dap", None, None),
        P("dp", None),
        P("dp", "dap"),
    ) + (P(),) * 8
    out_specs = (P("dp", "dap", None, None),) + (P(),) * 6
    return jax.shard_map(shards, mesh=mesh, in_specs=in_specs, out_specs=out_specs, check_vma=False)
```

time: 150 us -> 146 us (0.973)
  local copies, waits for them, and re-layouts: 29.8 us -> 7.46 us
  blocking collectives: 66.6 us -> 49.3 us
  starting transfers between devices: 26.7 us -> 43.3 us
  waiting for transfers between devices: 1.71 us -> 16.3 us
  Pallas kernels: 23.8 us -> 27.8 us
    unnamed x59 -> x5, local copies, waits for them, and re-layouts: 26.1 us -> 3.8 us
    all_to_all x3 -> x2, blocking collectives: 66.6 us -> 49.3 us  [exchange(): lax.all_to_all(a, axis, split_axis=0, concat_axis=0, tiled=True, axis_ind...]
    ppermute x0 -> x3, starting transfers between devices: none -> 10.3 us  [the longest x2 5.9 us: shards(): other = lax.ppermute(piece, 'dp', pairs)]
    all_to_all x1 -> x2, waiting for transfers between devices: 0.01 us -> 8.42 us  [exchange(): lax.all_to_all(a, axis, split_axis=0, concat_axis=0, tiled=True, axis_ind...]
    all_to_all x1 -> x2, starting transfers between devices: 17.6 us -> 24.3 us  [exchange(): lax.all_to_all(a, axis, split_axis=0, concat_axis=0, tiled=True, axis_ind...]
    ppermute x0 -> x3, waiting for transfers between devices: none -> 5.56 us  [the longest x2 3.99 us: shards(): other = lax.ppermute(piece, 'dp', pairs)]
    pallas_call x5 -> x6, Pallas kernels: 22.7 us -> 26.6 us  [the longest x1 15.1 us: back(): pl.pallas_call(back_kernel, grid=(members, HEADS // GROUP), out_shape=(pa...]
  transfers between devices with their start and end apart: 3 -> 7, of which waited for: 1 -> 6; matrix products, arithmetic and copies ran while one was open for 2% -> 2% of each run, Pallas kernels for 7% -> 7%
where the time goes in v3:
time: 146 us; the launch traced here: 145 us
  blocking collectives  49.3 us (34%)
  starting transfers between devices  43.3 us (30%)
  Pallas kernels  27.8 us (19%)
  waiting for transfers between devices  16.3 us (11%)
  local copies, waits for them, and re-layouts  7.46 us (5%)
    all_to_all x2, blocking collectives, exchange(): lax.all_to_all(a, axis, split_axis=0, concat_axis=0, tiled=True, axis_ind...  49.3 us
    all_to_all x2, starting transfers between devices, exchange(): lax.all_to_all(a, axis, split_axis=0, concat_axis=0, tiled=True, axis_ind...  24.3 us
    pallas_call x1, Pallas kernels, back(): pl.pallas_call(back_kernel, grid=(members, HEADS // GROUP), out_shape=(pa...  15.1 us
    pallas_call x1, Pallas kernels, front(): pl.pallas_call(front_kernel, grid=(members, HEADS // GROUP), out_shape=ou...  10.4 us
    all_to_all x2, waiting for transfers between devices, exchange(): lax.all_to_all(a, axis, split_axis=0, concat_axis=0, tiled=True, axis_ind...  8.42 us
    ppermute x1, starting transfers between devices, shards(): other = lax.ppermute(own, 'dap', partner)  6.85 us
    ppermute x2, starting transfers between devices, shards(): other = lax.ppermute(piece, 'dp', pairs)  5.9 us
    ppermute x1, starting transfers between devices, shards(): pieces = spread(piece, lax.ppermute(piece, 'dp', mirror_x), msa, chips)  4.37 us
  transfers between devices with their start and end apart: 7, of which 6 were waited for; matrix products, arithmetic and copies ran while one was open for 2% of the time, Pallas kernels for 7%

profile of v3, /device:TPU:1, one launch (start us, length us, event | category | flops | bytes accessed | tf_op | source)
XLA Modules:
  0.0 144.9 jit_solution(7507714232395609717)
XLA Ops:
  0.6 2.1 %copy.22 = bf16[1,8,128,256]{3,1,2,0:T(8,128)(2,1)} copy(bf16[1,8,128,256]{3,2,1,0:T(8,128)(2,1)} %param.13) | data formatting | bytes 1048576 | tf_op jit(solution)/shard_map/reshape;squeeze | solution.py:426
  2.8 17.6 %all-to-all-start = ((bf16[64,16,256]{2,1,0:T(8,128)(2,1)}), bf16[64,16,256]{2,1,0:T(8,128)(2,1)S(1)}, u32[]{:S(2)}, u32[]{:S(2)}) async-start(bf16[64,16,256]{2,1,0:T(8,128)(2,1)} %bitcast.3), calls=%async_computation | async-start | bytes 1048576 | tf_op jit(solution)/shard_map/all_to_all | solution.py:412
  20.4 1.9 %copy.24 = bf16[1,512,2,256]{3,1,2,0:T(8,128)(2,1)} copy(bf16[1,512,2,256]{3,2,1,0:T(2,128)(2,1)} %param.12) | data formatting | bytes 1048576 | tf_op args[0]
  22.3 10.4 %attention_front.1 = (f32[2,512,256]{2,1,0:T(8,128)}, f32[2,512,128]{2,1,0:T(8,128)}, bf16[2,256,512]{2,1,0:T(8,128)(2,1)}, bf16[2,512,256]{2,1,0:T(8,128)(2,1)}...) custom-call(bf16[2,512,256]{2,1,0:T(8,128)(2,1)} %bitcast.18, ...), custom_call_target="tpu_custom_call" | custom-call | flops 4294967296 | bytes 14680064 | tf_op jit(solution)/shard_map/attention_front/pallas_call | solution.py:261
  32.7 7.2 %all-to-all-done.up_ref = bf16[64,16,256]{2,1,0:T(8,128)(2,1)S(1)} async-done(((bf16[64,16,256]{2,1,0:T(8,128)(2,1)}), bf16[64,16,256]{2,1,0:T(8,128)(2,1)S(1)}, u32[]{:S(2)}, u32[]{:S(2)}) %all-to-all-start) | async-done | bytes 524320 | tf_op jit(solution)/shard_map/all_to_all | solution.py:412
  40.0 0.0 copy-start.1
  40.0 0.8 copy-done.1
  40.8 15.1 %attention_back.1 = (bf16[32,80,128]{2,1,0:T(8,128)(2,1)}, bf16[32,80,128]{2,1,0:T(8,128)(2,1)}) custom-call(bf16[64,16,256]{2,1,0:T(8,128)(2,1)} %copy-done.1, s32[1,2]{1,0:T(1,128)} %amino_ref.1, s32[1]{0:T(128)} %bitcast.core_ref, f32[2,512,256]{2,1,0:T(8,128)} %get-tuple-element.24.xhat_ref, f32[2,512,128]{2,1,0:T(8,128)} %get-tuple-element.25.inv_ref, ...), custom_call_target="tpu_custom_call" | custom-call | flops 8589934592 | bytes 14680064 | tf_op jit(solution)/shard_map/attention_back/pallas_call | solution.py:283
  55.9 1.9 %collective-permute-start = (bf16[32,80,128]{2,1,0:T(8,128)(2,1)}, bf16[32,80,128]{2,1,0:T(8,128)(2,1)S(1)}, u32[]{:S(2)}, u32[]{:S(2)}) collective-permute-start(bf16[32,80,128]{2,1,0:T(8,128)(2,1)} %get-tuple-element.34), channel_id=1, source_target_pairs={{0,1},{1,0},{2,3},{3,2},{4,5},{5,4},{6,7},{7,6},{8,9},{9,8},{10,11... | collective-permute-start | bytes 1966088 | tf_op jit(solution)/shard_map/ppermute | solution.py:433
  57.9 2.3 %collective-permute-done.got_ref = bf16[32,80,128]{2,1,0:T(8,128)(2,1)S(1)} collective-permute-done((bf16[32,80,128]{2,1,0:T(8,128)(2,1)}, bf16[32,80,128]{2,1,0:T(8,128)(2,1)S(1)}, u32[]{:S(2)}, u32[]{:S(2)}) %collective-permute-start) | collective-permute-done | bytes 655392 | tf_op jit(solution)/shard_map/ppermute | solution.py:433
  60.1 0.0 copy-start
  60.1 1.1 copy-done
  61.2 0.1 combine.1
  61.3 19.7 %all_to_all.20.after_ref.parts_ref = bf16[32,48,128]{2,1,0:T(8,128)(2,1)S(1)} all-to-all(bf16[32,48,128]{2,1,0:T(8,128)(2,1)S(1)} %combine.1), channel_id=1, replica_groups={{0,2,4,6,8,10,12,14,16,18,20,22,24,26,28,30,32,34,36,38,40,42,44,46,48,..., dimensions={0} | all-to-all | bytes 786432 | tf_op jit(solution)/shard_map/all_to_all | solution.py:412
  81.0 0.9 pack.1
  81.9 6.7 %all-to-all-start.2 = ((bf16[32,64,128]{2,1,0:T(8,128)(2,1)}), bf16[32,64,128]{2,1,0:T(8,128)(2,1)S(1)}, u32[]{:S(2)}, u32[]{:S(2)}) async-start(bf16[32,64,128]{2,1,0:T(8,128)(2,1)} %pack.1), calls=%async_computation.2 | async-start | bytes 1048576 | tf_op jit(solution)/shard_map/all_to_all | solution.py:412
  88.6 0.1 merge.1
  88.6 2.8 %collective-permute-start.1 = (bf16[48,128]{1,0:T(8,128)(2,1)S(1)}, bf16[48,128]{1,0:T(8,128)(2,1)S(1)}, u32[]{:S(2)}, u32[]{:S(2)}) collective-permute-start(bf16[48,128]{1,0:T(8,128)(2,1)S(1)} %merge.1), channel_id=1, source_target_pairs={{0,64},{64,0},{128,192},{192,128},{256,320},{320,256},{384,448},{4... | collective-permute-start | bytes 36872 | tf_op jit(solution)/shard_map/ppermute | solution.py:441
  91.4 2.4 %collective-permute-done.1 = bf16[48,128]{1,0:T(8,128)(2,1)S(1)} collective-permute-done((bf16[48,128]{1,0:T(8,128)(2,1)S(1)}, bf16[48,128]{1,0:T(8,128)(2,1)S(1)}, u32[]{:S(2)}, u32[]{:S(2)}) %collective-permute-start.1) | collective-permute-done | bytes 12320 | tf_op jit(solution)/shard_map/ppermute | solution.py:441
  93.8 3.1 %collective-permute-start.2 = (bf16[48,128]{1,0:T(8,128)(2,1)S(1)}, bf16[48,128]{1,0:T(8,128)(2,1)S(1)}, u32[]{:S(2)}, u32[]{:S(2)}) collective-permute-start(bf16[48,128]{1,0:T(8,128)(2,1)S(1)} %add_convert_fusion.1), channel_id=1, source_target_pairs={{0,128},{64,192},{128,0},{192,64},{256,384},{320,448},{384,256},{4... | collective-permute-start | bytes 36872 | tf_op jit(solution)/shard_map/ppermute | solution.py:441
  96.9 1.6 %collective-permute-done.2 = bf16[48,128]{1,0:T(8,128)(2,1)S(1)} collective-permute-done((bf16[48,128]{1,0:T(8,128)(2,1)S(1)}, bf16[48,128]{1,0:T(8,128)(2,1)S(1)}, u32[]{:S(2)}, u32[]{:S(2)}) %collective-permute-start.2) | collective-permute-done | bytes 12320 | tf_op jit(solution)/shard_map/ppermute | solution.py:441
  98.6 4.4 %collective-permute-start.3 = (bf16[48,128]{1,0:T(8,128)(2,1)S(1)}, bf16[48,128]{1,0:T(8,128)(2,1)S(1)}, u32[]{:S(2)}, u32[]{:S(2)}) collective-permute-start(bf16[48,128]{1,0:T(8,128)(2,1)S(1)} %add_convert_fusion.piece_ref), channel_id=1, source_target_pairs={{0,384},{64,448},{128,256},{192,320},{256,128},{320,192},{384,0},{... | collective-permute-start | bytes 36872 | tf_op jit(solution)/shard_map/ppermute | solution.py:443
  102.9 1.6 %collective-permute-done.3.got_ref = bf16[48,128]{1,0:T(8,128)(2,1)S(1)} collective-permute-done((bf16[48,128]{1,0:T(8,128)(2,1)S(1)}, bf16[48,128]{1,0:T(8,128)(2,1)S(1)}, u32[]{:S(2)}, u32[]{:S(2)}) %collective-permute-start.3) | collective-permute-done | bytes 12320 | tf_op jit(solution)/shard_map/ppermute | solution.py:443
  104.5 1.2 all-to-all-done.2.after_ref
  105.7 29.7 %all_to_all.21.own_ref = bf16[32,48,128]{2,1,0:T(8,128)(2,1)S(1)} all-to-all(bf16[32,48,128]{2,1,0:T(8,128)(2,1)S(1)} %spread.1), channel_id=1, replica_groups={{0,2,4,6,8,10,12,14,16,18,20,22,24,26,28,30,32,34,36,38,40,42,44,46,48,..., dimensions={0} | all-to-all | bytes 786432 | tf_op jit(solution)/shard_map/all_to_all | solution.py:412
  135.4 6.8 %collective-permute-start.4 = (bf16[32,48,128]{2,1,0:T(8,128)(2,1)S(1)}, bf16[32,48,128]{2,1,0:T(8,128)(2,1)S(1)}, u32[]{:S(2)}, u32[]{:S(2)}) collective-permute-start(bf16[32,48,128]{2,1,0:T(8,128)(2,1)S(1)} %all_to_all.21.own_ref), channel_id=1, source_target_pairs={{0,1},{1,0},{2,3},{3,2},{4,5},{5,4},{6,7},{7,6},{8,9},{9,8},{10,11... | collective-permute-start | bytes 1179656 | tf_op jit(solution)/shard_map/ppermute | solution.py:445
  142.2 0.4 copy.21
  142.6 1.1 reshape.29
  143.8 0.0 collective-permute-done.4.other_ref
  143.8 1.1 unpack.1
  (3 shorter events, 0.0 us)
Async XLA Ops:
  2.8 37.2 %all-to-all-start = ((bf16[64,16,256]{2,1,0:T(8,128)(2,1)}), bf16[64,16,256]{2,1,0:T(8,128)(2,1)S(1)}, u32[]{:S(2)}, u32[]{:S(2)}) async-start(bf16[64,16,256]{2,1,0:T(8,128)(2,1)} %bitcast.3), calls=%async_computation | async-start | bytes 1048576 | tf_op jit(solution)/shard_map/all_to_all | solution.py:412
  40.0 0.8 copy-start.1
  55.9 4.2 %collective-permute-start = (bf16[32,80,128]{2,1,0:T(8,128)(2,1)}, bf16[32,80,128]{2,1,0:T(8,128)(2,1)S(1)}, u32[]{:S(2)}, u32[]{:S(2)}) collective-permute-start(bf16[32,80,128]{2,1,0:T(8,128)(2,1)} %get-tuple-element.34), channel_id=1, source_target_pairs={{0,1},{1,0},{2,3},{3,2},{4,5},{5,4},{6,7},{7,6},{8,9},{9,8},{10,11... | collective-permute-start | bytes 1966088 | tf_op jit(solution)/shard_map/ppermute | solution.py:433
  60.1 1.1 copy-start
  81.9 23.8 %all-to-all-start.2 = ((bf16[32,64,128]{2,1,0:T(8,128)(2,1)}), bf16[32,64,128]{2,1,0:T(8,128)(2,1)S(1)}, u32[]{:S(2)}, u32[]{:S(2)}) async-start(bf16[32,64,128]{2,1,0:T(8,128)(2,1)} %pack.1), calls=%async_computation.2 | async-start | bytes 1048576 | tf_op jit(solution)/shard_map/all_to_all | solution.py:412
  88.6 5.2 %collective-permute-start.1 = (bf16[48,128]{1,0:T(8,128)(2,1)S(1)}, bf16[48,128]{1,0:T(8,128)(2,1)S(1)}, u32[]{:S(2)}, u32[]{:S(2)}) collective-permute-start(bf16[48,128]{1,0:T(8,128)(2,1)S(1)} %merge.1), channel_id=1, source_target_pairs={{0,64},{64,0},{128,192},{192,128},{256,320},{320,256},{384,448},{4... | collective-permute-start | bytes 36872 | tf_op jit(solution)/shard_map/ppermute | solution.py:441
  93.8 4.7 %collective-permute-start.2 = (bf16[48,128]{1,0:T(8,128)(2,1)S(1)}, bf16[48,128]{1,0:T(8,128)(2,1)S(1)}, u32[]{:S(2)}, u32[]{:S(2)}) collective-permute-start(bf16[48,128]{1,0:T(8,128)(2,1)S(1)} %add_convert_fusion.1), channel_id=1, source_target_pairs={{0,128},{64,192},{128,0},{192,64},{256,384},{320,448},{384,256},{4... | collective-permute-start | bytes 36872 | tf_op jit(solution)/shard_map/ppermute | solution.py:441
  98.6 5.9 %collective-permute-start.3 = (bf16[48,128]{1,0:T(8,128)(2,1)S(1)}, bf16[48,128]{1,0:T(8,128)(2,1)S(1)}, u32[]{:S(2)}, u32[]{:S(2)}) collective-permute-start(bf16[48,128]{1,0:T(8,128)(2,1)S(1)} %add_convert_fusion.piece_ref), channel_id=1, source_target_pairs={{0,384},{64,448},{128,256},{192,320},{256,128},{320,192},{384,0},{... | collective-permute-start | bytes 36872 | tf_op jit(solution)/shard_map/ppermute | solution.py:443
  135.4 8.4 %collective-permute-start.4 = (bf16[32,48,128]{2,1,0:T(8,128)(2,1)S(1)}, bf16[32,48,128]{2,1,0:T(8,128)(2,1)S(1)}, u32[]{:S(2)}, u32[]{:S(2)}) collective-permute-start(bf16[32,48,128]{2,1,0:T(8,128)(2,1)S(1)} %all_to_all.21.own_ref), channel_id=1, source_target_pairs={{0,1},{1,0},{2,3},{3,2},{4,5},{5,4},{6,7},{7,6},{8,9},{9,8},{10,11... | collective-permute-start | bytes 1179656 | tf_op jit(solution)/shard_map/ppermute | solution.py:445

commit v4 on v3

--- a/solution.py
+++ b/solution.py
@@ -10,8 +10,8 @@
 HEADS = 8
 HEAD_DIM = 32
 LANES = 128
-PIECE = 48
-MSA = 32
+PIECE = 24
+MSA = 16
 GROUP = 8
 VMEM_BYTES = 60 << 20
 EPS = 1e-05
@@ -202,22 +202,19 @@
     def _():
         low = core_ref[0] == 0
         chips = depth // 8
-        pairs = jnp.concatenate([out_s[i] for i in range(members)], 1)
-        pairs = pairs.reshape(chips, 2, 8 * members, depth)
-        for half in range(2):
-            lanes = slice(half * LANES, (half + 1) * LANES)
-            rows = slice(16 * half, 16 * half + 16)
-            zero, one = pairs[:, 0, :, lanes], pairs[:, 1, :, lanes]
-            keep_ref[:, rows, :] = jnp.where(low, zero, one).astype(BF16)
-            send_ref[:, rows, :] = jnp.where(low, one, zero).astype(BF16)
+        rows = jnp.concatenate([out_s[i] for i in range(members)], 1)
+        rows = rows.reshape(chips, 2, MSA, depth)
         pieces = []
         for half in range(2):
             lanes = slice(half * LANES, (half + 1) * LANES)
             parts = [grad_s[i][:, lanes].reshape(chips, 8, LANES) for i in range(5)]
             parts.append(jnp.broadcast_to(vec_s[:, lanes][None], (chips, 8, LANES)))
-            pieces.append(jnp.concatenate(parts, 1))
-        keep_ref[:, MSA:, :] = jnp.where(low, pieces[0], pieces[1]).astype(BF16)
-        send_ref[:, MSA:, :] = jnp.where(low, pieces[1], pieces[0]).astype(BF16)
+            left, right = jnp.concatenate(parts[:3], 1), jnp.concatenate(parts[3:], 1)
+            pieces.append(jnp.concatenate([left, right], 2))
+        zero = jnp.concatenate([rows[:, 0], pieces[0]], 1)
+        one = jnp.concatenate([rows[:, 1], pieces[1]], 1)
+        keep_ref[...] = jnp.where(low, zero, one).astype(BF16)
+        send_ref[...] = jnp.where(low, one, zero).astype(BF16)
 
 
 def specs(n):
@@ -279,7 +276,7 @@
     members, lines, depth = saved[0].shape
     tall, wide = (lines, depth), (depth, lines)
     pairs = members * HEADS
-    parcel = shape((depth // 8, MSA + PIECE, LANES), BF16)
+    parcel = shape((depth // 8, MSA + PIECE, depth), BF16)
     return pl.pallas_call(
         back_kernel,
         grid=(members, HEADS // GROUP),
@@ -313,85 +310,81 @@
 
 
 def combine_kernel(core_ref, keep_ref, got_ref, out_ref):
-    total = keep_ref[:, MSA:, :].astype(F32) + got_ref[:, MSA:, :].astype(F32)
-    out_ref[...] = total.astype(BF16)
+    low = core_ref[0] == 0
+    keep, got = keep_ref[...].astype(F32), got_ref[...].astype(F32)
+    first = jnp.where(low, keep[:, :MSA], got[:, :MSA])
+    second = jnp.where(low, got[:, :MSA], keep[:, :MSA])
+    total = keep[:, MSA:] + got[:, MSA:]
+    out_ref[...] = jnp.concatenate([first, second, total], 1).astype(BF16)
 
 
 def combine(core, keep, got):
+    chips, _, depth = keep.shape
     return pl.pallas_call(
         combine_kernel,
-        out_shape=shape((keep.shape[0], PIECE, LANES), BF16),
+        out_shape=shape((chips, 2 * MSA + PIECE, depth), BF16),
         in_specs=[SMEM] + specs(2),
         out_specs=specs(1)[0],
-        compiler_params=pltpu.CompilerParams(vmem_limit_bytes=16 << 20),
+        compiler_params=pltpu.CompilerParams(vmem_limit_bytes=24 << 20),
         name="combine",
     )(core, keep, got)
 
 
-def pack_kernel(core_ref, keep_ref, got_ref, after_ref, out_ref):
-    low = core_ref[0] == 0
-    for half in range(2):
-        rows = slice(16 * half, 16 * half + 16)
-        keep, got = keep_ref[:, rows, :], got_ref[:, rows, :]
-        at = 32 * half
-        out_ref[:, at : at + 16, :] = jnp.where(low, keep, got)
-        out_ref[:, at + 16 : at + 32, :] = jnp.where(low, got, keep)
-
-
-def pack(core, keep, got, after):
-    return pl.pallas_call(
-        pack_kernel,
-        out_shape=shape((keep.shape[0], 2 * MSA, LANES), BF16),
-        in_specs=[SMEM] + specs(2) + [pl.BlockSpec(memory_space=pl.ANY)],
-        out_specs=specs(1)[0],
-        compiler_params=pltpu.CompilerParams(vmem_limit_bytes=16 << 20),
-        name="pack",
-    )(core, keep, got, after)
-
-
 def merge_kernel(parts_ref, out_ref):
-    out_ref[...] = jnp.sum(parts_ref[...].astype(F32), 0).astype(BF16)
-
-
-def merge(parts):
+    start = parts_ref.shape[1] - PIECE
+    total = jnp.sum(parts_ref[...].astype(F32)[:, start:], 0, keepdims=True)
+    out_ref[...] = jnp.broadcast_to(total, out_ref.shape).astype(BF16)
+
+
+def merge(parts, copies):
     return pl.pallas_call(
         merge_kernel,
-        out_shape=shape((PIECE, LANES), BF16),
+        out_shape=shape((copies, PIECE, parts.shape[2]), BF16),
         in_specs=specs(1),
         out_specs=specs(1)[0],
-        compiler_params=pltpu.CompilerParams(vmem_limit_bytes=16 << 20),
+        compiler_params=pltpu.CompilerParams(vmem_limit_bytes=24 << 20),
         name="merge",
     )(parts)
 
 
-def spread_kernel(piece_ref, got_ref, after_ref, out_ref):
-    total = piece_ref[...].astype(F32) + got_ref[...].astype(F32)
-    out_ref[...] = jnp.broadcast_to(total[None], out_ref.shape).astype(BF16)
-
-
-def spread(piece, got, after, copies):
-    return pl.pallas_call(
-        spread_kernel,
-        out_shape=shape((copies, PIECE, LANES), BF16),
-        in_specs=specs(2) + [pl.BlockSpec(memory_space=pl.ANY)],
+def gather_kernel(up_ref, out_ref, rows_s):
+    near, residues, depth = up_ref.shape
+    for half in range(depth // LANES):
+        lanes = slice(half * LANES, (half + 1) * LANES)
+        rows_s[...] = up_ref[:, :, lanes].astype(F32).reshape(near * residues, LANES)
+        for n in range(0, residues, 2):
+            pair = [rows_s[pl.ds(n + r, near, stride=residues), :] for r in range(2)]
+            out_ref[n // 2, :, lanes] = jnp.concatenate(pair, 0).astype(BF16)
+
+
+def gather_rows(up):
+    near, residues, depth = up.shape
+    return pl.pallas_call(
+        gather_kernel,
+        out_shape=shape((residues // 2, 2 * near, depth), BF16),
+        in_specs=specs(1),
         out_specs=specs(1)[0],
+        scratch_shapes=[pltpu.VMEM((near * residues, LANES), F32)],
         compiler_params=pltpu.CompilerParams(vmem_limit_bytes=16 << 20),
-        name="spread",
-    )(piece, got, after)
+        name="gather_rows",
+    )(up)
 
 
 def unpack_kernel(factor, core_ref, own_ref, other_ref, *out_refs):
     low = core_ref[0] == 0
+    own, other = own_ref[...].astype(F32), other_ref[...].astype(F32)
+    depth = out_refs[0].shape[0]
     for half in range(2):
         lanes = slice(half * LANES, (half + 1) * LANES)
         first = low if half == 0 else jnp.logical_not(low)
-        own = own_ref[...].astype(F32)
-        other = other_ref[...].astype(F32)
         g = jnp.where(first, own, other) * factor
-        depth = out_refs[0].shape[0]
-        for i in range(5):
-            out_refs[i][:, lanes] = g[:, 8 * i : 8 * i + 8, :].reshape(depth, LANES)
-        out_refs[5][:, lanes] = g[0, 40:44, :]
+        for i in range(6):
+            side, at = i // 3, 8 * (i % 3)
+            block = g[:, at : at + 8, side * LANES : (side + 1) * LANES]
+            if i < 5:
+                out_refs[i][:, lanes] = block.reshape(depth, LANES)
+            else:
+                out_refs[i][:, lanes] = block[0, :4]
 
 
 def unpack(core, own, other, depth, factor):
@@ -423,8 +416,7 @@
     same_core = [[2 * i + c for i in range(chips)] for c in range(2)]
     core = (lax.axis_index("dap") % 2).astype(jnp.int32).reshape(1)
 
-    rows = jnp.transpose(up[0].reshape(near, n_dap, members, depth), (1, 2, 0, 3))
-    local_up = exchange(rows.reshape(n_dap, members * near, depth), "dap")
+    local_up = exchange(gather_rows(up[0]), "dap")
     swapped = jnp.transpose(x[0], (1, 0, 2))
     gain, off, bg = gain[None], off[None], bg[None]
     saved = front(swapped, hom, wq, wk, wv, wg, bg, gain, off)
@@ -432,22 +424,14 @@
 
     got = lax.ppermute(send, "dap", partner)
     parts = exchange(combine(core, keep, got), "dap", same_core)
-    msa = exchange(pack(core, keep, got, parts), "dap", same_core)
-    piece = merge(parts)
-    near_z = [(i, i ^ 1) for i in range(n_dp)]
-    near_x = [(i, i ^ 2) for i in range(n_dp)]
-    mirror_x = [(i, n_dp - 2 - (i & ~1) + (i & 1)) for i in range(n_dp)]
-    for pairs in (near_z, near_x):
-        other = lax.ppermute(piece, "dp", pairs)
-        piece = (piece.astype(F32) + other.astype(F32)).astype(BF16)
-    pieces = spread(piece, lax.ppermute(piece, "dp", mirror_x), msa, chips)
-    own = exchange(pieces, "dap", same_core)
+    pieces = exchange(merge(parts, n_dp), "dp")
+    own = exchange(merge(pieces, chips), "dap", same_core)
     other = lax.ppermute(own, "dap", partner)
     factor = float((n_dp * lines * residues) ** (-0.5))
     grads = unpack(core, own, other, depth, factor)
 
-    msa = msa.reshape(chips, depth // LANES, 2, members, near, LANES)
-    adjoint = jnp.transpose(msa, (4, 0, 2, 3, 1, 5)).reshape(1, near, residues, depth)
+    msa = parts[:, : 2 * MSA].reshape(chips, 2, members, near, depth)
+    adjoint = jnp.transpose(msa, (3, 0, 1, 2, 4)).reshape(1, near, residues, depth)
     return (adjoint,) + tuple(grads)
 
 

time: 146 us -> 131 us (0.90)
  starting transfers between devices: 43.3 us -> 26.3 us
  blocking collectives: 49.3 us -> 59.8 us
  waiting for transfers between devices: 16.3 us -> 9.91 us
  local copies, waits for them, and re-layouts: 7.46 us -> 5.77 us
    all_to_all x2 -> x3, blocking collectives: 49.3 us -> 59.8 us  [exchange(): lax.all_to_all(a, axis, split_axis=0, concat_axis=0, tiled=True, axis_ind...]
    ppermute x3 -> x0, starting transfers between devices: 10.3 us -> none  [the longest x2 5.9 us: shards(): other = lax.ppermute(piece, 'dp', pairs)]
    all_to_all x2 -> x1, starting transfers between devices: 24.3 us -> 17.6 us  [exchange(): lax.all_to_all(a, axis, split_axis=0, concat_axis=0, tiled=True, axis_ind...]
    ppermute x3 -> x0, waiting for transfers between devices: 5.56 us -> none  [the longest x2 3.99 us: shards(): other = lax.ppermute(piece, 'dp', pairs)]
    another operation x1 -> x0, local copies, waits for them, and re-layouts: 2.13 us -> none  [shards(): up[0].reshape(near, n_dap, members, depth)]
    all_to_all x2 -> x1, waiting for transfers between devices: 8.42 us -> 7.27 us  [exchange(): lax.all_to_all(a, axis, split_axis=0, concat_axis=0, tiled=True, axis_ind...]
    unnamed x5 -> x7, local copies, waits for them, and re-layouts: 3.8 us -> 4.82 us
  transfers between devices with their start and end apart: 7 -> 3, of which waited for: 6 -> 3; matrix products, arithmetic and copies ran while one was open for 2% -> 2% of each run, Pallas kernels for 7% -> 8%
where the time goes in v4:
time: 131 us
  blocking collectives  59.8 us (46%)
  Pallas kernels  28.4 us (22%)
  starting transfers between devices  26.3 us (20%)
  waiting for transfers between devices  9.91 us (8%)
  local copies, waits for them, and re-layouts  5.77 us (4%)
    all_to_all x3, blocking collectives, exchange(): lax.all_to_all(a, axis, split_axis=0, concat_axis=0, tiled=True, axis_ind...  59.8 us
    all_to_all x1, starting transfers between devices, exchange(): lax.all_to_all(a, axis, split_axis=0, concat_axis=0, tiled=True, axis_ind...  17.6 us
    pallas_call x1, Pallas kernels, back(): pl.pallas_call(back_kernel, grid=(members, HEADS // GROUP), out_shape=(pa...  15.2 us
    pallas_call x1, Pallas kernels, front(): pl.pallas_call(front_kernel, grid=(members, HEADS // GROUP), out_shape=ou...  10.4 us
    all_to_all x1, waiting for transfers between devices, exchange(): lax.all_to_all(a, axis, split_axis=0, concat_axis=0, tiled=True, axis_ind...  7.27 us
    ppermute x1, starting transfers between devices, shards(): other = lax.ppermute(own, 'dap', partner)  6.72 us
    unnamed x7, local copies, waits for them, and re-layouts  4.82 us
  transfers between devices with their start and end apart: 3, of which 3 were waited for; matrix products, arithmetic and copies ran while one was open for 2% of the time, Pallas kernels for 8%

profile of v4, /device:TPU:1, one launch (start us, length us, event | category | flops | bytes accessed | tf_op | source)
XLA Modules:
  0.0 130.8 jit_solution(7776360244600287022)
XLA Ops:
  0.6 0.0 copy-start.1
  0.6 1.0 copy-done.1
  1.7 1.5 %gather_rows.1 = bf16[64,16,256]{2,1,0:T(8,128)(2,1)} custom-call(bf16[8,128,256]{2,1,0:T(8,128)(2,1)S(1)} %bitcast.15), custom_call_target="tpu_custom_call" | custom-call | tf_op jit(solution)/shard_map/gather_rows/pallas_call | solution.py:362
  3.1 17.6 %all-to-all-start = ((bf16[64,16,256]{2,1,0:T(8,128)(2,1)}), bf16[64,16,256]{2,1,0:T(8,128)(2,1)S(1)}, u32[]{:S(2)}, u32[]{:S(2)}) async-start(bf16[64,16,256]{2,1,0:T(8,128)(2,1)} %gather_rows.1), calls=%async_computation | async-start | bytes 1048576 | tf_op jit(solution)/shard_map/all_to_all | solution.py:405
  20.8 1.9 %copy.23 = bf16[1,512,2,256]{3,1,2,0:T(8,128)(2,1)} copy(bf16[1,512,2,256]{3,2,1,0:T(2,128)(2,1)} %param.12) | data formatting | bytes 1048576 | tf_op args[0]
  22.7 10.4 %attention_front.1 = (f32[2,512,256]{2,1,0:T(8,128)}, f32[2,512,128]{2,1,0:T(8,128)}, bf16[2,256,512]{2,1,0:T(8,128)(2,1)}, bf16[2,512,256]{2,1,0:T(8,128)(2,1)}...) custom-call(bf16[2,512,256]{2,1,0:T(8,128)(2,1)} %bitcast.17, ...), custom_call_target="tpu_custom_call" | custom-call | flops 4294967296 | bytes 14680064 | tf_op jit(solution)/shard_map/attention_front/pallas_call | solution.py:258
  33.1 7.3 %all-to-all-done.up_ref = bf16[64,16,256]{2,1,0:T(8,128)(2,1)S(1)} async-done(((bf16[64,16,256]{2,1,0:T(8,128)(2,1)}), bf16[64,16,256]{2,1,0:T(8,128)(2,1)S(1)}, u32[]{:S(2)}, u32[]{:S(2)}) %all-to-all-start) | async-done | bytes 524320 | tf_op jit(solution)/shard_map/all_to_all | solution.py:405
  40.4 0.0 copy-start.2
  40.4 0.8 copy-done.2
  41.1 15.2 %attention_back.1 = (bf16[32,40,256]{2,1,0:T(8,128)(2,1)}, bf16[32,40,256]{2,1,0:T(8,128)(2,1)}) custom-call(bf16[64,16,256]{2,1,0:T(8,128)(2,1)} %copy-done.2, s32[1,2]{1,0:T(1,128)} %amino_ref.1, s32[1]{0:T(128)} %bitcast.core_ref, f32[2,512,256]{2,1,0:T(8,128)} %get-tuple-element.24.xhat_ref, f32[2,512,128]{2,1,0:T(8,128)} %get-tuple-element.25.inv_ref, ...), custom_call_target="tpu_custom_call" | custom-call | flops 8589934592 | bytes 14680064 | tf_op jit(solution)/shard_map/attention_back/pallas_call | solution.py:280
  56.3 1.9 %collective-permute-start = (bf16[32,40,256]{2,1,0:T(8,128)(2,1)}, bf16[32,40,256]{2,1,0:T(8,128)(2,1)S(1)}, u32[]{:S(2)}, u32[]{:S(2)}) collective-permute-start(bf16[32,40,256]{2,1,0:T(8,128)(2,1)} %get-tuple-element.34), channel_id=1, source_target_pairs={{0,1},{1,0},{2,3},{3,2},{4,5},{5,4},{6,7},{7,6},{8,9},{9,8},{10,11... | collective-permute-start | bytes 1966088 | tf_op jit(solution)/shard_map/ppermute | solution.py:425
  58.2 2.3 %collective-permute-done.got_ref = bf16[32,40,256]{2,1,0:T(8,128)(2,1)S(1)} collective-permute-done((bf16[32,40,256]{2,1,0:T(8,128)(2,1)}, bf16[32,40,256]{2,1,0:T(8,128)(2,1)S(1)}, u32[]{:S(2)}, u32[]{:S(2)}) %collective-permute-start) | collective-permute-done | bytes 655392 | tf_op jit(solution)/shard_map/ppermute | solution.py:425
  60.5 0.0 copy-start
  60.5 1.1 copy-done
  61.6 0.2 combine.1
  61.8 30.4 %all_to_all.20.parts_ref = bf16[32,56,256]{2,1,0:T(8,128)(2,1)S(1)} all-to-all(bf16[32,56,256]{2,1,0:T(8,128)(2,1)S(1)} %combine.1), channel_id=1, replica_groups={{0,2,4,6,8,10,12,14,16,18,20,22,24,26,28,30,32,34,36,38,40,42,44,46,48,..., dimensions={0} | all-to-all | bytes 1835008 | tf_op jit(solution)/shard_map/all_to_all | solution.py:405
  92.2 0.1 merge.2
  92.3 9.8 %all_to_all.21.parts_ref = bf16[8,24,256]{2,1,0:T(8,128)(2,1)S(1)} all-to-all(bf16[8,24,256]{2,1,0:T(8,128)(2,1)S(1)} %merge.2), channel_id=1, replica_groups=mesh['dp'=8,'dap'=64] {'dp'}, dimensions={0} | all-to-all | bytes 196608 | tf_op jit(solution)/shard_map/all_to_all | solution.py:405
  102.1 19.5 %all_to_all.22.own_ref = bf16[32,24,256]{2,1,0:T(8,128)(2,1)S(1)} all-to-all(bf16[32,24,256]{2,1,0:T(8,128)(2,1)S(1)} %merge.3), channel_id=1, replica_groups={{0,2,4,6,8,10,12,14,16,18,20,22,24,26,28,30,32,34,36,38,40,42,44,46,48,..., dimensions={0} | all-to-all | bytes 786432 | tf_op jit(solution)/shard_map/all_to_all | solution.py:405
  121.7 6.7 %collective-permute-start.1 = (bf16[32,24,256]{2,1,0:T(8,128)(2,1)S(1)}, bf16[32,24,256]{2,1,0:T(8,128)(2,1)S(1)}, u32[]{:S(2)}, u32[]{:S(2)}) collective-permute-start(bf16[32,24,256]{2,1,0:T(8,128)(2,1)S(1)} %all_to_all.22.own_ref), channel_id=1, source_target_pairs={{0,1},{1,0},{2,3},{3,2},{4,5},{5,4},{6,7},{7,6},{8,9},{9,8},{10,11... | collective-permute-start | bytes 1179656 | tf_op jit(solution)/shard_map/ppermute | solution.py:429
  128.4 0.1 slice.4
  128.5 0.9 copy.21
  129.4 0.4 collective-permute-done.1.other_ref
  129.7 1.1 unpack.1
  (1 shorter events, 0.0 us)
Async XLA Ops:
  0.6 1.0 copy-start.1
  3.1 37.2 %all-to-all-start = ((bf16[64,16,256]{2,1,0:T(8,128)(2,1)}), bf16[64,16,256]{2,1,0:T(8,128)(2,1)S(1)}, u32[]{:S(2)}, u32[]{:S(2)}) async-start(bf16[64,16,256]{2,1,0:T(8,128)(2,1)} %gather_rows.1), calls=%async_computation | async-start | bytes 1048576 | tf_op jit(solution)/shard_map/all_to_all | solution.py:405
  40.4 0.8 copy-start.2
  56.3 4.2 %collective-permute-start = (bf16[32,40,256]{2,1,0:T(8,128)(2,1)}, bf16[32,40,256]{2,1,0:T(8,128)(2,1)S(1)}, u32[]{:S(2)}, u32[]{:S(2)}) collective-permute-start(bf16[32,40,256]{2,1,0:T(8,128)(2,1)} %get-tuple-element.34), channel_id=1, source_target_pairs={{0,1},{1,0},{2,3},{3,2},{4,5},{5,4},{6,7},{7,6},{8,9},{9,8},{10,11... | collective-permute-start | bytes 1966088 | tf_op jit(solution)/shard_map/ppermute | solution.py:425
  60.5 1.1 copy-start
  121.7 8.1 %collective-permute-start.1 = (bf16[32,24,256]{2,1,0:T(8,128)(2,1)S(1)}, bf16[32,24,256]{2,1,0:T(8,128)(2,1)S(1)}, u32[]{:S(2)}, u32[]{:S(2)}) collective-permute-start(bf16[32,24,256]{2,1,0:T(8,128)(2,1)S(1)} %all_to_all.22.own_ref), channel_id=1, source_target_pairs={{0,1},{1,0},{2,3},{3,2},{4,5},{5,4},{6,7},{7,6},{8,9},{9,8},{10,11... | collective-permute-start | bytes 1179656 | tf_op jit(solution)/shard_map/ppermute | solution.py:429

commit v5 on v4

--- a/solution.py
+++ b/solution.py
@@ -14,6 +14,8 @@
 MSA = 16
 GROUP = 8
 VMEM_BYTES = 60 << 20
+FRONT_BYTES = 51 << 20
+BACK_BYTES = 50 << 20
 EPS = 1e-05
 MASKED = 1000000000.0
 F32, BF16 = jnp.float32, jnp.bfloat16
@@ -33,39 +35,38 @@
 
 def front_kernel(
     x_ref,
-    hom_ref,
-    wq_ref,
-    wk_ref,
-    wv_ref,
-    wg_ref,
-    bg_ref,
-    gain_ref,
-    off_ref,
-    xhat_ref,
-    inv_ref,
-    nt_ref,
-    k_ref,
-    v_ref,
-    qt_ref,
-    gate_ref,
-    att_ref,
-    probs_ref,
-    q_s,
+    *refs,
 ):
+    ins, outs, scratch = refs[:8], refs[8:17], refs[17:]
+    xhat_ref, inv_ref, nt_ref, k_ref, v_ref, qt_ref, gate_ref, att_ref, probs_ref = outs
+    bufs, (q_s, sems) = scratch[:8], scratch[8:]
+    hom_ref, wq_ref, wk_ref, wv_ref, wg_ref, bg_ref, gain_ref, off_ref = bufs
     _, lines, depth = x_ref.shape
     group = probs_ref.shape[1]
+    r = pl.program_id(0)
+    loads = [pltpu.make_async_copy(ins[i], bufs[i], sems.at[i]) for i in range(8)]
     step = pl.program_id(1)
-    bias = (hom_ref[...].astype(F32) - 1.0) * MASKED
     lane_head = lax.broadcasted_iota(jnp.int32, (1, depth), 1) // HEAD_DIM
 
     @pl.when(step == 0)
     def _():
+        @pl.when(r == 0)
+        def _():
+            for load in loads:
+                load.start()
+
         x = x_ref[0].astype(F32)
         centred = x - jnp.mean(x, -1, keepdims=True)
         inv = lax.rsqrt(jnp.mean(centred * centred, -1, keepdims=True) + EPS)
         xhat = centred * inv
+
+        @pl.when(r == 0)
+        def _():
+            for load in loads:
+                load.wait()
+
         xhat_ref[0] = xhat
-        inv_ref[0] = jnp.broadcast_to(inv, (lines, LANES))
+        inv_ref[0] = jnp.broadcast_to(inv, (lines, LANES)).T[:8]
         normed = (xhat * gain_ref[...] + off_ref[...]).astype(BF16)
         nt_ref[0] = normed.T
         query = (mm(normed, wq_ref[...]) * HEAD_DIM**-0.5).astype(BF16)
@@ -76,6 +77,7 @@
         gate_ref[0] = jax.nn.sigmoid(mm(normed, wg_ref[...]) + bg_ref[...])
         att_ref[0] = jnp.zeros((lines, depth), F32)
 
+    bias = (hom_ref[...].astype(F32) - 1.0) * MASKED
     for j in range(group):
         own = (lane_head == step * group + j).astype(F32).astype(BF16)
         raised = jnp.exp(against(q_s[...] * own, k_ref[0]) + bias)
@@ -173,7 +175,7 @@
             + against(d_logit, wg_ref[...])
         )
         d_hat = d_normed * gain_ref[...]
-        d_branch = inv_ref[0][:, :1] * (
+        d_branch = inv_ref[0].T[:, :1] * (
             d_hat
             - jnp.mean(d_hat, -1, keepdims=True)
             - xhat * jnp.mean(d_hat * xhat, -1, keepdims=True)
@@ -222,12 +224,17 @@
 
 
 SMEM = pl.BlockSpec(memory_space=pltpu.SMEM)
+HBM = pl.BlockSpec(memory_space=pltpu.HBM)
 
 
 def shape(dims, dtype):
     return jax.ShapeDtypeStruct(dims, dtype)
 
 
+def in_hbm(a):
+    return pltpu.with_memory_space_constraint(a, pltpu.HBM)
+
+
 def whole(a):
     return pl.BlockSpec(a.shape, lambda r, h: (0,) * len(a.shape))
 
@@ -241,12 +248,14 @@
 
 
 def front(x, hom, wq, wk, wv, wg, bg, gain, off):
+    fixed = (hom, wq, wk, wv, wg, bg, gain, off)
+    fixed = tuple(in_hbm(a) for a in fixed)
     members, lines, depth = x.shape
     tall, wide = (members, lines, depth), (members, depth, lines)
     pairs = members * HEADS
     outs = (
         shape(tall, F32),
-        shape((members, lines, LANES), F32),
+        shape((members, 8, lines), F32),
         shape(wide, BF16),
         shape(tall, BF16),
         shape(tall, BF16),
@@ -259,21 +268,24 @@
         front_kernel,
         grid=(members, HEADS // GROUP),
         out_shape=outs,
-        in_specs=[by_member(x)] + [whole(a) for a in (hom, wq, wk, wv, wg, bg, gain, off)],
+        in_specs=[by_member(x)] + [HBM] * len(fixed),
         out_specs=[by_member(a) for a in outs[:-1]] + [by_group(outs[-1])],
-        scratch_shapes=[pltpu.VMEM((lines, depth), BF16)],
-        compiler_params=pltpu.CompilerParams(vmem_limit_bytes=VMEM_BYTES),
+        scratch_shapes=[pltpu.VMEM(a.shape, a.dtype) for a in fixed]
+        + [pltpu.VMEM((lines, depth), BF16), pltpu.SemaphoreType.DMA((len(fixed),))],
+        compiler_params=pltpu.CompilerParams(vmem_limit_bytes=FRONT_BYTES),
         cost_estimate=pl.CostEstimate(
             flops=pairs * 32 * lines * lines * HEAD_DIM,
             bytes_accessed=14 << 20,
             transcendentals=pairs * lines * lines,
         ),
         name="attention_front",
-    )(x, hom, wq, wk, wv, wg, bg, gain, off)
+    )(x, *fixed)
 
 
 def back(up, amino, core, saved, wq, wk, wv, wg, wo, gain):
-    members, lines, depth = saved[0].shape
+    xhat, inv, nt, k, v, qt, gate, att, probs = saved
+    saved = (in_hbm(xhat), inv, nt, k, v, *(in_hbm(a) for a in (qt, gate, att, probs)))
+    members, lines, depth = xhat.shape
     tall, wide = (lines, depth), (depth, lines)
     pairs = members * HEADS
     parcel = shape((depth // 8, MSA + PIECE, depth), BF16)
@@ -299,7 +311,7 @@
             pltpu.VMEM((5, depth, depth), F32),
             pltpu.VMEM((8, depth), F32),
         ],
-        compiler_params=pltpu.CompilerParams(vmem_limit_bytes=VMEM_BYTES),
+        compiler_params=pltpu.CompilerParams(vmem_limit_bytes=BACK_BYTES),
         cost_estimate=pl.CostEstimate(
             flops=pairs * 64 * lines * lines * HEAD_DIM,
             bytes_accessed=14 << 20,
@@ -365,7 +377,7 @@
         in_specs=specs(1),
         out_specs=specs(1)[0],
         scratch_shapes=[pltpu.VMEM((near * residues, LANES), F32)],
-        compiler_params=pltpu.CompilerParams(vmem_limit_bytes=16 << 20),
+        compiler_params=pltpu.CompilerParams(vmem_limit_bytes=VMEM_BYTES),
         name="gather_rows",
     )(up)
 

time: 131 us -> 127 us (0.969)
  local copies, waits for them, and re-layouts: 5.77 us -> 3.02 us
    unnamed x7 -> x17, local copies, waits for them, and re-layouts: 4.82 us -> 2.07 us
    pallas_call x1, Pallas kernels: 15.2 us -> 13.4 us  [back(): pl.pallas_call(back_kernel, grid=(members, HEADS // GROUP), out_shape=(pa...]
where the time goes in v5:
time: 127 us
  blocking collectives  59.9 us (47%)
  Pallas kernels  27.9 us (22%)
  starting transfers between devices  26.2 us (21%)
  waiting for transfers between devices  9.22 us (7%)
  local copies, waits for them, and re-layouts  3.02 us (2%)
    all_to_all x3, blocking collectives, exchange(): lax.all_to_all(a, axis, split_axis=0, concat_axis=0, tiled=True, axis_ind...  59.9 us
    all_to_all x1, starting transfers between devices, exchange(): lax.all_to_all(a, axis, split_axis=0, concat_axis=0, tiled=True, axis_ind...  17.6 us
    pallas_call x1, Pallas kernels, back(): pl.pallas_call(back_kernel, grid=(members, HEADS // GROUP), out_shape=(pa...  13.4 us
    pallas_call x1, Pallas kernels, front(): pl.pallas_call(front_kernel, grid=(members, HEADS // GROUP), out_shape=ou...  10.6 us
    all_to_all x1, waiting for transfers between devices, exchange(): lax.all_to_all(a, axis, split_axis=0, concat_axis=0, tiled=True, axis_ind...  6.8 us
    ppermute x1, starting transfers between devices, shards(): other = lax.ppermute(own, 'dap', partner)  6.63 us
  transfers between devices with their start and end apart: 3, of which 3 were waited for; matrix products, arithmetic and copies ran while one was open for 2% of the time, Pallas kernels for 8%

profile of v5, /device:TPU:1, one launch (start us, length us, event | category | flops | bytes accessed | tf_op | source)
XLA Modules:
  0.0 127.1 jit_solution(2886670197541141210)
XLA Ops:
  0.6 2.5 %gather_rows.1 = bf16[64,16,256]{2,1,0:T(8,128)(2,1)} custom-call(bf16[8,128,256]{2,1,0:T(8,128)(2,1)} %bitcast.19), custom_call_target="tpu_custom_call" | custom-call | tf_op jit(solution)/shard_map/gather_rows/pallas_call | solution.py:374
  3.1 17.6 %all-to-all-start = ((bf16[64,16,256]{2,1,0:T(8,128)(2,1)}), bf16[64,16,256]{2,1,0:T(8,128)(2,1)S(1)}, u32[]{:S(2)}, u32[]{:S(2)}) async-start(bf16[64,16,256]{2,1,0:T(8,128)(2,1)} %gather_rows.1), calls=%async_computation | async-start | bytes 1048576 | tf_op jit(solution)/shard_map/all_to_all | solution.py:417
  20.8 0.0 copy-start
  20.8 0.0 copy-start.1
  20.8 0.0 copy-start.2
  20.8 0.0 copy-start.3
  20.8 0.0 copy-start.4
  20.8 0.0 copy-start.5
  20.8 0.0 copy-start.6
  20.9 1.2 copy.23
  22.1 10.6 %attention_front.1 = (f32[2,512,256]{2,1,0:T(8,128)}, f32[2,8,512]{2,1,0:T(8,128)S(1)}, bf16[2,256,512]{2,1,0:T(8,128)(2,1)S(1)}, bf16[2,512,256]{2,1,0:T(8,128)...) custom-call(bf16[2,512,256]{2,1,0:T(8,128)(2,1)S(1)} %bitcast.15, ...), custom_call_target="tpu_custom_call" | custom-call | flops 4294967296 | bytes 14680064 | tf_op jit(solution)/shard_map/attention_front/pallas_call | solution.py:267
  32.8 0.0 copy-start.7
  32.8 0.8 copy-done.7
  33.6 6.8 %all-to-all-done.up_ref = bf16[64,16,256]{2,1,0:T(8,128)(2,1)S(1)} async-done(((bf16[64,16,256]{2,1,0:T(8,128)(2,1)}), bf16[64,16,256]{2,1,0:T(8,128)(2,1)S(1)}, u32[]{:S(2)}, u32[]{:S(2)}) %all-to-all-start) | async-done | bytes 524320 | tf_op jit(solution)/shard_map/all_to_all | solution.py:417
  40.4 0.0 copy-done
  40.4 0.0 copy-done.3
  40.4 0.0 copy-done.4
  40.4 0.0 copy-done.5
  40.4 0.0 copy-done.6
  40.4 13.4 %attention_back.1 = (bf16[32,40,256]{2,1,0:T(8,128)(2,1)S(1)}, bf16[32,40,256]{2,1,0:T(8,128)(2,1)S(1)}) custom-call(bf16[64,16,256]{2,1,0:T(8,128)(2,1)S(1)} %all-to-all-done.up_ref, s32[1,2]{1,0:T(1,128)S(1)} %copy-done.6, s32[1]{0:T(128)} %bitcast.core_ref, f32[2,512,256]{2,1,0:T(8,128)} %get-tuple-element.24.xhat_ref, ...), custom_call_target="tpu_custom_call" | custom-call | flops 8589934592 | bytes 14680064 | tf_op jit(solution)/shard_map/attention_back/pallas_call | solution.py:292
  53.8 1.9 %collective-permute-start = (bf16[32,40,256]{2,1,0:T(8,128)(2,1)S(1)}, bf16[32,40,256]{2,1,0:T(8,128)(2,1)S(1)}, u32[]{:S(2)}, u32[]{:S(2)}) collective-permute-start(bf16[32,40,256]{2,1,0:T(8,128)(2,1)S(1)} %get-tuple-element.34), channel_id=1, source_target_pairs={{0,1},{1,0},{2,3},{3,2},{4,5},{5,4},{6,7},{7,6},{8,9},{9,8},{10,11... | collective-permute-start | bytes 1966088 | tf_op jit(solution)/shard_map/ppermute | solution.py:437
  55.7 2.1 %collective-permute-done.got_ref = bf16[32,40,256]{2,1,0:T(8,128)(2,1)S(1)} collective-permute-done((bf16[32,40,256]{2,1,0:T(8,128)(2,1)S(1)}, bf16[32,40,256]{2,1,0:T(8,128)(2,1)S(1)}, u32[]{:S(2)}, u32[]{:S(2)}) %collective-permute-start) | collective-permute-done | bytes 655392 | tf_op jit(solution)/shard_map/ppermute | solution.py:437
  57.8 0.2 combine.1
  57.9 30.6 %all_to_all.20.parts_ref = bf16[32,56,256]{2,1,0:T(8,128)(2,1)S(1)} all-to-all(bf16[32,56,256]{2,1,0:T(8,128)(2,1)S(1)} %combine.1), channel_id=1, replica_groups={{0,2,4,6,8,10,12,14,16,18,20,22,24,26,28,30,32,34,36,38,40,42,44,46,48,..., dimensions={0} | all-to-all | bytes 1835008 | tf_op jit(solution)/shard_map/all_to_all | solution.py:417
  88.5 0.1 merge.2
  88.6 9.9 %all_to_all.21.parts_ref = bf16[8,24,256]{2,1,0:T(8,128)(2,1)S(1)} all-to-all(bf16[8,24,256]{2,1,0:T(8,128)(2,1)S(1)} %merge.2), channel_id=1, replica_groups=mesh['dp'=8,'dap'=64] {'dp'}, dimensions={0} | all-to-all | bytes 196608 | tf_op jit(solution)/shard_map/all_to_all | solution.py:417
  98.5 19.5 %all_to_all.22.own_ref = bf16[32,24,256]{2,1,0:T(8,128)(2,1)S(1)} all-to-all(bf16[32,24,256]{2,1,0:T(8,128)(2,1)S(1)} %merge.3), channel_id=1, replica_groups={{0,2,4,6,8,10,12,14,16,18,20,22,24,26,28,30,32,34,36,38,40,42,44,46,48,..., dimensions={0} | all-to-all | bytes 786432 | tf_op jit(solution)/shard_map/all_to_all | solution.py:417
  118.0 6.6 %collective-permute-start.1 = (bf16[32,24,256]{2,1,0:T(8,128)(2,1)S(1)}, bf16[32,24,256]{2,1,0:T(8,128)(2,1)S(1)}, u32[]{:S(2)}, u32[]{:S(2)}) collective-permute-start(bf16[32,24,256]{2,1,0:T(8,128)(2,1)S(1)} %all_to_all.22.own_ref), channel_id=1, source_target_pairs={{0,1},{1,0},{2,3},{3,2},{4,5},{5,4},{6,7},{7,6},{8,9},{9,8},{10,11... | collective-permute-start | bytes 1179656 | tf_op jit(solution)/shard_map/ppermute | solution.py:441
  124.6 0.1 slice.4
  124.7 0.9 copy.21
  125.6 0.4 collective-permute-done.1.other_ref
  125.9 1.1 unpack.1
  (3 shorter events, 0.0 us)
Async XLA Ops:
  3.1 37.2 %all-to-all-start = ((bf16[64,16,256]{2,1,0:T(8,128)(2,1)}), bf16[64,16,256]{2,1,0:T(8,128)(2,1)S(1)}, u32[]{:S(2)}, u32[]{:S(2)}) async-start(bf16[64,16,256]{2,1,0:T(8,128)(2,1)} %gather_rows.1), calls=%async_computation | async-start | bytes 1048576 | tf_op jit(solution)/shard_map/all_to_all | solution.py:417
  20.8 19.6 %copy-start = (bf16[256,256]{1,0:T(8,128)(2,1)S(1)}, bf16[256,256]{1,0:T(8,128)(2,1)}, u32[]{:S(2)}) copy-start(bf16[256,256]{1,0:T(8,128)(2,1)} %wq_ref.1) | copy-start | bytes 393220
  20.8 19.6 %copy-start.1 = (bf16[256,256]{1,0:T(8,128)(2,1)S(1)}, bf16[256,256]{1,0:T(8,128)(2,1)}, u32[]{:S(2)}) copy-start(bf16[256,256]{1,0:T(8,128)(2,1)} %wk_ref.1) | copy-start | bytes 393220
  20.8 19.6 %copy-start.2 = (bf16[256,256]{1,0:T(8,128)(2,1)S(1)}, bf16[256,256]{1,0:T(8,128)(2,1)}, u32[]{:S(2)}) copy-start(bf16[256,256]{1,0:T(8,128)(2,1)} %wv_ref.1) | copy-start | bytes 393220
  20.8 19.6 %copy-start.3 = (bf16[256,256]{1,0:T(8,128)(2,1)S(1)}, bf16[256,256]{1,0:T(8,128)(2,1)}, u32[]{:S(2)}) copy-start(bf16[256,256]{1,0:T(8,128)(2,1)} %wg_ref.1) | copy-start | bytes 393220
  20.8 19.6 %copy-start.4 = (bf16[256,256]{1,0:T(8,128)(2,1)S(1)}, bf16[256,256]{1,0:T(8,128)(2,1)}, u32[]{:S(2)}) copy-start(bf16[256,256]{1,0:T(8,128)(2,1)} %wo_ref.1) | copy-start | bytes 393220
  20.8 19.6 %copy-start.5 = (f32[256]{0:T(256)S(1)}, f32[256]{0:T(256)}, u32[]{:S(2)}) copy-start(f32[256]{0:T(256)} %param.22) | copy-start | bytes 3076
  20.8 19.6 %copy-start.6 = (s32[1,2]{1,0:T(1,128)S(1)}, s32[1,2]{1,0:T(1,128)}, u32[]{:S(2)}) copy-start(s32[1,2]{1,0:T(1,128)} %amino_ref.1) | copy-start | bytes 28
  32.8 0.8 copy-start.7
  53.8 4.0 %collective-permute-start = (bf16[32,40,256]{2,1,0:T(8,128)(2,1)S(1)}, bf16[32,40,256]{2,1,0:T(8,128)(2,1)S(1)}, u32[]{:S(2)}, u32[]{:S(2)}) collective-permute-start(bf16[32,40,256]{2,1,0:T(8,128)(2,1)S(1)} %get-tuple-element.34), channel_id=1, source_target_pairs={{0,1},{1,0},{2,3},{3,2},{4,5},{5,4},{6,7},{7,6},{8,9},{9,8},{10,11... | collective-permute-start | bytes 1966088 | tf_op jit(solution)/shard_map/ppermute | solution.py:437
  118.0 8.0 %collective-permute-start.1 = (bf16[32,24,256]{2,1,0:T(8,128)(2,1)S(1)}, bf16[32,24,256]{2,1,0:T(8,128)(2,1)S(1)}, u32[]{:S(2)}, u32[]{:S(2)}) collective-permute-start(bf16[32,24,256]{2,1,0:T(8,128)(2,1)S(1)} %all_to_all.22.own_ref), channel_id=1, source_target_pairs={{0,1},{1,0},{2,3},{3,2},{4,5},{5,4},{6,7},{7,6},{8,9},{9,8},{10,11... | collective-permute-start | bytes 1179656 | tf_op jit(solution)/shard_map/ppermute | solution.py:441

commit v6 on v5

--- a/solution.py
+++ b/solution.py
@@ -206,11 +206,12 @@
         chips = depth // 8
         rows = jnp.concatenate([out_s[i] for i in range(members)], 1)
         rows = rows.reshape(chips, 2, MSA, depth)
+        vecs = jnp.concatenate([vec_s[:4, :LANES], vec_s[:4, LANES:]], 0)
         pieces = []
         for half in range(2):
             lanes = slice(half * LANES, (half + 1) * LANES)
             parts = [grad_s[i][:, lanes].reshape(chips, 8, LANES) for i in range(5)]
-            parts.append(jnp.broadcast_to(vec_s[:, lanes][None], (chips, 8, LANES)))
+            parts.append(jnp.broadcast_to(vecs[None], (chips, 8, LANES)))
             left, right = jnp.concatenate(parts[:3], 1), jnp.concatenate(parts[3:], 1)
             pieces.append(jnp.concatenate([left, right], 2))
         zero = jnp.concatenate([rows[:, 0], pieces[0]], 1)
@@ -359,58 +360,46 @@
     )(parts)
 
 
-def gather_kernel(up_ref, out_ref, rows_s):
-    near, residues, depth = up_ref.shape
-    for half in range(depth // LANES):
-        lanes = slice(half * LANES, (half + 1) * LANES)
-        rows_s[...] = up_ref[:, :, lanes].astype(F32).reshape(near * residues, LANES)
-        for n in range(0, residues, 2):
-            pair = [rows_s[pl.ds(n + r, near, stride=residues), :] for r in range(2)]
-            out_ref[n // 2, :, lanes] = jnp.concatenate(pair, 0).astype(BF16)
-
-
-def gather_rows(up):
-    near, residues, depth = up.shape
-    return pl.pallas_call(
-        gather_kernel,
-        out_shape=shape((residues // 2, 2 * near, depth), BF16),
+def spread_kernel(parts_ref, mats_ref, vecs_ref):
+    total = jnp.sum(parts_ref[...].astype(F32), 0)
+    mats = jnp.concatenate([total[:, :LANES], total[:16, LANES:]], 0)
+    mats_ref[...] = jnp.broadcast_to(mats[None], mats_ref.shape).astype(BF16)
+    vecs_ref[...] = total[16:, LANES:]
+
+
+def spread(parts, copies):
+    return pl.pallas_call(
+        spread_kernel,
+        out_shape=(shape((copies, 40, LANES), BF16), shape((8, LANES), F32)),
         in_specs=specs(1),
-        out_specs=specs(1)[0],
-        scratch_shapes=[pltpu.VMEM((near * residues, LANES), F32)],
-        compiler_params=pltpu.CompilerParams(vmem_limit_bytes=VMEM_BYTES),
-        name="gather_rows",
-    )(up)
-
-
-def unpack_kernel(factor, core_ref, own_ref, other_ref, *out_refs):
+        out_specs=specs(2),
+        compiler_params=pltpu.CompilerParams(vmem_limit_bytes=24 << 20),
+        name="spread",
+    )(parts)
+
+
+def unpack_kernel(factor, core_ref, own_ref, other_ref, vecs_ref, *out_refs):
     low = core_ref[0] == 0
     own, other = own_ref[...].astype(F32), other_ref[...].astype(F32)
     depth = out_refs[0].shape[0]
     for half in range(2):
         lanes = slice(half * LANES, (half + 1) * LANES)
         first = low if half == 0 else jnp.logical_not(low)
-        g = jnp.where(first, own, other) * factor
-        for i in range(6):
-            side, at = i // 3, 8 * (i % 3)
-            block = g[:, at : at + 8, side * LANES : (side + 1) * LANES]
-            if i < 5:
-                out_refs[i][:, lanes] = block.reshape(depth, LANES)
-            else:
-                out_refs[i][:, lanes] = block[0, :4]
-
-
-def unpack(core, own, other, depth, factor):
-    vm = pl.BlockSpec(memory_space=pltpu.VMEM)
-    sm = pl.BlockSpec(memory_space=pltpu.SMEM)
+        mats = jnp.where(first, own, other) * factor
+        for i in range(5):
+            out_refs[i][:, lanes] = mats[:, 8 * i : 8 * i + 8].reshape(depth, LANES)
+        out_refs[5][:, lanes] = vecs_ref[4 * half : 4 * half + 4, :] * factor
+
+
+def unpack(core, own, other, vecs, depth, factor):
     return pl.pallas_call(
         functools.partial(unpack_kernel, factor),
-        out_shape=(jax.ShapeDtypeStruct((depth, depth), F32),) * 5
-        + (jax.ShapeDtypeStruct((4, depth), F32),),
-        in_specs=[sm, vm, vm],
-        out_specs=(vm,) * 6,
+        out_shape=(shape((depth, depth), F32),) * 5 + (shape((4, depth), F32),),
+        in_specs=[SMEM] + specs(3),
+        out_specs=specs(6),
         compiler_params=pltpu.CompilerParams(vmem_limit_bytes=32 << 20),
         name="unpack",
-    )(core, own, other)
+    )(core, own, other, vecs)
 
 
 def exchange(a, axis, groups=None):
@@ -428,7 +417,8 @@
     same_core = [[2 * i + c for i in range(chips)] for c in range(2)]
     core = (lax.axis_index("dap") % 2).astype(jnp.int32).reshape(1)
 
-    local_up = exchange(gather_rows(up[0]), "dap")
+    rows = jnp.transpose(up[0].reshape(near, n_dap, members, depth), (1, 2, 0, 3))
+    local_up = exchange(rows.reshape(n_dap, members * near, depth), "dap")
     swapped = jnp.transpose(x[0], (1, 0, 2))
     gain, off, bg = gain[None], off[None], bg[None]
     saved = front(swapped, hom, wq, wk, wv, wg, bg, gain, off)
@@ -437,10 +427,11 @@
     got = lax.ppermute(send, "dap", partner)
     parts = exchange(combine(core, keep, got), "dap", same_core)
     pieces = exchange(merge(parts, n_dp), "dp")
-    own = exchange(merge(pieces, chips), "dap", same_core)
+    mats, vecs = spread(pieces, chips)
+    own = exchange(mats, "dap", same_core)
     other = lax.ppermute(own, "dap", partner)
     factor = float((n_dp * lines * residues) ** (-0.5))
-    grads = unpack(core, own, other, depth, factor)
+    grads = unpack(core, own, other, vecs, depth, factor)
 
     msa = parts[:, : 2 * MSA].reshape(chips, 2, members, near, depth)
     adjoint = jnp.transpose(msa, (3, 0, 1, 2, 4)).reshape(1, near, residues, depth)

time: 127 us -> 126 us (level)
  Pallas kernels: 27.9 us -> 25.4 us
  local copies, waits for them, and re-layouts: 3.02 us -> 5.15 us
    pallas_call x2, Pallas kernels: 3.61 us -> 1.15 us  [the longest x1 1.12 us: unpack(): pl.pallas_call(functools.partial(unpack_kernel, factor), out_shape=(shape...]
    another operation x0 -> x1, local copies, waits for them, and re-layouts: none -> 2.13 us  [shards(): up[0].reshape(near, n_dap, members, depth)]
  transfers between devices with their start and end apart: 3 -> 3, of which waited for: 3 -> 3; matrix products, arithmetic and copies ran while one was open for 2% -> 2% of each run, Pallas kernels for 8% -> 9%
where the time goes in v6:
time: 126 us; the launch traced here: 125 us
  blocking collectives  59.2 us (47%)
  starting transfers between devices  25.7 us (20%)
  Pallas kernels  25.4 us (20%)
  waiting for transfers between devices  9.12 us (7%)
  local copies, waits for them, and re-layouts  5.15 us (4%)
    all_to_all x3, blocking collectives, exchange(): lax.all_to_all(a, axis, split_axis=0, concat_axis=0, tiled=True, axis_ind...  59.2 us
    all_to_all x1, starting transfers between devices, exchange(): lax.all_to_all(a, axis, split_axis=0, concat_axis=0, tiled=True, axis_ind...  17.6 us
    pallas_call x1, Pallas kernels, back(): pl.pallas_call(back_kernel, grid=(members, HEADS // GROUP), out_shape=(pa...  13.4 us
    pallas_call x1, Pallas kernels, front(): pl.pallas_call(front_kernel, grid=(members, HEADS // GROUP), out_shape=ou...  10.7 us
    all_to_all x1, waiting for transfers between devices, exchange(): lax.all_to_all(a, axis, split_axis=0, concat_axis=0, tiled=True, axis_ind...  6.78 us
    ppermute x1, starting transfers between devices, shards(): other = lax.ppermute(own, 'dap', partner)  6.16 us
  transfers between devices with their start and end apart: 3, of which 3 were waited for; matrix products, arithmetic and copies ran while one was open for 2% of the time, Pallas kernels for 9%

profile of v6, /device:TPU:1, one launch (start us, length us, event | category | flops | bytes accessed | tf_op | source)
XLA Modules:
  0.0 125.4 jit_solution(9748992643685651716)
XLA Ops:
  0.6 2.1 %copy.22 = bf16[1,8,128,256]{3,1,2,0:T(8,128)(2,1)} copy(bf16[1,8,128,256]{3,2,1,0:T(8,128)(2,1)} %param.13) | data formatting | bytes 1048576 | tf_op jit(solution)/shard_map/reshape;squeeze | solution.py:420
  2.8 17.6 %all-to-all-start = ((bf16[64,16,256]{2,1,0:T(8,128)(2,1)}), bf16[64,16,256]{2,1,0:T(8,128)(2,1)S(1)}, u32[]{:S(2)}, u32[]{:S(2)}) async-start(bf16[64,16,256]{2,1,0:T(8,128)(2,1)} %bitcast.3), calls=%async_computation | async-start | bytes 1048576 | tf_op jit(solution)/shard_map/all_to_all | solution.py:406
  20.4 0.0 copy-start
  20.4 0.0 copy-start.1
  20.4 0.0 copy-start.2
  20.4 0.0 copy-start.3
  20.4 0.0 copy-start.4
  20.5 0.0 copy-start.5
  20.5 0.0 copy-start.6
  20.5 1.2 copy.25
  21.7 10.7 %attention_front.1 = (f32[2,512,256]{2,1,0:T(8,128)}, f32[2,8,512]{2,1,0:T(8,128)S(1)}, bf16[2,256,512]{2,1,0:T(8,128)(2,1)S(1)}, bf16[2,512,256]{2,1,0:T(8,128)...) custom-call(bf16[2,512,256]{2,1,0:T(8,128)(2,1)S(1)} %bitcast.19, ...), custom_call_target="tpu_custom_call" | custom-call | flops 4294967296 | bytes 14680064 | tf_op jit(solution)/shard_map/attention_front/pallas_call | solution.py:268
  32.4 0.0 copy-start.7
  32.4 0.8 copy-done.7
  33.2 6.8 %all-to-all-done.up_ref = bf16[64,16,256]{2,1,0:T(8,128)(2,1)S(1)} async-done(((bf16[64,16,256]{2,1,0:T(8,128)(2,1)}), bf16[64,16,256]{2,1,0:T(8,128)(2,1)S(1)}, u32[]{:S(2)}, u32[]{:S(2)}) %all-to-all-start) | async-done | bytes 524320 | tf_op jit(solution)/shard_map/all_to_all | solution.py:406
  40.0 0.0 copy-done
  40.0 0.0 copy-done.3
  40.0 0.0 copy-done.4
  40.0 0.0 copy-done.5
  40.0 0.0 copy-done.6
  40.0 13.4 %attention_back.1 = (bf16[32,40,256]{2,1,0:T(8,128)(2,1)S(1)}, bf16[32,40,256]{2,1,0:T(8,128)(2,1)S(1)}) custom-call(bf16[64,16,256]{2,1,0:T(8,128)(2,1)S(1)} %all-to-all-done.up_ref, s32[1,2]{1,0:T(1,128)S(1)} %copy-done.6, s32[1]{0:T(128)} %bitcast.core_ref, f32[2,512,256]{2,1,0:T(8,128)} %get-tuple-element.26.xhat_ref, ...), custom_call_target="tpu_custom_call" | custom-call | flops 8589934592 | bytes 14680064 | tf_op jit(solution)/shard_map/attention_back/pallas_call | solution.py:293
  53.4 1.9 %collective-permute-start = (bf16[32,40,256]{2,1,0:T(8,128)(2,1)S(1)}, bf16[32,40,256]{2,1,0:T(8,128)(2,1)S(1)}, u32[]{:S(2)}, u32[]{:S(2)}) collective-permute-start(bf16[32,40,256]{2,1,0:T(8,128)(2,1)S(1)} %get-tuple-element.36), channel_id=1, source_target_pairs={{0,1},{1,0},{2,3},{3,2},{4,5},{5,4},{6,7},{7,6},{8,9},{9,8},{10,11... | collective-permute-start | bytes 1966088 | tf_op jit(solution)/shard_map/ppermute | solution.py:427
  55.3 2.1 %collective-permute-done.got_ref = bf16[32,40,256]{2,1,0:T(8,128)(2,1)S(1)} collective-permute-done((bf16[32,40,256]{2,1,0:T(8,128)(2,1)S(1)}, bf16[32,40,256]{2,1,0:T(8,128)(2,1)S(1)}, u32[]{:S(2)}, u32[]{:S(2)}) %collective-permute-start) | collective-permute-done | bytes 655392 | tf_op jit(solution)/shard_map/ppermute | solution.py:427
  57.4 0.2 combine.1
  57.6 30.6 %all_to_all.20.parts_ref = bf16[32,56,256]{2,1,0:T(8,128)(2,1)S(1)} all-to-all(bf16[32,56,256]{2,1,0:T(8,128)(2,1)S(1)} %combine.1), channel_id=1, replica_groups={{0,2,4,6,8,10,12,14,16,18,20,22,24,26,28,30,32,34,36,38,40,42,44,46,48,..., dimensions={0} | all-to-all | bytes 1835008 | tf_op jit(solution)/shard_map/all_to_all | solution.py:406
  88.1 0.1 merge.1
  88.2 9.9 %all_to_all.21.parts_ref = bf16[8,24,256]{2,1,0:T(8,128)(2,1)S(1)} all-to-all(bf16[8,24,256]{2,1,0:T(8,128)(2,1)S(1)} %merge.1), channel_id=1, replica_groups=mesh['dp'=8,'dap'=64] {'dp'}, dimensions={0} | all-to-all | bytes 196608 | tf_op jit(solution)/shard_map/all_to_all | solution.py:406
  98.1 18.8 %all_to_all.22.own_ref = bf16[32,40,128]{2,1,0:T(8,128)(2,1)S(1)} all-to-all(bf16[32,40,128]{2,1,0:T(8,128)(2,1)S(1)} %get-tuple-element.37), channel_id=1, replica_groups={{0,2,4,6,8,10,12,14,16,18,20,22,24,26,28,30,32,34,36,38,40,42,44,46,48,..., dimensions={0} | all-to-all | bytes 655360 | tf_op jit(solution)/shard_map/all_to_all | solution.py:406
  116.9 6.2 %collective-permute-start.1 = (bf16[32,40,128]{2,1,0:T(8,128)(2,1)S(1)}, bf16[32,40,128]{2,1,0:T(8,128)(2,1)S(1)}, u32[]{:S(2)}, u32[]{:S(2)}) collective-permute-start(bf16[32,40,128]{2,1,0:T(8,128)(2,1)S(1)} %all_to_all.22.own_ref), channel_id=1, source_target_pairs={{0,1},{1,0},{2,3},{3,2},{4,5},{5,4},{6,7},{7,6},{8,9},{9,8},{10,11... | collective-permute-start | bytes 983048 | tf_op jit(solution)/shard_map/ppermute | solution.py:432
  123.0 0.1 slice.4
  123.1 0.9 copy.23
  124.0 0.3 collective-permute-done.1.other_ref
  124.3 1.1 unpack.1
  (3 shorter events, 0.0 us)
Async XLA Ops:
  2.8 37.2 %all-to-all-start = ((bf16[64,16,256]{2,1,0:T(8,128)(2,1)}), bf16[64,16,256]{2,1,0:T(8,128)(2,1)S(1)}, u32[]{:S(2)}, u32[]{:S(2)}) async-start(bf16[64,16,256]{2,1,0:T(8,128)(2,1)} %bitcast.3), calls=%async_computation | async-start | bytes 1048576 | tf_op jit(solution)/shard_map/all_to_all | solution.py:406
  20.4 19.6 %copy-start = (bf16[256,256]{1,0:T(8,128)(2,1)S(1)}, bf16[256,256]{1,0:T(8,128)(2,1)}, u32[]{:S(2)}) copy-start(bf16[256,256]{1,0:T(8,128)(2,1)} %wq_ref.1) | copy-start | bytes 393220
  20.4 19.6 %copy-start.1 = (bf16[256,256]{1,0:T(8,128)(2,1)S(1)}, bf16[256,256]{1,0:T(8,128)(2,1)}, u32[]{:S(2)}) copy-start(bf16[256,256]{1,0:T(8,128)(2,1)} %wk_ref.1) | copy-start | bytes 393220
  20.4 19.6 %copy-start.2 = (bf16[256,256]{1,0:T(8,128)(2,1)S(1)}, bf16[256,256]{1,0:T(8,128)(2,1)}, u32[]{:S(2)}) copy-start(bf16[256,256]{1,0:T(8,128)(2,1)} %wv_ref.1) | copy-start | bytes 393220
  20.4 19.6 %copy-start.3 = (bf16[256,256]{1,0:T(8,128)(2,1)S(1)}, bf16[256,256]{1,0:T(8,128)(2,1)}, u32[]{:S(2)}) copy-start(bf16[256,256]{1,0:T(8,128)(2,1)} %wg_ref.1) | copy-start | bytes 393220
  20.4 19.6 %copy-start.4 = (bf16[256,256]{1,0:T(8,128)(2,1)S(1)}, bf16[256,256]{1,0:T(8,128)(2,1)}, u32[]{:S(2)}) copy-start(bf16[256,256]{1,0:T(8,128)(2,1)} %wo_ref.1) | copy-start | bytes 393220
  20.5 19.6 %copy-start.5 = (f32[256]{0:T(256)S(1)}, f32[256]{0:T(256)}, u32[]{:S(2)}) copy-start(f32[256]{0:T(256)} %param.22) | copy-start | bytes 3076
  20.5 19.6 %copy-start.6 = (s32[1,2]{1,0:T(1,128)S(1)}, s32[1,2]{1,0:T(1,128)}, u32[]{:S(2)}) copy-start(s32[1,2]{1,0:T(1,128)} %amino_ref.1) | copy-start | bytes 28
  32.4 0.8 copy-start.7
  53.4 4.0 %collective-permute-start = (bf16[32,40,256]{2,1,0:T(8,128)(2,1)S(1)}, bf16[32,40,256]{2,1,0:T(8,128)(2,1)S(1)}, u32[]{:S(2)}, u32[]{:S(2)}) collective-permute-start(bf16[32,40,256]{2,1,0:T(8,128)(2,1)S(1)} %get-tuple-element.36), channel_id=1, source_target_pairs={{0,1},{1,0},{2,3},{3,2},{4,5},{5,4},{6,7},{7,6},{8,9},{9,8},{10,11... | collective-permute-start | bytes 1966088 | tf_op jit(solution)/shard_map/ppermute | solution.py:427
  116.9 7.4 %collective-permute-start.1 = (bf16[32,40,128]{2,1,0:T(8,128)(2,1)S(1)}, bf16[32,40,128]{2,1,0:T(8,128)(2,1)S(1)}, u32[]{:S(2)}, u32[]{:S(2)}) collective-permute-start(bf16[32,40,128]{2,1,0:T(8,128)(2,1)S(1)} %all_to_all.22.own_ref), channel_id=1, source_target_pairs={{0,1},{1,0},{2,3},{3,2},{4,5},{5,4},{6,7},{7,6},{8,9},{9,8},{10,11... | collective-permute-start | bytes 983048 | tf_op jit(solution)/shard_map/ppermute | solution.py:432

commit v7 on v6

--- a/solution.py
+++ b/solution.py
@@ -10,8 +10,8 @@
 HEADS = 8
 HEAD_DIM = 32
 LANES = 128
-PIECE = 24
-MSA = 16
+PIECE = 384
+MSA = 256
 GROUP = 8
 VMEM_BYTES = 60 << 20
 FRONT_BYTES = 51 << 20
@@ -205,17 +205,17 @@
         low = core_ref[0] == 0
         chips = depth // 8
         rows = jnp.concatenate([out_s[i] for i in range(members)], 1)
-        rows = rows.reshape(chips, 2, MSA, depth)
+        rows = rows.reshape(chips, 2, 8 * members, depth)
         vecs = jnp.concatenate([vec_s[:4, :LANES], vec_s[:4, LANES:]], 0)
         pieces = []
         for half in range(2):
             lanes = slice(half * LANES, (half + 1) * LANES)
             parts = [grad_s[i][:, lanes].reshape(chips, 8, LANES) for i in range(5)]
             parts.append(jnp.broadcast_to(vecs[None], (chips, 8, LANES)))
-            left, right = jnp.concatenate(parts[:3], 1), jnp.concatenate(parts[3:], 1)
-            pieces.append(jnp.concatenate([left, right], 2))
-        zero = jnp.concatenate([rows[:, 0], pieces[0]], 1)
-        one = jnp.concatenate([rows[:, 1], pieces[1]], 1)
+            pairs = [jnp.concatenate(parts[i : i + 2], 1) for i in (0, 2, 4)]
+            pieces.append(jnp.concatenate(pairs, 2))
+        zero = jnp.concatenate([rows[:, 0], pieces[0]], 2)
+        one = jnp.concatenate([rows[:, 1], pieces[1]], 2)
         keep_ref[...] = jnp.where(low, zero, one).astype(BF16)
         send_ref[...] = jnp.where(low, one, zero).astype(BF16)
 
@@ -289,7 +289,7 @@
     members, lines, depth = xhat.shape
     tall, wide = (lines, depth), (depth, lines)
     pairs = members * HEADS
-    parcel = shape((depth // 8, MSA + PIECE, depth), BF16)
+    parcel = shape((depth // 8, 8 * members, MSA + PIECE), BF16)
     return pl.pallas_call(
         back_kernel,
         grid=(members, HEADS // GROUP),
@@ -325,17 +325,17 @@
 def combine_kernel(core_ref, keep_ref, got_ref, out_ref):
     low = core_ref[0] == 0
     keep, got = keep_ref[...].astype(F32), got_ref[...].astype(F32)
-    first = jnp.where(low, keep[:, :MSA], got[:, :MSA])
-    second = jnp.where(low, got[:, :MSA], keep[:, :MSA])
-    total = keep[:, MSA:] + got[:, MSA:]
-    out_ref[...] = jnp.concatenate([first, second, total], 1).astype(BF16)
+    first = jnp.where(low, keep[..., :MSA], got[..., :MSA])
+    second = jnp.where(low, got[..., :MSA], keep[..., :MSA])
+    total = keep[..., MSA:] + got[..., MSA:]
+    out_ref[...] = jnp.concatenate([first, second, total], 2).astype(BF16)
 
 
 def combine(core, keep, got):
-    chips, _, depth = keep.shape
+    chips, rows, _ = keep.shape
     return pl.pallas_call(
         combine_kernel,
-        out_shape=shape((chips, 2 * MSA + PIECE, depth), BF16),
+        out_shape=shape((chips, rows, 2 * MSA + PIECE), BF16),
         in_specs=[SMEM] + specs(2),
         out_specs=specs(1)[0],
         compiler_params=pltpu.CompilerParams(vmem_limit_bytes=24 << 20),
@@ -344,15 +344,14 @@
 
 
 def merge_kernel(parts_ref, out_ref):
-    start = parts_ref.shape[1] - PIECE
-    total = jnp.sum(parts_ref[...].astype(F32)[:, start:], 0, keepdims=True)
+    total = jnp.sum(parts_ref[:, :, 2 * MSA :].astype(F32), 0, keepdims=True)
     out_ref[...] = jnp.broadcast_to(total, out_ref.shape).astype(BF16)
 
 
 def merge(parts, copies):
     return pl.pallas_call(
         merge_kernel,
-        out_shape=shape((copies, PIECE, parts.shape[2]), BF16),
+        out_shape=shape((copies, parts.shape[1], PIECE), BF16),
         in_specs=specs(1),
         out_specs=specs(1)[0],
         compiler_params=pltpu.CompilerParams(vmem_limit_bytes=24 << 20),
@@ -362,9 +361,10 @@
 
 def spread_kernel(parts_ref, mats_ref, vecs_ref):
     total = jnp.sum(parts_ref[...].astype(F32), 0)
-    mats = jnp.concatenate([total[:, :LANES], total[:16, LANES:]], 0)
+    a, b, c = (total[:, i * LANES : (i + 1) * LANES] for i in range(3))
+    mats = jnp.concatenate([a, b, c[:8]], 0)
     mats_ref[...] = jnp.broadcast_to(mats[None], mats_ref.shape).astype(BF16)
-    vecs_ref[...] = total[16:, LANES:]
+    vecs_ref[...] = c[8:]
 
 
 def spread(parts, copies):
@@ -433,8 +433,8 @@
     factor = float((n_dp * lines * residues) ** (-0.5))
     grads = unpack(core, own, other, vecs, depth, factor)
 
-    msa = parts[:, : 2 * MSA].reshape(chips, 2, members, near, depth)
-    adjoint = jnp.transpose(msa, (3, 0, 1, 2, 4)).reshape(1, near, residues, depth)
+    msa = parts[:, :, : 2 * MSA].reshape(chips, members, near, 2, depth)
+    adjoint = jnp.transpose(msa, (2, 0, 3, 1, 4)).reshape(1, near, residues, depth)
     return (adjoint,) + tuple(grads)
 
 

time: 126 us -> 126 us (level)
  transfers between devices with their start and end apart: 3 -> 3, of which waited for: 3 -> 2; matrix products, arithmetic and copies ran while one was open for 2% -> 2% of each run, Pallas kernels for 9% -> 8%
where the time goes in v7:
time: 126 us
  blocking collectives  59.2 us (47%)
  starting transfers between devices  25.7 us (20%)
  Pallas kernels  25.5 us (20%)
  waiting for transfers between devices  8.85 us (7%)
  local copies, waits for them, and re-layouts  5.65 us (4%)
    all_to_all x3, blocking collectives, exchange(): lax.all_to_all(a, axis, split_axis=0, concat_axis=0, tiled=True, axis_ind...  59.2 us
    all_to_all x1, starting transfers between devices, exchange(): lax.all_to_all(a, axis, split_axis=0, concat_axis=0, tiled=True, axis_ind...  17.6 us
    pallas_call x1, Pallas kernels, back(): pl.pallas_call(back_kernel, grid=(members, HEADS // GROUP), out_shape=(pa...  13.4 us
    pallas_call x1, Pallas kernels, front(): pl.pallas_call(front_kernel, grid=(members, HEADS // GROUP), out_shape=ou...  10.7 us
    all_to_all x1, waiting for transfers between devices, exchange(): lax.all_to_all(a, axis, split_axis=0, concat_axis=0, tiled=True, axis_ind...  6.78 us
    ppermute x1, starting transfers between devices, shards(): other = lax.ppermute(own, 'dap', partner)  6.16 us
  transfers between devices with their start and end apart: 3, of which 2 were waited for; matrix products, arithmetic and copies ran while one was open for 2% of the time, Pallas kernels for 8%

profile of v7, /device:TPU:1, one launch (start us, length us, event | category | flops | bytes accessed | tf_op | source)
XLA Modules:
  0.0 125.7 jit_solution(15942981056568525506)
XLA Ops:
  0.6 2.1 %copy.22 = bf16[1,8,128,256]{3,1,2,0:T(8,128)(2,1)} copy(bf16[1,8,128,256]{3,2,1,0:T(8,128)(2,1)} %param.13) | data formatting | bytes 1048576 | tf_op jit(solution)/shard_map/reshape;squeeze | solution.py:420
  2.8 17.6 %all-to-all-start = ((bf16[64,16,256]{2,1,0:T(8,128)(2,1)}), bf16[64,16,256]{2,1,0:T(8,128)(2,1)S(1)}, u32[]{:S(2)}, u32[]{:S(2)}) async-start(bf16[64,16,256]{2,1,0:T(8,128)(2,1)} %bitcast.3), calls=%async_computation | async-start | bytes 1048576 | tf_op jit(solution)/shard_map/all_to_all | solution.py:406
  20.4 0.0 copy-start
  20.4 0.0 copy-start.1
  20.4 0.0 copy-start.2
  20.4 0.0 copy-start.3
  20.4 0.0 copy-start.4
  20.5 0.0 copy-start.5
  20.5 0.0 copy-start.6
  20.5 1.2 copy.24
  21.7 10.7 %attention_front.1 = (f32[2,512,256]{2,1,0:T(8,128)}, f32[2,8,512]{2,1,0:T(8,128)S(1)}, bf16[2,256,512]{2,1,0:T(8,128)(2,1)S(1)}, bf16[2,512,256]{2,1,0:T(8,128)...) custom-call(bf16[2,512,256]{2,1,0:T(8,128)(2,1)S(1)} %bitcast.17, ...), custom_call_target="tpu_custom_call" | custom-call | flops 4294967296 | bytes 14680064 | tf_op jit(solution)/shard_map/attention_front/pallas_call | solution.py:268
  32.4 0.8 copy-done.7
  33.2 6.8 %all-to-all-done.up_ref = bf16[64,16,256]{2,1,0:T(8,128)(2,1)S(1)} async-done(((bf16[64,16,256]{2,1,0:T(8,128)(2,1)}), bf16[64,16,256]{2,1,0:T(8,128)(2,1)S(1)}, u32[]{:S(2)}, u32[]{:S(2)}) %all-to-all-start) | async-done | bytes 524320 | tf_op jit(solution)/shard_map/all_to_all | solution.py:406
  40.0 0.0 copy-done.2
  40.0 0.0 copy-done.3
  40.0 0.0 copy-done.4
  40.0 0.0 copy-done.5
  40.0 0.0 copy-done.6
  40.0 13.4 %attention_back.1 = (bf16[32,16,640]{2,1,0:T(8,128)(2,1)S(1)}, bf16[32,16,640]{2,1,0:T(8,128)(2,1)S(1)}) custom-call(bf16[64,16,256]{2,1,0:T(8,128)(2,1)S(1)} %all-to-all-done.up_ref, s32[1,2]{1,0:T(1,128)S(1)} %copy-done.6, s32[1]{0:T(128)} %bitcast.core_ref, f32[2,512,256]{2,1,0:T(8,128)} %get-tuple-element.26.xhat_ref, ...), custom_call_target="tpu_custom_call" | custom-call | flops 8589934592 | bytes 14680064 | tf_op jit(solution)/shard_map/attention_back/pallas_call | solution.py:293
  53.4 1.9 %collective-permute-start = (bf16[32,16,640]{2,1,0:T(8,128)(2,1)S(1)}, bf16[32,16,640]{2,1,0:T(8,128)(2,1)S(1)}, u32[]{:S(2)}, u32[]{:S(2)}) collective-permute-start(bf16[32,16,640]{2,1,0:T(8,128)(2,1)S(1)} %get-tuple-element.36), channel_id=1, source_target_pairs={{0,1},{1,0},{2,3},{3,2},{4,5},{5,4},{6,7},{7,6},{8,9},{9,8},{10,11... | collective-permute-start | bytes 1966088 | tf_op jit(solution)/shard_map/ppermute | solution.py:427
  55.3 2.1 %collective-permute-done.got_ref = bf16[32,16,640]{2,1,0:T(8,128)(2,1)S(1)} collective-permute-done((bf16[32,16,640]{2,1,0:T(8,128)(2,1)S(1)}, bf16[32,16,640]{2,1,0:T(8,128)(2,1)S(1)}, u32[]{:S(2)}, u32[]{:S(2)}) %collective-permute-start) | collective-permute-done | bytes 655392 | tf_op jit(solution)/shard_map/ppermute | solution.py:427
  57.4 0.2 combine.1
  57.6 30.6 %all_to_all.20.parts_ref = bf16[32,16,896]{2,1,0:T(8,128)(2,1)S(1)} all-to-all(bf16[32,16,896]{2,1,0:T(8,128)(2,1)S(1)} %combine.1), channel_id=1, replica_groups={{0,2,4,6,8,10,12,14,16,18,20,22,24,26,28,30,32,34,36,38,40,42,44,46,48,..., dimensions={0} | all-to-all | bytes 1835008 | tf_op jit(solution)/shard_map/all_to_all | solution.py:406
  88.2 0.1 merge.1
  88.2 9.9 %all_to_all.21.parts_ref = bf16[8,16,384]{2,1,0:T(8,128)(2,1)S(1)} all-to-all(bf16[8,16,384]{2,1,0:T(8,128)(2,1)S(1)} %merge.1), channel_id=1, replica_groups=mesh['dp'=8,'dap'=64] {'dp'}, dimensions={0} | all-to-all | bytes 196608 | tf_op jit(solution)/shard_map/all_to_all | solution.py:406
  98.1 18.8 %all_to_all.22.own_ref = bf16[32,40,128]{2,1,0:T(8,128)(2,1)S(1)} all-to-all(bf16[32,40,128]{2,1,0:T(8,128)(2,1)S(1)} %get-tuple-element.37), channel_id=1, replica_groups={{0,2,4,6,8,10,12,14,16,18,20,22,24,26,28,30,32,34,36,38,40,42,44,46,48,..., dimensions={0} | all-to-all | bytes 655360 | tf_op jit(solution)/shard_map/all_to_all | solution.py:406
  116.9 6.2 %collective-permute-start.1 = (bf16[32,40,128]{2,1,0:T(8,128)(2,1)S(1)}, bf16[32,40,128]{2,1,0:T(8,128)(2,1)S(1)}, u32[]{:S(2)}, u32[]{:S(2)}) collective-permute-start(bf16[32,40,128]{2,1,0:T(8,128)(2,1)S(1)} %all_to_all.22.own_ref), channel_id=1, source_target_pairs={{0,1},{1,0},{2,3},{3,2},{4,5},{5,4},{6,7},{7,6},{8,9},{9,8},{10,11... | collective-permute-start | bytes 983048 | tf_op jit(solution)/shard_map/ppermute | solution.py:432
  123.1 0.1 slice.4
  123.1 0.4 copy.21
  123.6 1.0 reshape.29
  124.5 0.0 collective-permute-done.1.other_ref
  124.5 1.1 unpack.1
  (4 shorter events, 0.0 us)
Async XLA Ops:
  2.8 37.2 %all-to-all-start = ((bf16[64,16,256]{2,1,0:T(8,128)(2,1)}), bf16[64,16,256]{2,1,0:T(8,128)(2,1)S(1)}, u32[]{:S(2)}, u32[]{:S(2)}) async-start(bf16[64,16,256]{2,1,0:T(8,128)(2,1)} %bitcast.3), calls=%async_computation | async-start | bytes 1048576 | tf_op jit(solution)/shard_map/all_to_all | solution.py:406
  20.4 19.6 %copy-start = (bf16[256,256]{1,0:T(8,128)(2,1)S(1)}, bf16[256,256]{1,0:T(8,128)(2,1)}, u32[]{:S(2)}) copy-start(bf16[256,256]{1,0:T(8,128)(2,1)} %wq_ref.1) | copy-start | bytes 393220
  20.4 19.6 %copy-start.1 = (bf16[256,256]{1,0:T(8,128)(2,1)S(1)}, bf16[256,256]{1,0:T(8,128)(2,1)}, u32[]{:S(2)}) copy-start(bf16[256,256]{1,0:T(8,128)(2,1)} %wk_ref.1) | copy-start | bytes 393220
  20.4 19.6 %copy-start.2 = (bf16[256,256]{1,0:T(8,128)(2,1)S(1)}, bf16[256,256]{1,0:T(8,128)(2,1)}, u32[]{:S(2)}) copy-start(bf16[256,256]{1,0:T(8,128)(2,1)} %wv_ref.1) | copy-start | bytes 393220
  20.4 19.6 %copy-start.3 = (bf16[256,256]{1,0:T(8,128)(2,1)S(1)}, bf16[256,256]{1,0:T(8,128)(2,1)}, u32[]{:S(2)}) copy-start(bf16[256,256]{1,0:T(8,128)(2,1)} %wg_ref.1) | copy-start | bytes 393220
  20.4 19.6 %copy-start.4 = (bf16[256,256]{1,0:T(8,128)(2,1)S(1)}, bf16[256,256]{1,0:T(8,128)(2,1)}, u32[]{:S(2)}) copy-start(bf16[256,256]{1,0:T(8,128)(2,1)} %wo_ref.1) | copy-start | bytes 393220
  20.5 19.6 %copy-start.5 = (f32[256]{0:T(256)S(1)}, f32[256]{0:T(256)}, u32[]{:S(2)}) copy-start(f32[256]{0:T(256)} %param.22) | copy-start | bytes 3076
  20.5 19.6 %copy-start.6 = (s32[1,2]{1,0:T(1,128)S(1)}, s32[1,2]{1,0:T(1,128)}, u32[]{:S(2)}) copy-start(s32[1,2]{1,0:T(1,128)} %amino_ref.1) | copy-start | bytes 28
  32.4 0.8 copy-start.7
  53.4 4.0 %collective-permute-start = (bf16[32,16,640]{2,1,0:T(8,128)(2,1)S(1)}, bf16[32,16,640]{2,1,0:T(8,128)(2,1)S(1)}, u32[]{:S(2)}, u32[]{:S(2)}) collective-permute-start(bf16[32,16,640]{2,1,0:T(8,128)(2,1)S(1)} %get-tuple-element.36), channel_id=1, source_target_pairs={{0,1},{1,0},{2,3},{3,2},{4,5},{5,4},{6,7},{7,6},{8,9},{9,8},{10,11... | collective-permute-start | bytes 1966088 | tf_op jit(solution)/shard_map/ppermute | solution.py:427
  116.9 7.6 %collective-permute-start.1 = (bf16[32,40,128]{2,1,0:T(8,128)(2,1)S(1)}, bf16[32,40,128]{2,1,0:T(8,128)(2,1)S(1)}, u32[]{:S(2)}, u32[]{:S(2)}) collective-permute-start(bf16[32,40,128]{2,1,0:T(8,128)(2,1)S(1)} %all_to_all.22.own_ref), channel_id=1, source_target_pairs={{0,1},{1,0},{2,3},{3,2},{4,5},{5,4},{6,7},{7,6},{8,9},{9,8},{10,11... | collective-permute-start | bytes 983048 | tf_op jit(solution)/shard_map/ppermute | solution.py:432

commit v8 on v6

--- a/solution.py
+++ b/solution.py
@@ -360,22 +360,22 @@
     )(parts)
 
 
-def spread_kernel(parts_ref, mats_ref, vecs_ref):
+def spread_kernel(parts_ref, after_ref, mats_ref, vecs_ref):
     total = jnp.sum(parts_ref[...].astype(F32), 0)
     mats = jnp.concatenate([total[:, :LANES], total[:16, LANES:]], 0)
     mats_ref[...] = jnp.broadcast_to(mats[None], mats_ref.shape).astype(BF16)
     vecs_ref[...] = total[16:, LANES:]
 
 
-def spread(parts, copies):
+def spread(parts, after, copies):
     return pl.pallas_call(
         spread_kernel,
         out_shape=(shape((copies, 40, LANES), BF16), shape((8, LANES), F32)),
-        in_specs=specs(1),
+        in_specs=specs(1) + [pl.BlockSpec(memory_space=pl.ANY)],
         out_specs=specs(2),
         compiler_params=pltpu.CompilerParams(vmem_limit_bytes=24 << 20),
         name="spread",
-    )(parts)
+    )(parts, after)
 
 
 def unpack_kernel(factor, core_ref, own_ref, other_ref, vecs_ref, *out_refs):
@@ -427,14 +427,14 @@
     got = lax.ppermute(send, "dap", partner)
     parts = exchange(combine(core, keep, got), "dap", same_core)
     pieces = exchange(merge(parts, n_dp), "dp")
-    mats, vecs = spread(pieces, chips)
+    msa = parts[:, : 2 * MSA].reshape(chips, 2, members, near, depth)
+    adjoint = jnp.transpose(msa, (3, 0, 1, 2, 4)).reshape(1, near, residues, depth)
+    mats, vecs = spread(pieces, adjoint, chips)
     own = exchange(mats, "dap", same_core)
     other = lax.ppermute(own, "dap", partner)
     factor = float((n_dp * lines * residues) ** (-0.5))
     grads = unpack(core, own, other, vecs, depth, factor)
 
-    msa = parts[:, : 2 * MSA].reshape(chips, 2, members, near, depth)
-    adjoint = jnp.transpose(msa, (3, 0, 1, 2, 4)).reshape(1, near, residues, depth)
     return (adjoint,) + tuple(grads)
 
 

time: 126 us -> 127 us (level)
  blocking collectives: 59.2 us -> 49.3 us
  waiting for transfers between devices: 9.12 us -> 14.8 us
  starting transfers between devices: 25.7 us -> 30.4 us
    all_to_all x3 -> x2, blocking collectives: 59.2 us -> 49.3 us  [exchange(): lax.all_to_all(a, axis, split_axis=0, concat_axis=0, tiled=True, axis_ind...]
    all_to_all x1 -> x2, waiting for transfers between devices: 6.78 us -> 11.5 us  [exchange(): lax.all_to_all(a, axis, split_axis=0, concat_axis=0, tiled=True, axis_ind...]
    all_to_all x1 -> x2, starting transfers between devices: 17.6 us -> 22.3 us  [exchange(): lax.all_to_all(a, axis, split_axis=0, concat_axis=0, tiled=True, axis_ind...]
  transfers between devices with their start and end apart: 3 -> 4, of which waited for: 3 -> 4; matrix products, arithmetic and copies ran while one was open for 2% -> 1% of each run, Pallas kernels for 9% -> 8%
where the time goes in v8:
time: 127 us; the launch traced here: 126 us
  blocking collectives  49.3 us (39%)
  starting transfers between devices  30.4 us (24%)
  Pallas kernels  26.1 us (21%)
  waiting for transfers between devices  14.8 us (12%)
  local copies, waits for them, and re-layouts  4.86 us (4%)
    all_to_all x2, blocking collectives, exchange(): lax.all_to_all(a, axis, split_axis=0, concat_axis=0, tiled=True, axis_ind...  49.3 us
    all_to_all x2, starting transfers between devices, exchange(): lax.all_to_all(a, axis, split_axis=0, concat_axis=0, tiled=True, axis_ind...  22.3 us
    pallas_call x1, Pallas kernels, back(): pl.pallas_call(back_kernel, grid=(members, HEADS // GROUP), out_shape=(pa...  13.4 us
    all_to_all x2, waiting for transfers between devices, exchange(): lax.all_to_all(a, axis, split_axis=0, concat_axis=0, tiled=True, axis_ind...  11.5 us
    pallas_call x1, Pallas kernels, front(): pl.pallas_call(front_kernel, grid=(members, HEADS // GROUP), out_shape=ou...  10.7 us
    ppermute x1, starting transfers between devices, shards(): other = lax.ppermute(own, 'dap', partner)  6.2 us
  transfers between devices with their start and end apart: 4, of which 4 were waited for; matrix products, arithmetic and copies ran while one was open for 1% of the time, Pallas kernels for 8%

profile of v8, /device:TPU:1, one launch (start us, length us, event | category | flops | bytes accessed | tf_op | source)
XLA Modules:
  0.0 126.3 jit_solution(11433190896659366961)
XLA Ops:
  0.6 2.1 %copy.22 = bf16[1,8,128,256]{3,1,2,0:T(8,128)(2,1)} copy(bf16[1,8,128,256]{3,2,1,0:T(8,128)(2,1)} %param.13) | data formatting | bytes 1048576 | tf_op jit(solution)/shard_map/reshape;squeeze | solution.py:420
  2.8 17.6 %all-to-all-start = ((bf16[64,16,256]{2,1,0:T(8,128)(2,1)}), bf16[64,16,256]{2,1,0:T(8,128)(2,1)S(1)}, u32[]{:S(2)}, u32[]{:S(2)}) async-start(bf16[64,16,256]{2,1,0:T(8,128)(2,1)} %bitcast.3), calls=%async_computation | async-start | bytes 1048576 | tf_op jit(solution)/shard_map/all_to_all | solution.py:406
  20.4 0.0 copy-start.1
  20.4 0.0 copy-start.2
  20.4 0.0 copy-start.3
  20.4 0.0 copy-start.4
  20.4 0.0 copy-start.5
  20.5 0.0 copy-start.6
  20.5 0.0 copy-start.7
  20.5 1.2 copy.26
  21.7 10.7 %attention_front.1 = (f32[2,512,256]{2,1,0:T(8,128)}, f32[2,8,512]{2,1,0:T(8,128)S(1)}, bf16[2,256,512]{2,1,0:T(8,128)(2,1)S(1)}, bf16[2,512,256]{2,1,0:T(8,128)...) custom-call(bf16[2,512,256]{2,1,0:T(8,128)(2,1)S(1)} %bitcast.18, ...), custom_call_target="tpu_custom_call" | custom-call | flops 4294967296 | bytes 14680064 | tf_op jit(solution)/shard_map/attention_front/pallas_call | solution.py:268
  32.4 0.0 copy-start.8
  32.4 0.8 copy-done.8
  33.2 6.8 %all-to-all-done.up_ref = bf16[64,16,256]{2,1,0:T(8,128)(2,1)S(1)} async-done(((bf16[64,16,256]{2,1,0:T(8,128)(2,1)}), bf16[64,16,256]{2,1,0:T(8,128)(2,1)S(1)}, u32[]{:S(2)}, u32[]{:S(2)}) %all-to-all-start) | async-done | bytes 524320 | tf_op jit(solution)/shard_map/all_to_all | solution.py:406
  40.0 0.0 copy-done.1
  40.0 0.0 copy-done.2
  40.0 13.4 %attention_back.1 = (bf16[32,40,256]{2,1,0:T(8,128)(2,1)S(1)}, bf16[32,40,256]{2,1,0:T(8,128)(2,1)S(1)}) custom-call(bf16[64,16,256]{2,1,0:T(8,128)(2,1)S(1)} %all-to-all-done.up_ref, s32[1,2]{1,0:T(1,128)S(1)} %copy-done.7, s32[1]{0:T(128)} %bitcast.core_ref, f32[2,512,256]{2,1,0:T(8,128)} %get-tuple-element.26.xhat_ref, ...), custom_call_target="tpu_custom_call" | custom-call | flops 8589934592 | bytes 14680064 | tf_op jit(solution)/shard_map/attention_back/pallas_call | solution.py:293
  53.4 1.9 %collective-permute-start = (bf16[32,40,256]{2,1,0:T(8,128)(2,1)S(1)}, bf16[32,40,256]{2,1,0:T(8,128)(2,1)S(1)}, u32[]{:S(2)}, u32[]{:S(2)}) collective-permute-start(bf16[32,40,256]{2,1,0:T(8,128)(2,1)S(1)} %get-tuple-element.36), channel_id=1, source_target_pairs={{0,1},{1,0},{2,3},{3,2},{4,5},{5,4},{6,7},{7,6},{8,9},{9,8},{10,11... | collective-permute-start | bytes 1966088 | tf_op jit(solution)/shard_map/ppermute | solution.py:427
  55.3 2.1 %collective-permute-done.got_ref = bf16[32,40,256]{2,1,0:T(8,128)(2,1)S(1)} collective-permute-done((bf16[32,40,256]{2,1,0:T(8,128)(2,1)S(1)}, bf16[32,40,256]{2,1,0:T(8,128)(2,1)S(1)}, u32[]{:S(2)}, u32[]{:S(2)}) %collective-permute-start) | collective-permute-done | bytes 655392 | tf_op jit(solution)/shard_map/ppermute | solution.py:427
  57.4 0.2 combine.1
  57.6 30.6 %all_to_all.20.parts_ref = bf16[32,56,256]{2,1,0:T(8,128)(2,1)S(1)} all-to-all(bf16[32,56,256]{2,1,0:T(8,128)(2,1)S(1)} %combine.1), channel_id=1, replica_groups={{0,2,4,6,8,10,12,14,16,18,20,22,24,26,28,30,32,34,36,38,40,42,44,46,48,..., dimensions={0} | all-to-all | bytes 1835008 | tf_op jit(solution)/shard_map/all_to_all | solution.py:406
  88.2 0.7 merge.1
  88.9 4.7 %all-to-all-start.2 = ((bf16[8,24,256]{2,1,0:T(8,128)(2,1)}), bf16[8,24,256]{2,1,0:T(8,128)(2,1)S(1)}, u32[]{:S(2)}, u32[]{:S(2)}) async-start(bf16[8,24,256]{2,1,0:T(8,128)(2,1)} %merge.1), calls=%async_computation.2 | async-start | bytes 196608 | tf_op jit(solution)/shard_map/all_to_all | solution.py:406
  93.5 0.1 slice.4
  93.6 0.4 copy.25
  94.0 0.2 reshape.29.after_ref
  94.2 0.0 copy-start
  94.2 4.7 %all-to-all-done.2.parts_ref = bf16[8,24,256]{2,1,0:T(8,128)(2,1)S(1)} async-done(((bf16[8,24,256]{2,1,0:T(8,128)(2,1)}), bf16[8,24,256]{2,1,0:T(8,128)(2,1)S(1)}, u32[]{:S(2)}, u32[]{:S(2)}) %all-to-all-start.2) | async-done | bytes 98336 | tf_op jit(solution)/shard_map/all_to_all | solution.py:406
  98.9 18.8 %all_to_all.21.own_ref = bf16[32,40,128]{2,1,0:T(8,128)(2,1)S(1)} all-to-all(bf16[32,40,128]{2,1,0:T(8,128)(2,1)S(1)} %get-tuple-element.37), channel_id=1, replica_groups={{0,2,4,6,8,10,12,14,16,18,20,22,24,26,28,30,32,34,36,38,40,42,44,46,48,..., dimensions={0} | all-to-all | bytes 655360 | tf_op jit(solution)/shard_map/all_to_all | solution.py:406
  117.7 6.2 %collective-permute-start.1 = (bf16[32,40,128]{2,1,0:T(8,128)(2,1)S(1)}, bf16[32,40,128]{2,1,0:T(8,128)(2,1)S(1)}, u32[]{:S(2)}, u32[]{:S(2)}) collective-permute-start(bf16[32,40,128]{2,1,0:T(8,128)(2,1)S(1)} %all_to_all.21.own_ref), channel_id=1, source_target_pairs={{0,1},{1,0},{2,3},{3,2},{4,5},{5,4},{6,7},{7,6},{8,9},{9,8},{10,11... | collective-permute-start | bytes 983048 | tf_op jit(solution)/shard_map/ppermute | solution.py:434
  123.9 1.2 collective-permute-done.1.other_ref
  125.1 1.1 unpack.1
  (7 shorter events, 0.0 us)
Async XLA Ops:
  2.8 37.2 %all-to-all-start = ((bf16[64,16,256]{2,1,0:T(8,128)(2,1)}), bf16[64,16,256]{2,1,0:T(8,128)(2,1)S(1)}, u32[]{:S(2)}, u32[]{:S(2)}) async-start(bf16[64,16,256]{2,1,0:T(8,128)(2,1)} %bitcast.3), calls=%async_computation | async-start | bytes 1048576 | tf_op jit(solution)/shard_map/all_to_all | solution.py:406
  20.4 19.6 %copy-start.1 = (bf16[256,256]{1,0:T(8,128)(2,1)S(1)}, bf16[256,256]{1,0:T(8,128)(2,1)}, u32[]{:S(2)}) copy-start(bf16[256,256]{1,0:T(8,128)(2,1)} %wq_ref.1) | copy-start | bytes 393220
  20.4 19.6 %copy-start.2 = (bf16[256,256]{1,0:T(8,128)(2,1)S(1)}, bf16[256,256]{1,0:T(8,128)(2,1)}, u32[]{:S(2)}) copy-start(bf16[256,256]{1,0:T(8,128)(2,1)} %wk_ref.1) | copy-start | bytes 393220
  20.4 19.6 %copy-start.3 = (bf16[256,256]{1,0:T(8,128)(2,1)S(1)}, bf16[256,256]{1,0:T(8,128)(2,1)}, u32[]{:S(2)}) copy-start(bf16[256,256]{1,0:T(8,128)(2,1)} %wv_ref.1) | copy-start | bytes 393220
  20.4 19.6 %copy-start.4 = (bf16[256,256]{1,0:T(8,128)(2,1)S(1)}, bf16[256,256]{1,0:T(8,128)(2,1)}, u32[]{:S(2)}) copy-start(bf16[256,256]{1,0:T(8,128)(2,1)} %wg_ref.1) | copy-start | bytes 393220
  20.4 19.6 %copy-start.5 = (bf16[256,256]{1,0:T(8,128)(2,1)S(1)}, bf16[256,256]{1,0:T(8,128)(2,1)}, u32[]{:S(2)}) copy-start(bf16[256,256]{1,0:T(8,128)(2,1)} %wo_ref.1) | copy-start | bytes 393220
  20.5 19.6 %copy-start.6 = (f32[256]{0:T(256)S(1)}, f32[256]{0:T(256)}, u32[]{:S(2)}) copy-start(f32[256]{0:T(256)} %param.22) | copy-start | bytes 3076
  20.5 19.6 %copy-start.7 = (s32[1,2]{1,0:T(1,128)S(1)}, s32[1,2]{1,0:T(1,128)}, u32[]{:S(2)}) copy-start(s32[1,2]{1,0:T(1,128)} %amino_ref.1) | copy-start | bytes 28
  32.4 0.8 copy-start.8
  53.4 4.0 %collective-permute-start = (bf16[32,40,256]{2,1,0:T(8,128)(2,1)S(1)}, bf16[32,40,256]{2,1,0:T(8,128)(2,1)S(1)}, u32[]{:S(2)}, u32[]{:S(2)}) collective-permute-start(bf16[32,40,256]{2,1,0:T(8,128)(2,1)S(1)} %get-tuple-element.36), channel_id=1, source_target_pairs={{0,1},{1,0},{2,3},{3,2},{4,5},{5,4},{6,7},{7,6},{8,9},{9,8},{10,11... | collective-permute-start | bytes 1966088 | tf_op jit(solution)/shard_map/ppermute | solution.py:427
  88.9 10.0 %all-to-all-start.2 = ((bf16[8,24,256]{2,1,0:T(8,128)(2,1)}), bf16[8,24,256]{2,1,0:T(8,128)(2,1)S(1)}, u32[]{:S(2)}, u32[]{:S(2)}) async-start(bf16[8,24,256]{2,1,0:T(8,128)(2,1)} %merge.1), calls=%async_computation.2 | async-start | bytes 196608 | tf_op jit(solution)/shard_map/all_to_all | solution.py:406
  94.2 32.1 %copy-start = (bf16[1,8,128,256]{3,2,1,0:T(8,128)(2,1)}, bf16[1,8,128,256]{3,2,1,0:T(8,128)(2,1)S(1)}, u32[]{:S(2)}) copy-start(bf16[1,8,128,256]{3,2,1,0:T(8,128)(2,1)S(1)} %reshape.29.after_ref) | copy-start | bytes 1572868
  117.7 7.4 %collective-permute-start.1 = (bf16[32,40,128]{2,1,0:T(8,128)(2,1)S(1)}, bf16[32,40,128]{2,1,0:T(8,128)(2,1)S(1)}, u32[]{:S(2)}, u32[]{:S(2)}) collective-permute-start(bf16[32,40,128]{2,1,0:T(8,128)(2,1)S(1)} %all_to_all.21.own_ref), channel_id=1, source_target_pairs={{0,1},{1,0},{2,3},{3,2},{4,5},{5,4},{6,7},{7,6},{8,9},{9,8},{10,11... | collective-permute-start | bytes 983048 | tf_op jit(solution)/shard_map/ppermute | solution.py:434
